TPU v7x, 256 devices: a whole 4x4x8 slice. The times are simulated.
256 devices in a mesh: dp: 8 (over y, core), expert: 32 (over z, x).
Axes of the slice: x: 4, y: 4, z: 8, core: 2. Of those that a mesh axis runs over, the one named last changes fastest.
Arguments:
- frames: bfloat16 [49152, 1024], P(('dp', 'expert')), may hold values from -6 to 6
- norm_gain_vector: float32 [1024], replicated, may hold values from 0.1 to 1.9
- router: bfloat16 [1024, 32], replicated, may hold values from -0.1875 to 0.1875
- w_in: bfloat16 [32, 1024, 2048], P('expert', 'dp'), may hold values from -0.1875 to 0.1875
- w_out: bfloat16 [32, 2048, 1024], P('expert', 'dp'), may hold values from -0.125 to 0.125
- expert_ids: int32 [49152, 2], P(('dp', 'expert')), may hold values from 0 to 31, all different within a row; in each aligned block of 192 rows (0 to 191, 192 to 383, ...) at most 18 rows name the same one
- frame_mask: int32 [49152], P(('dp', 'expert')), may hold values 0 or 1
- out_grad: bfloat16 [49152, 1024], P(('dp', 'expert')), may hold values from -6 to 6
Outputs:
- mixed: bfloat16 [49152, 1024], P(('dp', 'expert'))
- grad_frames: bfloat16 [49152, 1024], P(('dp', 'expert'))
- grad_w_in: float32 [32, 1024, 2048], P('expert', 'dp')
- grad_w_out: float32 [32, 2048, 1024], P('expert', 'dp')
- grad_router: float32 [1024, 32], replicated
- gain_gradient: float32 [1024], replicated
Inputs may be any that keep to these rules, and one draw needn't show every extreme that they name: `expert_ids`: each row names two different experts; among the frames of one device no expert is named more than 18 times, a bound that some block reaches.
All inputs are finite; a program needn't handle non-finite values. No bound on the sum of `frame_mask` on one device may be relied on, other than what follows from the above.
Results may differ from a plain program's by a relative error of at most 0.015.
Values may be sent and summed in bfloat16 or wider, within the bound.
No kernel may reach another device: no remote copies, remote signals or barrier semaphores. Data moves between devices by JAX's collectives and lax.ppermute only.
A program may use at most 128 MiB of HBM per device.

v0:
```python
import jax
import jax.numpy as jnp
from jax import lax
from jax.sharding import PartitionSpec as P

CAP = 18


EPS = 1e-05


def assign_slots(flat_ids, expert_count):
    onehot = (flat_ids[:, None] == jnp.arange(expert_count, dtype=jnp.int32)[None, :]).astype(
        jnp.int32
    )
    before = jnp.cumsum(onehot, axis=0) - onehot
    return jnp.sum(before * onehot, axis=1)


def on_device(frames, norm_gain_vector, router, w_in, w_out, expert_ids, frame_mask, out_grad):
    row_count = frames.shape[0]
    feature_count = frames.shape[1]
    expert_count = router.shape[1]
    pair_count = expert_ids.shape[1]
    floats = frames.astype(jnp.float32)
    average = jnp.mean(floats, axis=1, keepdims=True)
    centered_input = floats - average
    inverse_deviation = lax.rsqrt(
        jnp.mean(centered_input * centered_input, axis=1, keepdims=True) + EPS
    )
    standardized_input = centered_input * inverse_deviation
    normalized_rows = (standardized_input * norm_gain_vector).astype(jnp.bfloat16)
    logits = jnp.dot(normalized_rows, router, preferred_element_type=jnp.float32)
    choose = (
        expert_ids[:, :, None] == jnp.arange(expert_count, dtype=jnp.int32)[None, None, :]
    ).astype(jnp.float32)
    picked_logit = jnp.sum(logits[:, None, :] * choose, axis=2)
    scores = jax.nn.sigmoid(picked_logit)
    totals = jnp.sum(scores, axis=1, keepdims=True)
    live_mask = frame_mask.astype(jnp.float32)[:, None]
    weight = live_mask * scores / totals
    flat_ids = expert_ids.reshape(-1)
    slot_flat = assign_slots(flat_ids, expert_count)
    slot_pair = slot_flat.reshape(row_count, pair_count)
    empty_buffer = jnp.zeros((expert_count, CAP, feature_count), jnp.bfloat16)
    outgoing = empty_buffer.at[flat_ids, slot_flat].set(
        jnp.repeat(normalized_rows, pair_count, axis=0)
    )
    incoming = lax.all_to_all(outgoing, "expert", split_axis=0, concat_axis=1, tiled=True)
    pre_act = jnp.einsum(
        "erd,edf->erf",
        incoming,
        lax.all_gather(w_in, "dp", axis=1, tiled=True),
        preferred_element_type=jnp.float32,
    )
    logistic = jax.nn.sigmoid(pre_act)
    hidden = (pre_act * logistic).astype(jnp.bfloat16)
    derivative = logistic * (1.0 + pre_act * (1.0 - logistic))
    expert_out = jnp.einsum(
        "erf,efd->erd",
        hidden,
        lax.all_gather(w_out, "dp", axis=1, tiled=True),
        preferred_element_type=jnp.float32,
    ).astype(jnp.bfloat16)
    returned = lax.all_to_all(expert_out, "expert", split_axis=1, concat_axis=0, tiled=True)
    picked = returned[expert_ids, slot_pair]
    mixed = (floats + jnp.sum(weight[:, :, None] * picked.astype(jnp.float32), axis=1)).astype(
        jnp.bfloat16
    )
    grad_f = out_grad.astype(jnp.float32)
    grad_weight = jnp.sum(grad_f[:, None, :] * picked.astype(jnp.float32), axis=2)
    grad_rows_out = (
        (weight[:, :, None] * grad_f[:, None, :])
        .astype(jnp.bfloat16)
        .reshape(row_count * pair_count, feature_count)
    )
    grad_outgoing = empty_buffer.at[flat_ids, slot_flat].set(grad_rows_out)
    grad_incoming = lax.all_to_all(grad_outgoing, "expert", split_axis=0, concat_axis=1, tiled=True)
    portion_grad = jnp.einsum(
        "erd,efd->erf",
        grad_incoming,
        lax.all_gather(w_out, "dp", axis=1, tiled=True),
        preferred_element_type=jnp.float32,
    )
    grad_pre = (portion_grad * derivative).astype(jnp.bfloat16)
    grad_rows = jnp.einsum(
        "erf,edf->erd",
        grad_pre,
        lax.all_gather(w_in, "dp", axis=1, tiled=True),
        preferred_element_type=jnp.float32,
    ).astype(jnp.bfloat16)
    part_in = jnp.einsum("erd,erf->edf", incoming, grad_pre, preferred_element_type=jnp.float32)
    part_out = jnp.einsum("erf,erd->efd", hidden, grad_incoming, preferred_element_type=jnp.float32)
    grad_w_in, grad_w_out = (
        lax.psum_scatter(
            part_in.astype(jnp.bfloat16), "dp", scatter_dimension=1, tiled=True
        ).astype(jnp.float32),
        lax.psum_scatter(
            part_out.astype(jnp.bfloat16), "dp", scatter_dimension=1, tiled=True
        ).astype(jnp.float32),
    )
    grad_back = lax.all_to_all(grad_rows, "expert", split_axis=1, concat_axis=0, tiled=True)
    grad_moe = jnp.sum(grad_back[expert_ids, slot_pair].astype(jnp.float32), axis=1)
    first_score = scores[:, 0]
    second_score = scores[:, 1]
    sum_scores = totals[:, 0]
    weight_gap = grad_weight[:, 0] - grad_weight[:, 1]
    live_flat = live_mask[:, 0]
    grad_first = live_flat * weight_gap * second_score / (sum_scores * sum_scores)
    grad_second = -live_flat * weight_gap * first_score / (sum_scores * sum_scores)
    grad_picked = jnp.stack([grad_first, grad_second], axis=1) * scores * (1.0 - scores)
    grad_logits = jnp.sum(grad_picked[:, :, None] * choose, axis=1)
    normalized_gradient = grad_moe + jnp.dot(
        grad_logits, router.astype(jnp.float32).T, precision=lax.Precision.HIGHEST
    )
    router_part = jnp.dot(
        normalized_rows.astype(jnp.float32).T, grad_logits, precision=lax.Precision.HIGHEST
    )
    gain_partial_sum = jnp.sum(normalized_gradient * standardized_input, axis=0)
    grad_router, gain_gradient = lax.psum((router_part, gain_partial_sum), ("dp", "expert"))
    standardized_gradient = normalized_gradient * norm_gain_vector
    statistic_gradient = inverse_deviation * (
        standardized_gradient
        - jnp.mean(standardized_gradient, axis=1, keepdims=True)
        - standardized_input
        * jnp.mean(standardized_gradient * standardized_input, axis=1, keepdims=True)
    )
    grad_frames = (grad_f + statistic_gradient).astype(jnp.bfloat16)
    return (mixed, grad_frames, grad_w_in, grad_w_out, grad_router, gain_gradient)


def solution(mesh):
    return jax.shard_map(
        on_device,
        mesh=mesh,
        in_specs=(
            P(("dp", "expert"), None),
            P(),
            P(),
            P("expert", "dp", None),
            P("expert", "dp", None),
            P(("dp", "expert"), None),
            P(("dp", "expert")),
            P(("dp", "expert"), None),
        ),
        out_specs=(
            P(("dp", "expert"), None),
            P(("dp", "expert"), None),
            P("expert", "dp", None),
            P("expert", "dp", None),
            P(),
            P(),
        ),
        check_vma=False,
    )
```

profile of v0, /device:TPU:1, one launch (start us, length us, event | category | flops | bytes accessed | tf_op | source)
XLA Modules:
  0.0 549.4 jit_solution(15928173705861903766)
XLA Ops:
  12.2 1.2 fusion.35
  14.7 24.9 %scatter_fusion = bf16[32,18,1024]{2,0,1:T(8,128)(2,1)S(1)} fusion(bf16[32,18,1024]{2,0,1:T(8,128)(2,1)S(1)} %broadcast_in_dim.6.clone, s32[384]{0:T(512)S(1)} %fusion.50, bf16[384,1024]{1,0:T(8,128)(2,1)S(1)} %reshape.290), kind=kCustom, calls=%fused_computation.2 | custom fusion | bytes 2362368 | tf_op jit(solution)/shard_map/scatter | solution.py:46
  39.7 1.8 copy.78
  41.5 12.0 %all-to-all-start = ((bf16[32,18,1024]{2,1,0:T(8,128)(2,1)}), bf16[32,18,1024]{2,1,0:T(8,128)(2,1)S(1)}, u32[]{:S(2)}, u32[]{:S(2)}) async-start(bf16[32,18,1024]{2,1,0:T(8,128)(2,1)} %copy.78), calls=%async_computation | async-start | bytes 3145728 | tf_op jit(solution)/shard_map/all_to_all | solution.py:49
  54.1 1.6 mul.173
  55.7 3.1 mul.174
  58.8 2.4 multiply_convert_fusion.2
  61.4 38.6 %scatter_fusion.1 = bf16[32,18,1024]{2,0,1:T(8,128)(2,1)S(1)} fusion(bf16[32,18,1024]{2,0,1:T(8,128)(2,1)S(1)} %broadcast_in_dim.6.clone.1, s32[384]{0:T(512)S(1)} %fusion.50, bf16[384,1024]{1,0:T(8,128)(2,1)} %multiply_convert_fusion.2), kind=kCustom, calls=%fused_computation.3 | custom fusion | bytes 2362368 | tf_op jit(solution)/shard_map/scatter | solution.py:77
  100.0 1.8 copy.86
  101.8 9.3 %all-to-all-start.2 = ((bf16[32,18,1024]{2,1,0:T(8,128)(2,1)}), bf16[32,18,1024]{2,1,0:T(8,128)(2,1)}, u32[]{:S(2)}, u32[]{:S(2)}) async-start(bf16[32,18,1024]{2,1,0:T(8,128)(2,1)} %copy.86), calls=%async_computation.2 | async-start | bytes 3145728 | tf_op jit(solution)/shard_map/all_to_all | solution.py:78
  111.9 35.5 %all-to-all-done.2 = bf16[32,18,1024]{2,1,0:T(8,128)(2,1)} async-done(((bf16[32,18,1024]{2,1,0:T(8,128)(2,1)}), bf16[32,18,1024]{2,1,0:T(8,128)(2,1)}, u32[]{:S(2)}, u32[]{:S(2)}) %all-to-all-start.2) | async-done | bytes 1179680 | tf_op jit(solution)/shard_map/all_to_all | solution.py:78
  147.4 1.6 reshape.273
  149.0 6.4 %fusion.6 = f32[576,2048]{1,0:T(8,128)} fusion(bf16[576,1024]{1,0:T(8,128)(2,1)S(1)} %reshape.269, bf16[1,1024,2048]{2,1,0:T(8,128)(2,1)} %all-gather.3.cloned.1.call-done), kind=kOutput, calls=%fused_computation.13 | convolution fusion | flops 2415919104 | bytes 10092544 | tf_op jit(solution)/shard_map/erd,edf->erf/dot_general | solution.py:50
  155.4 6.2 %multiply_convert_fusion = bf16[576,2048]{1,0:T(8,128)(2,1)S(1)} fusion(f32[576,2048]{1,0:T(8,128)} %fusion.6, bf16[576,1024]{1,0:T(8,128)(2,1)S(1)} %reshape.273, bf16[1,2048,1024]{2,1,0:T(8,128)(2,1)} %all-gather.5.cloned.1.call-done), kind=kOutput, calls=%fused_computation.4 | convolution fusion | flops 2426535936 | bytes 12451840 | tf_op jit(solution)/shard_map/erd,efd->erf/dot_general | solution.py:79
  161.6 1.4 copy-done.12
  163.1 5.1 convert_bitcast_fusion.1
  168.2 8.1 %convert_bitcast_fusion = bf16[1,2048,1024]{2,1,0:T(8,128)(2,1)} fusion(bf16[576,1024]{1,0:T(8,128)(2,1)S(1)} %reshape.273, f32[576,2048]{1,0:T(8,128)} %fusion.6), kind=kOutput, calls=%fused_computation.15 | convolution fusion | flops 2423914496 | bytes 10092544 | tf_op jit(solution)/shard_map/erf,erd->efd/dot_general | solution.py:93
  176.3 6.2 %fusion.16 = bf16[1,576,1024]{2,1,0:T(8,128)(2,1)S(1)} fusion(bf16[1,2048,1024]{2,1,0:T(8,128)(2,1)} %all-gather.5.cloned.1.call-done, f32[576,2048]{1,0:T(8,128)} %fusion.6), kind=kOutput, calls=%fused_computation.22 | convolution fusion | flops 2422407168 | bytes 10092544 | tf_op jit(solution)/shard_map/erf,efd->erd/dot_general | solution.py:59
  182.6 1.8 copy.96
  184.9 8.6 %reduce.11 = bf16[576,1024]{1,0:T(8,128)(2,1)} reduce(bf16[576,1,1024]{2,1,0:T(2,128)(2,1)S(1)} %bitcast.80, bf16[]{:T(256)} %broadcast.288), dimensions={1}, to_apply=%bitcast.78.reduce_sub_computation | reduce | bytes 2359298
  193.5 2.8 reshape.312
  196.3 7.2 %all-to-all-start.1 = ((bf16[32,2,9216]{2,1,0:T(2,128)(2,1)}), bf16[32,2,9216]{2,1,0:T(2,128)(2,1)}, u32[]{:S(2)}, u32[]{:S(2)}) async-start(bf16[32,2,9216]{2,1,0:T(2,128)(2,1)} %reshape.312), calls=%async_computation.1 | async-start | bytes 2359296 | tf_op jit(solution)/shard_map/all_to_all | solution.py:65
  203.5 4.9 fusion.19
  208.4 1.8 copy.95
  210.3 8.6 %reduce.10 = bf16[576,1024]{1,0:T(8,128)(2,1)} reduce(bf16[576,1,1024]{2,1,0:T(2,128)(2,1)S(1)} %bitcast.81, bf16[]{:T(256)} %broadcast.288), dimensions={1}, to_apply=%bitcast.77.reduce_sub_computation | reduce | bytes 2359298
  218.8 2.7 reshape.314
  221.5 9.3 %all-to-all-done.1 = bf16[32,2,9216]{2,1,0:T(2,128)(2,1)} async-done(((bf16[32,2,9216]{2,1,0:T(2,128)(2,1)}), bf16[32,2,9216]{2,1,0:T(2,128)(2,1)}, u32[]{:S(2)}, u32[]{:S(2)}) %all-to-all-start.1) | async-done | bytes 1179680 | tf_op jit(solution)/shard_map/all_to_all | solution.py:65
  230.8 7.6 %all-to-all-start.3 = ((bf16[32,2,9216]{2,1,0:T(2,128)(2,1)}), bf16[32,2,9216]{2,1,0:T(2,128)(2,1)}, u32[]{:S(2)}, u32[]{:S(2)}) async-start(bf16[32,2,9216]{2,1,0:T(2,128)(2,1)} %reshape.314), calls=%async_computation.3 | async-start | bytes 2359296 | tf_op jit(solution)/shard_map/all_to_all | solution.py:102
  240.0 4.3 reshape.313
  244.3 7.9 %bitcast_reduce_fusion.1 = bf16[576,1024]{1,0:T(8,128)(2,1)} fusion(bf16[576,1,1024]{2,1,0:T(2,128)(2,1)S(1)} %reshape.313), kind=kLoop, calls=%fused_computation.86 | loop fusion | bytes 2359296 | tf_op jit(solution)/shard_map/all_to_all | solution.py:65
  252.2 1.4 all_to_all.14
  254.3 5.1 gather_fusion
  259.5 2.1 reshape.300
  261.6 3.6 all-to-all-done.3
  265.2 4.7 reshape.315
  269.9 7.9 %bitcast_reduce_fusion = bf16[576,1024]{1,0:T(8,128)(2,1)} fusion(bf16[576,1,1024]{2,1,0:T(2,128)(2,1)S(1)} %reshape.315), kind=kLoop, calls=%fused_computation.85 | loop fusion | bytes 2359296 | tf_op jit(solution)/shard_map/all_to_all | solution.py:102
  277.8 1.4 all_to_all.17
  279.9 5.3 gather_fusion.1
  285.2 2.1 reshape.301
  287.3 3.3 reduce_sum.117
  290.6 5.0 multiply_reduce_fusion
  295.9 1.6 fusion.34
  298.5 2.3 fusion.33
  300.8 79.0 %psum.15 = f32[1024]{0:T(1024)} all-reduce(f32[1024]{0:T(1024)S(1)} %get-tuple-element.8), channel_id=1, replica_groups=mesh['dp'=8,'expert'=32] {'dp','expert'}, use_global_device_ids=true, to_apply=%region_19.20 | all-reduce | flops 1024 | bytes 8192 | tf_op jit(solution)/shard_map/psum | solution.py:120
  379.8 2.1 convert_element_type.96
  381.9 2.1 convert_element_type.99
  384.0 157.1 %all-reduce.2.cloned.1.call-done = f32[1024,32]{0,1:T(8,128)} async-done(((f32[1024,32]{0,1:T(8,128)}), f32[1024,32]{0,1:T(8,128)}) %all-reduce.2.cloned.1.call-update) | async-done | bytes 131088 | tf_op jit(solution)/shard_map/psum | solution.py:120
  541.1 1.6 copy.100
  (84 shorter events, 12.3 us)
Async XLA Ops:
  7.2 46.4 %copy-start = (bf16[1024,32]{0,1:T(8,128)(2,1)S(1)}, bf16[1024,32]{0,1:T(8,128)(2,1)}, u32[]{:S(2)}) copy-start(bf16[1024,32]{0,1:T(8,128)(2,1)} %param.10) | copy-start | bytes 196612
  7.2 6.3 %copy-start.1 = (bf16[192,1024]{1,0:T(8,128)(2,1)S(1)}, bf16[192,1024]{1,0:T(8,128)(2,1)}, u32[]{:S(2)}) copy-start(bf16[192,1024]{1,0:T(8,128)(2,1)} %param.8) | copy-start | bytes 1179652
  7.2 6.3 %copy-start.9 = (f32[1024]{0:T(1024)S(1)}, f32[1024]{0:T(1024)}, u32[]{:S(2)}) copy-start(f32[1024]{0:T(1024)} %param.9) | copy-start | bytes 12292
  7.2 141.8 %all-gather.3.cloned.1.call-start = ((), (), s32[]{:S(2)}) async-start(), calls=%async_computation.6 | async-start | bytes 4718592 | tf_op jit(solution)/shard_map/all_gather | solution.py:53
  7.9 147.5 %all-gather.5.cloned.1.call-start = ((), (), s32[]{:S(2)}) async-start(), calls=%async_computation.7 | async-start | bytes 4718592 | tf_op jit(solution)/shard_map/all_gather | solution.py:62
  13.7 39.8 %copy-start.3 = (bf16[192,1024]{1,0:T(8,128)(2,1)}, bf16[192,1024]{1,0:T(8,128)(2,1)S(1)}, u32[]{:S(2)}) copy-start(bf16[192,1024]{1,0:T(8,128)(2,1)S(1)} %fusion.28) | copy-start | bytes 1179652
  39.6 13.8 %copy-start.11 = (s32[192]{0:T(256)S(1)}, s32[192]{0:T(256)}, u32[]{:S(2)}) copy-start(s32[192]{0:T(256)} %param.14) | copy-start | bytes 2308
  41.5 12.3 %copy-start.10 = (s32[192,2]{0,1:T(2,128)S(1)}, s32[192,2]{0,1:T(2,128)}, u32[]{:S(2)}) copy-start(s32[192,2]{0,1:T(2,128)} %param.13) | copy-start | bytes 4612
  41.5 12.6 %copy-start.5 = (bf16[192,1024]{1,0:T(8,128)(2,1)S(1)}, bf16[192,1024]{1,0:T(8,128)(2,1)}, u32[]{:S(2)}) copy-start(bf16[192,1024]{1,0:T(8,128)(2,1)} %param.15) | copy-start | bytes 1179652
  41.5 60.3 %all-to-all-start = ((bf16[32,18,1024]{2,1,0:T(8,128)(2,1)}), bf16[32,18,1024]{2,1,0:T(8,128)(2,1)S(1)}, u32[]{:S(2)}, u32[]{:S(2)}) async-start(bf16[32,18,1024]{2,1,0:T(8,128)(2,1)} %copy.78), calls=%async_computation | async-start | bytes 3145728 | tf_op jit(solution)/shard_map/all_to_all | solution.py:49
  101.8 45.6 %all-to-all-start.2 = ((bf16[32,18,1024]{2,1,0:T(8,128)(2,1)}), bf16[32,18,1024]{2,1,0:T(8,128)(2,1)}, u32[]{:S(2)}, u32[]{:S(2)}) async-start(bf16[32,18,1024]{2,1,0:T(8,128)(2,1)} %copy.86), calls=%async_computation.2 | async-start | bytes 3145728 | tf_op jit(solution)/shard_map/all_to_all | solution.py:78
  111.1 268.6 %reduce-scatter.3.cloned.1.call-start = ((), (), s32[]{:S(2)}) async-start(), calls=%async_computation.8 | async-start | bytes 4718592 | tf_op jit(solution)/shard_map/reduce_scatter | solution.py:95
  161.6 1.4 copy-start.12
  168.2 213.7 %reduce-scatter.5.cloned.1.call-start = ((), (), s32[]{:S(2)}) async-start(), calls=%async_computation.9 | async-start | bytes 4718592 | tf_op jit(solution)/shard_map/reduce_scatter | solution.py:98
  193.5 10.0 %copy-start.13 = (bf16[576,2048]{1,0:T(8,128)(2,1)S(1)}, bf16[576,2048]{1,0:T(8,128)(2,1)}, u32[]{:S(2)}) copy-start(bf16[576,2048]{1,0:T(8,128)(2,1)} %copy-done.12) | copy-start | bytes 7077892
  196.3 34.5 %all-to-all-start.1 = ((bf16[32,2,9216]{2,1,0:T(2,128)(2,1)}), bf16[32,2,9216]{2,1,0:T(2,128)(2,1)}, u32[]{:S(2)}, u32[]{:S(2)}) async-start(bf16[32,2,9216]{2,1,0:T(2,128)(2,1)} %reshape.312), calls=%async_computation.1 | async-start | bytes 2359296 | tf_op jit(solution)/shard_map/all_to_all | solution.py:65
  218.8 19.8 %copy-start.6 = (bf16[192,1024]{1,0:T(8,128)(2,1)S(1)}, bf16[192,1024]{1,0:T(8,128)(2,1)}, u32[]{:S(2)}) copy-start(bf16[192,1024]{1,0:T(8,128)(2,1)} %param.15) | copy-start | bytes 1179652
  230.8 34.4 %all-to-all-start.3 = ((bf16[32,2,9216]{2,1,0:T(2,128)(2,1)}), bf16[32,2,9216]{2,1,0:T(2,128)(2,1)}, u32[]{:S(2)}, u32[]{:S(2)}) async-start(bf16[32,2,9216]{2,1,0:T(2,128)(2,1)} %reshape.314), calls=%async_computation.3 | async-start | bytes 2359296 | tf_op jit(solution)/shard_map/all_to_all | solution.py:102
  238.5 302.7 %all-reduce.2.cloned.1.call-start = ((), (), s32[]{:S(2)}) async-start(), calls=%async_computation.10 | async-start | bytes 262144 | tf_op jit(solution)/shard_map/psum | solution.py:120
  285.2 5.4 copy-start.2
  290.6 6.9 %copy-start.4 = (bf16[192,1024]{1,0:T(8,128)(2,1)S(1)}, bf16[192,1024]{1,0:T(8,128)(2,1)}, u32[]{:S(2)}) copy-start(bf16[192,1024]{1,0:T(8,128)(2,1)} %copy-done.3) | copy-start | bytes 1179652
  295.7 2.8 copy-start.7
  295.7 2.8 copy-start.8
Sparse Core Ops, SparseCore 0:
  9.9 38.9 all-gather.2
  50.7 34.6 all-gather.4
  168.3 38.0 reduce-scatter.2
  208.8 39.8 reduce-scatter.4
  298.6 242.5 all-reduce.1
where the time goes:
time: 559 us; the launch traced here: 549 us
  waiting for transfers between devices  207 us (37%)
  local copies, waits for them, and re-layouts  133 us (24%)
  blocking collectives  79 us (14%)
  matrix products  39.6 us (7%)
  other arithmetic  39.4 us (7%)
  starting transfers between devices  36.6 us (7%)
  between operations  14.5 us (3%)
    psum x1, waiting for transfers between devices, on_device(): lax.psum((router_part, gain_partial_sum), ('dp', 'expert'))  157 us
    psum x1, blocking collectives, on_device(): lax.psum((router_part, gain_partial_sum), ('dp', 'expert'))  79 us
    scatter x2, local copies, waits for them, and re-layouts, on_device(): grad_outgoing = empty_buffer.at[flat_ids, slot_flat].set(grad_rows_out)  40.4 us
    all_to_all x1, waiting for transfers between devices, on_device(): lax.all_to_all(grad_outgoing, 'expert', split_axis=0, concat_axis=1, tile...  35.5 us
    scatter x2, local copies, waits for them, and re-layouts, on_device(): empty_buffer.at[flat_ids, slot_flat]  26.7 us
    unnamed x35, local copies, waits for them, and re-layouts  18.9 us
    unnamed x2, other arithmetic  17.2 us
    all_to_all x1, starting transfers between devices, on_device(): lax.all_to_all(outgoing, 'expert', split_axis=0, concat_axis=1, tiled=True)  12 us
  transfers between devices with their start and end apart: 9, of which 4 were waited for; matrix products, arithmetic and copies ran while one was open for 36% of the time, Pallas kernels for 0%

commit v1 on v0

v1 whole, which is shorter than its diff:
```python
import functools

import jax
import jax.numpy as jnp
from jax import lax
from jax.experimental import pallas as pl
from jax.experimental.pallas import tpu as pltpu
from jax.sharding import PartitionSpec as P

CAP = 18
MAIN = 16
EPS = 1e-05
LANES = 128

f32 = jnp.float32
bf16 = jnp.bfloat16


def iota(shape, dim):
    return lax.broadcasted_iota(jnp.int32, shape, dim)


def indicator(condition):
    return jnp.where(condition, 1.0, 0.0).astype(bf16)


def matmul(a, b, **kw):
    return jnp.dot(a, b, preferred_element_type=f32, **kw)


def matmul_nt(a, b, **kw):
    return lax.dot_general(a, b, (((1,), (1,)), ((), ())), preferred_element_type=f32, **kw)


def extra_order(peers, pieces):
    rows = peers * MAIN
    i = iota((rows, rows), 0)
    j = iota((rows, rows), 1)
    return i, j, rows


def pack(rows, out_ref, peers):
    width = rows.shape[1]
    pieces = width // LANES
    main = peers * MAIN
    out_ref[:, :width] = rows[:main]
    extra = rows[main:]
    stacked = jnp.concatenate([extra[:, p * LANES : (p + 1) * LANES] for p in range(pieces)], axis=0)
    i, j, _ = extra_order(peers, pieces)
    source = (i % pieces) * (2 * peers) + ((i // pieces) % 2) * peers + i // MAIN
    out_ref[:, width:] = matmul(indicator(j == source), stacked).astype(bf16)


def unpack(ref, peers):
    width = ref.shape[1] - LANES
    pieces = width // LANES
    i, j, _ = extra_order(peers, pieces)
    target = (i % peers) * MAIN + ((i // peers) % 2) * pieces + i // (2 * peers)
    stacked = matmul(indicator(j == target), ref[:, width:]).astype(bf16)
    extra = jnp.concatenate(
        [stacked[p * 2 * peers : (p + 1) * 2 * peers] for p in range(pieces)], axis=1
    )
    return ref[:, :width], extra


def layer_norm(frames_ref):
    floats = frames_ref[...].astype(f32)
    average = jnp.mean(floats, axis=1, keepdims=True)
    centered = floats - average
    inverse = lax.rsqrt(jnp.mean(centered * centered, axis=1, keepdims=True) + EPS)
    return floats, centered * inverse, inverse


def dispatch_kernel(peers, frames_ref, gain_ref, ids_ref, out_ref, normed_ref, place_ref):
    _, standardized, _ = layer_norm(frames_ref)
    normed = (standardized * gain_ref[...]).astype(bf16)
    normed_ref[...] = normed
    count = normed.shape[0]
    ids = ids_ref[...]
    expert = iota((peers, count), 0)
    first, second = expert == ids[0:1], expert == ids[1:2]
    earlier = indicator(iota((count, count), 0) < iota((count, count), 1))
    before = matmul(indicator(first | second), earlier)
    places = []
    for k, chosen in enumerate((first, second)):
        slot = jnp.sum(jnp.where(chosen, before, 0.0), axis=0, keepdims=True).astype(jnp.int32)
        e = ids[k : k + 1]
        places.append(
            jnp.where(slot < MAIN, e * MAIN + slot, peers * MAIN + (slot - MAIN) * peers + e)
        )
    place = jnp.concatenate(places, axis=0)
    place_ref[...] = place
    row = iota((peers * CAP, count), 0)
    select = indicator((row == place[0:1]) | (row == place[1:2]))
    pack(matmul(select, normed).astype(bf16), out_ref, peers)


def grads_kernel(peers, normed_ref, router_ref, ids_ref, mask_ref, place_ref, grad_ref, out_ref, meta_ref):
    logits = matmul_nt(router_ref[...], normed_ref[...])
    count = logits.shape[1]
    ids = ids_ref[...]
    place = place_ref[...]
    expert = iota((peers, count), 0)
    scores = [
        jax.nn.sigmoid(
            jnp.sum(jnp.where(expert == ids[k : k + 1], logits, 0.0), axis=0, keepdims=True)
        )
        for k in range(2)
    ]
    total = scores[0] + scores[1]
    live = mask_ref[...].astype(f32)
    weights = [live * s / total for s in scores]
    row = iota((peers * CAP, count), 0)
    here = [row == place[k : k + 1] for k in range(2)]
    scale = jnp.sum(
        jnp.where(here[0], weights[0], 0.0) + jnp.where(here[1], weights[1], 0.0),
        axis=1,
        keepdims=True,
    )
    rows = matmul(indicator(here[0] | here[1]), grad_ref[...])
    pack((rows * scale).astype(bf16), out_ref, peers)
    facts = jnp.concatenate(
        [
            place.astype(f32),
            ids.astype(f32),
            weights[0],
            weights[1],
            scores[0],
            scores[1],
        ],
        axis=0,
    )
    padded = jnp.concatenate([facts, jnp.zeros((8, 256 - count), f32)], axis=1)
    meta_ref[...] = padded.T[:count]


def unpack_kernel(peers, packed_ref, out_ref):
    main, extra = unpack(packed_ref, peers)
    out_ref[: peers * MAIN] = main
    out_ref[peers * MAIN :] = extra


def pack_kernel(peers, rows_ref, out_ref):
    pack(rows_ref[...], out_ref, peers)


def mix_kernel(
    peers, packed_ref, frames_ref, normed_ref, grad_ref, meta_ref, mask_ref, router_ref,
    mixed_ref, base_ref, router_part_ref,
):
    main, extra = unpack(packed_ref, peers)
    meta = meta_ref[...]
    column = [meta[:, k : k + 1] for k in range(8)]
    count = meta.shape[0]
    places = [c.astype(jnp.int32) for c in column[0:2]]
    experts = [c.astype(jnp.int32) for c in column[2:4]]
    weights, scores = column[4:6], column[6:8]
    cut = peers * MAIN
    lane = iota((count, cut), 1)
    lane_extra = iota((count, 2 * peers), 1) + cut
    grad = grad_ref[...].astype(f32)
    picked = [
        matmul(indicator(lane == p), main) + matmul(indicator(lane_extra == p), extra)
        for p in places
    ]
    mixed = frames_ref[...].astype(f32) + (weights[0] * picked[0] + weights[1] * picked[1])
    mixed_ref[...] = mixed.astype(bf16)
    grad_weight = [jnp.sum(grad * p, axis=1, keepdims=True) for p in picked]
    total = scores[0] + scores[1]
    gap = mask_ref[...].astype(f32) * (grad_weight[0] - grad_weight[1]) / (total * total)
    first = gap * scores[1] * scores[0] * (1.0 - scores[0])
    second = -gap * scores[0] * scores[1] * (1.0 - scores[1])
    which = iota((count, peers), 1)
    grad_logits = jnp.where(which == experts[0], first, 0.0) + jnp.where(
        which == experts[1], second, 0.0
    )
    base_ref[...] = matmul(grad_logits, router_ref[...].astype(f32), precision=lax.Precision.HIGHEST)
    router_part_ref[...] = lax.dot_general(
        grad_logits,
        normed_ref[...].astype(f32),
        (((0,), (0,)), ((), ())),
        precision=lax.Precision.HIGHEST,
        preferred_element_type=f32,
    )


def finish_kernel(
    peers, packed_ref, frames_ref, gain_ref, grad_ref, meta_ref, base_ref, out_ref, gain_part_ref
):
    main, extra = unpack(packed_ref, peers)
    meta = meta_ref[...]
    count = meta.shape[0]
    places = [meta[:, k : k + 1].astype(jnp.int32) for k in range(2)]
    cut = peers * MAIN
    lane = iota((count, cut), 1)
    lane_extra = iota((count, 2 * peers), 1) + cut
    grad_moe = matmul(indicator((lane == places[0]) | (lane == places[1])), main) + matmul(
        indicator((lane_extra == places[0]) | (lane_extra == places[1])), extra
    )
    _, standardized, inverse = layer_norm(frames_ref)
    grad_normed = grad_moe + base_ref[...]
    gain_part_ref[...] = jnp.sum(grad_normed * standardized, axis=0, keepdims=True)
    g = grad_normed * gain_ref[...]
    statistic = inverse * (
        g
        - jnp.mean(g, axis=1, keepdims=True)
        - standardized * jnp.mean(g * standardized, axis=1, keepdims=True)
    )
    out_ref[...] = (grad_ref[...].astype(f32) + statistic).astype(bf16)


def call(kernel, name, *outs, flops=0):
    params = pltpu.CompilerParams(vmem_limit_bytes=48 * 1024 * 1024)

    def run(*args):
        size = sum(a.size * a.dtype.itemsize for a in args)
        size += sum(o.size * o.dtype.itemsize for o in outs)
        return pl.pallas_call(
            kernel,
            out_shape=outs if len(outs) > 1 else outs[0],
            compiler_params=params,
            cost_estimate=pl.CostEstimate(flops=flops, bytes_accessed=size, transcendentals=0),
            name=name,
        )(*args)

    return run


def shape(*dims, dtype=bf16):
    return jax.ShapeDtypeStruct(dims, dtype)


def exchange(packed, peers):
    out = lax.all_to_all(
        packed.reshape(peers, MAIN, packed.shape[1]), "expert", split_axis=0, concat_axis=0, tiled=True
    )
    return out.reshape(packed.shape)


def sum_over_all(rows, peers, groups):
    width = rows.shape[1]
    blocks = rows.reshape(peers, 8, width // 8)
    mine = jnp.sum(lax.all_to_all(blocks, "expert", 0, 0, tiled=True), axis=0)
    spread = jnp.broadcast_to(mine[None], (groups,) + mine.shape)
    mine = jnp.sum(lax.all_to_all(spread, "dp", 0, 0, tiled=True), axis=0)
    spread = jnp.broadcast_to(mine[None], (peers,) + mine.shape)
    return lax.all_to_all(spread, "expert", 0, 0, tiled=True).reshape(rows.shape)


def on_device(groups, frames, gain, router, w_in, w_out, expert_ids, frame_mask, out_grad):
    count, width = frames.shape
    peers = router.shape[1]
    rows = peers * CAP
    packed = shape(peers * MAIN, width + LANES)
    gain = gain[None]
    router_rows = router.T
    ids = expert_ids.T
    weights_in = lax.all_gather(w_in[0], "dp", axis=0, tiled=True)
    weights_out = lax.all_gather(w_out[0], "dp", axis=0, tiled=True)

    part = functools.partial
    sent, normed, place = call(
        part(dispatch_kernel, peers), "dispatch", packed, shape(count, width), shape(2, count, dtype=jnp.int32)
    )(frames, gain, ids)
    arrived = exchange(sent, peers)
    sent_grads, meta = call(
        part(grads_kernel, peers), "grads", packed, shape(count, 8, dtype=f32)
    )(normed, router_rows, ids, frame_mask[None], place, out_grad)
    arrived_grads = exchange(sent_grads, peers)

    incoming = call(part(unpack_kernel, peers), "unpack", shape(rows, width))(arrived)
    pre = matmul(incoming, weights_in)
    logistic = jax.nn.sigmoid(pre)
    hidden = (pre * logistic).astype(bf16)
    derivative = logistic * (1.0 + pre * (1.0 - logistic))
    expert_out = matmul(hidden, weights_out).astype(bf16)
    returned = exchange(call(part(pack_kernel, peers), "pack", packed)(expert_out), peers)

    grad_incoming = call(part(unpack_kernel, peers), "unpack_grads", shape(rows, width))(arrived_grads)
    part_out = lax.dot_general(
        hidden, grad_incoming, (((0,), (0,)), ((), ())), preferred_element_type=f32
    ).astype(bf16)
    grad_w_out = lax.psum_scatter(part_out, "dp", scatter_dimension=0, tiled=True).astype(f32)
    grad_pre = (matmul_nt(grad_incoming, weights_out) * derivative).astype(bf16)
    part_in = lax.dot_general(
        incoming, grad_pre, (((0,), (0,)), ((), ())), preferred_element_type=f32
    ).astype(bf16)
    grad_w_in = lax.psum_scatter(part_in, "dp", scatter_dimension=0, tiled=True).astype(f32)
    grad_rows = matmul_nt(grad_pre, weights_in).astype(bf16)
    back = exchange(call(part(pack_kernel, peers), "pack_grads", packed)(grad_rows), peers)

    mixed, base, router_part = call(
        part(mix_kernel, peers),
        "mix",
        shape(count, width),
        shape(count, width, dtype=f32),
        shape(peers, width, dtype=f32),
    )(returned, frames, normed, out_grad, meta, frame_mask[:, None], router_rows)
    grad_router = sum_over_all(router_part, peers, groups).T
    grad_frames, gain_part = call(
        part(finish_kernel, peers), "finish", shape(count, width), shape(1, width, dtype=f32)
    )(back, frames, gain, out_grad, meta, base)
    spread = jnp.broadcast_to(gain_part.reshape(1, 8, width // 8), (peers, 8, width // 8))
    gain_mine = jnp.sum(lax.all_to_all(spread, "expert", 0, 0, tiled=True), axis=0)
    spread = jnp.broadcast_to(gain_mine[None], (groups,) + gain_mine.shape)
    gain_gradient = jnp.sum(lax.all_to_all(spread, "dp", 0, 0, tiled=True), axis=0).reshape(width)
    return (mixed, grad_frames, grad_w_in[None], grad_w_out[None], grad_router, gain_gradient)


def solution(mesh):
    return jax.shard_map(
        functools.partial(on_device, mesh.shape["dp"]),
        mesh=mesh,
        in_specs=(
            P(("dp", "expert"), None),
            P(),
            P(),
            P("expert", "dp", None),
            P("expert", "dp", None),
            P(("dp", "expert"), None),
            P(("dp", "expert")),
            P(("dp", "expert"), None),
        ),
        out_specs=(
            P(("dp", "expert"), None),
            P(("dp", "expert"), None),
            P("expert", "dp", None),
            P("expert", "dp", None),
            P(),
            P(),
        ),
        check_vma=False,
    )
```

time: 559 us -> 275 us (0.49); the launches traced: 549 us -> 273 us
  local copies, waits for them, and re-layouts: 133 us -> 20 us
  waiting for transfers between devices: 207 us -> 122 us
  blocking collectives: 79 us -> 0 us
  other arithmetic: 39.4 us -> 4.93 us
  starting transfers between devices: 36.6 us -> 62.7 us
  Pallas kernels: 0 us -> 11 us
    psum x1 -> x0, waiting for transfers between devices: 157 us -> none  [on_device(): lax.psum((router_part, gain_partial_sum), ('dp', 'expert'))]
    psum x1 -> x0, blocking collectives: 79 us -> none  [on_device(): lax.psum((router_part, gain_partial_sum), ('dp', 'expert'))]
    all_to_all x4 -> x9, waiting for transfers between devices: 48.4 us -> 121 us  [the longest x4 88.2 us: exchange(): lax.all_to_all(packed.reshape(peers, MAIN, packed.shape[1]), 'expert', sp...]
    scatter x4 -> x0, local copies, waits for them, and re-layouts: 67.1 us -> none  [the longest x2 40.4 us: on_device(): grad_outgoing = empty_buffer.at[flat_ids, slot_flat].set(grad_rows_out)]
    all_to_all x4 -> x9, starting transfers between devices: 36.1 us -> 62.4 us  [the longest x4 33.2 us: exchange(): lax.all_to_all(packed.reshape(peers, MAIN, packed.shape[1]), 'expert', sp...]
    all_to_all x6 -> x0, local copies, waits for them, and re-layouts: 20 us -> none  [the longest x3 10 us: on_device(): lax.all_to_all(grad_rows, 'expert', split_axis=1, concat_axis=0, tiled=True)]
    unnamed x2 -> x0, other arithmetic: 17.2 us -> none
    pallas_call x0 -> x8, Pallas kernels: none -> 11 us  [run(): pl.pallas_call(kernel, out_shape=outs if len(outs) > 1 else outs[0], comp...]
  transfers between devices with their start and end apart: 9 -> 13, of which waited for: 4 -> 9; matrix products, arithmetic and copies ran while one was open for 36% -> 13% of each run, Pallas kernels for 0% -> 4%
where the time goes in v1:
time: 275 us; the launch traced here: 273 us
  waiting for transfers between devices  122 us (44%)
  starting transfers between devices  62.7 us (23%)
  matrix products  38.2 us (14%)
  local copies, waits for them, and re-layouts  20 us (7%)
  between operations  14 us (5%)
  Pallas kernels  11 us (4%)
  other arithmetic  4.93 us (2%)
    all_to_all x4, waiting for transfers between devices, exchange(): lax.all_to_all(packed.reshape(peers, MAIN, packed.shape[1]), 'expert', sp...  88.2 us
    all_to_all x4, starting transfers between devices, exchange(): lax.all_to_all(packed.reshape(peers, MAIN, packed.shape[1]), 'expert', sp...  33.2 us
    unnamed x46, local copies, waits for them, and re-layouts  16.6 us
    dot_general x2, matrix products, matmul(): return jnp.dot(a, b, preferred_element_type=f32, **kw)  13.6 us
    dot_general x2, matrix products, matmul_nt(): lax.dot_general(a, b, (((1,), (1,)), ((), ())), preferred_element_type=f3...  11.9 us
    pallas_call x8, Pallas kernels, run(): pl.pallas_call(kernel, out_shape=outs if len(outs) > 1 else outs[0], comp...  11 us
    all_to_all x1, starting transfers between devices, sum_over_all(): mine = jnp.sum(lax.all_to_all(spread, 'dp', 0, 0, tiled=True), axis=0)  9.48 us
    all_to_all x1, waiting for transfers between devices, on_device(): lax.all_to_all(spread, 'expert', 0, 0, tiled=True)  9.31 us
  transfers between devices with their start and end apart: 13, of which 9 were waited for; matrix products, arithmetic and copies ran while one was open for 13% of the time, Pallas kernels for 4%

profile of v1, /device:TPU:1, one launch (start us, length us, event | category | flops | bytes accessed | tf_op | source)
XLA Modules:
  0.0 273.3 jit_solution(9095936737187600955)
XLA Ops:
  7.9 0.7 all-gather.7.cloned.1.call-update
  8.7 1.0 copy-done
  9.7 0.7 copy-done.15
  11.0 2.2 dispatch.1
  13.2 11.9 %all-to-all-start = ((bf16[32,16,1152]{2,1,0:T(8,128)(2,1)}), bf16[32,16,1152]{2,1,0:T(8,128)(2,1)S(1)}, u32[]{:S(2)}, u32[]{:S(2)}) async-start(bf16[32,16,1152]{2,1,0:T(8,128)(2,1)} %bitcast.2), calls=%async_computation | async-start | bytes 2359296 | tf_op jit(solution)/shard_map/all_to_all | solution.py:234
  25.1 1.0 copy-done.2
  26.1 0.8 copy-done.13
  26.9 0.7 copy-done.18
  28.3 1.0 grads.1
  29.3 1.0 copy-done.4
  31.0 22.7 %all-to-all-done = bf16[32,16,1152]{2,1,0:T(8,128)(2,1)S(1)} async-done(((bf16[32,16,1152]{2,1,0:T(8,128)(2,1)}), bf16[32,16,1152]{2,1,0:T(8,128)(2,1)S(1)}, u32[]{:S(2)}, u32[]{:S(2)}) %all-to-all-start) | async-done | bytes 1179680 | tf_op jit(solution)/shard_map/all_to_all | solution.py:234
  53.7 6.6 %all-to-all-start.2 = ((bf16[32,16,1152]{2,1,0:T(8,128)(2,1)}), bf16[32,16,1152]{2,1,0:T(8,128)(2,1)S(1)}, u32[]{:S(2)}, u32[]{:S(2)}) async-start(bf16[32,16,1152]{2,1,0:T(8,128)(2,1)} %bitcast.56), calls=%async_computation.2 | async-start | bytes 2359296 | tf_op jit(solution)/shard_map/all_to_all | solution.py:234
  60.7 1.0 copy-done.5
  61.7 26.4 %all-to-all-done.2 = bf16[32,16,1152]{2,1,0:T(8,128)(2,1)S(1)} async-done(((bf16[32,16,1152]{2,1,0:T(8,128)(2,1)}), bf16[32,16,1152]{2,1,0:T(8,128)(2,1)S(1)}, u32[]{:S(2)}, u32[]{:S(2)}) %all-to-all-start.2) | async-done | bytes 1179680 | tf_op jit(solution)/shard_map/all_to_all | solution.py:234
  88.4 7.3 %fusion.6 = f32[576,2048]{1,0:T(8,128)} fusion(bf16[576,1024]{1,0:T(8,128)(2,1)} %copy-done.5, bf16[1,1024,2048]{2,1,0:T(8,128)(2,1)} %all-gather.5.cloned.1.call-done), kind=kOutput, calls=%fused_computation.9 | convolution fusion | flops 2415919104 | bytes 10092544 | tf_op jit(solution)/shard_map/dot_general | solution.py:28
  95.8 6.3 %multiply_convert_fusion = bf16[576,2048]{1,0:T(8,128)(2,1)S(1)} fusion(f32[576,2048]{1,0:T(8,128)} %fusion.6, bf16[576,1024]{1,0:T(8,128)(2,1)S(1)} %unpack_grads.1, bf16[1,2048,1024]{2,1,0:T(8,128)(2,1)} %all-gather.7.cloned.1.call-done), kind=kOutput, calls=%fused_computation | convolution fusion | flops 2426535936 | bytes 12451840 | tf_op jit(solution)/shard_map/dot_general | solution.py:32
  102.1 1.4 copy-done.21
  103.5 5.1 %convolution_convert_fusion.1 = bf16[1024,2048]{1,0:T(8,128)(2,1)} fusion(bf16[576,1024]{1,0:T(8,128)(2,1)S(1)} %copy-done.6, bf16[576,2048]{1,0:T(8,128)(2,1)S(1)} %multiply_convert_fusion), kind=kOutput, calls=%fused_computation.12 | convolution fusion | flops 2418016256 | bytes 7733248 | tf_op jit(solution)/shard_map/dot_general | solution.py:285
  108.8 7.7 %convolution_convert_fusion = bf16[2048,1024]{1,0:T(8,128)(2,1)} fusion(bf16[576,1024]{1,0:T(8,128)(2,1)S(1)} %unpack_grads.1, f32[576,2048]{1,0:T(8,128)} %fusion.6), kind=kOutput, calls=%fused_computation.11 | convolution fusion | flops 2423914496 | bytes 10092544 | tf_op jit(solution)/shard_map/dot_general | solution.py:280
  116.5 6.2 %fusion.13.rows_ref = bf16[576,1024]{1,0:T(8,128)(2,1)S(1)} fusion(bf16[1,2048,1024]{2,1,0:T(8,128)(2,1)} %all-gather.7.cloned.1.call-done, f32[576,2048]{1,0:T(8,128)} %fusion.6), kind=kOutput, calls=%fused_computation.14 | convolution fusion | flops 2422407168 | bytes 10092544 | tf_op jit(solution)/shard_map/dot_general | solution.py:28
  122.8 1.3 pack.1
  124.1 6.9 %all-to-all-start.1 = ((bf16[32,16,1152]{2,1,0:T(8,128)(2,1)}), bf16[32,16,1152]{2,1,0:T(8,128)(2,1)S(1)}, u32[]{:S(2)}, u32[]{:S(2)}) async-start(bf16[32,16,1152]{2,1,0:T(8,128)(2,1)} %bitcast.6), calls=%async_computation.1 | async-start | bytes 2359296 | tf_op jit(solution)/shard_map/all_to_all | solution.py:234
  131.0 5.7 %fusion.10.rows_ref = bf16[576,1024]{1,0:T(8,128)(2,1)S(1)} fusion(bf16[576,2048]{1,0:T(8,128)(2,1)} %copy-done.21, bf16[1,1024,2048]{2,1,0:T(8,128)(2,1)} %all-gather.5.cloned.1.call-done), kind=kOutput, calls=%fused_computation.13 | convolution fusion | flops 2416508928 | bytes 7733248 | tf_op jit(solution)/shard_map/dot_general | solution.py:32
  136.8 1.3 pack_grads.1
  138.1 19.8 %all-to-all-done.1 = bf16[32,16,1152]{2,1,0:T(8,128)(2,1)S(1)} async-done(((bf16[32,16,1152]{2,1,0:T(8,128)(2,1)}), bf16[32,16,1152]{2,1,0:T(8,128)(2,1)S(1)}, u32[]{:S(2)}, u32[]{:S(2)}) %all-to-all-start.1) | async-done | bytes 1179680 | tf_op jit(solution)/shard_map/all_to_all | solution.py:234
  157.9 7.8 %all-to-all-start.3 = ((bf16[32,16,1152]{2,1,0:T(8,128)(2,1)}), bf16[32,16,1152]{2,1,0:T(8,128)(2,1)S(1)}, u32[]{:S(2)}, u32[]{:S(2)}) async-start(bf16[32,16,1152]{2,1,0:T(8,128)(2,1)} %bitcast.13), calls=%async_computation.3 | async-start | bytes 2359296 | tf_op jit(solution)/shard_map/all_to_all | solution.py:234
  165.7 0.8 copy.15.mask_ref
  166.5 0.9 copy-done.10
  167.4 0.9 copy-done.12
  168.3 0.8 copy-done.14
  169.1 2.4 mix.1
  171.5 0.9 copy-done.7
  173.1 19.3 %all-to-all-done.3 = bf16[32,16,1152]{2,1,0:T(8,128)(2,1)S(1)} async-done(((bf16[32,16,1152]{2,1,0:T(8,128)(2,1)}), bf16[32,16,1152]{2,1,0:T(8,128)(2,1)S(1)}, u32[]{:S(2)}, u32[]{:S(2)}) %all-to-all-start.3) | async-done | bytes 1179680 | tf_op jit(solution)/shard_map/all_to_all | solution.py:234
  192.4 7.9 %all-to-all-start.4 = ((f32[32,8,128]{2,1,0:T(8,128)}), f32[32,8,128]{2,1,0:T(8,128)S(1)}, u32[]{:S(2)}, u32[]{:S(2)}) async-start(f32[32,8,128]{2,1,0:T(8,128)} %bitcast.23), calls=%async_computation.6 | async-start | bytes 262144 | tf_op jit(solution)/shard_map/all_to_all | solution.py:243
  200.3 1.1 copy-done.8
  201.5 0.9 copy-done.11
  202.4 2.1 finish.1
  204.5 5.2 %all-to-all-done.4 = f32[32,8,128]{2,1,0:T(8,128)S(1)} async-done(((f32[32,8,128]{2,1,0:T(8,128)}), f32[32,8,128]{2,1,0:T(8,128)S(1)}, u32[]{:S(2)}, u32[]{:S(2)}) %all-to-all-start.4) | async-done | bytes 131104 | tf_op jit(solution)/shard_map/all_to_all | solution.py:243
  210.3 4.0 %all-to-all-start.7 = ((f32[32,8,128]{2,1,0:T(8,128)}), f32[32,8,128]{2,1,0:T(8,128)S(1)}, u32[]{:S(2)}, u32[]{:S(2)}) async-start(f32[32,8,128]{2,1,0:T(8,128)} %broadcast_in_dim.56), calls=%async_computation.9 | async-start | bytes 262144 | tf_op jit(solution)/shard_map/all_to_all | solution.py:304
  214.4 9.3 %all-to-all-done.7 = f32[32,8,128]{2,1,0:T(8,128)S(1)} async-done(((f32[32,8,128]{2,1,0:T(8,128)}), f32[32,8,128]{2,1,0:T(8,128)S(1)}, u32[]{:S(2)}, u32[]{:S(2)}) %all-to-all-start.7) | async-done | bytes 131104 | tf_op jit(solution)/shard_map/all_to_all | solution.py:304
  224.3 9.5 %all-to-all-start.5 = ((f32[8,8,128]{2,1,0:T(8,128)}), f32[8,8,128]{2,1,0:T(8,128)S(1)}, u32[]{:S(2)}, u32[]{:S(2)}) async-start(f32[8,8,128]{2,1,0:T(8,128)} %broadcast_in_dim.53), calls=%async_computation.7 | async-start | bytes 65536 | tf_op jit(solution)/shard_map/all_to_all | solution.py:245
  233.8 4.7 %all-to-all-done.5 = f32[8,8,128]{2,1,0:T(8,128)S(1)} async-done(((f32[8,8,128]{2,1,0:T(8,128)}), f32[8,8,128]{2,1,0:T(8,128)S(1)}, u32[]{:S(2)}, u32[]{:S(2)}) %all-to-all-start.5) | async-done | bytes 32800 | tf_op jit(solution)/shard_map/all_to_all | solution.py:245
  239.1 4.0 %all-to-all-start.8 = ((f32[8,8,128]{2,1,0:T(8,128)}), f32[8,8,128]{2,1,0:T(8,128)S(1)}, u32[]{:S(2)}, u32[]{:S(2)}) async-start(f32[8,8,128]{2,1,0:T(8,128)} %broadcast_in_dim.57), calls=%async_computation.10 | async-start | bytes 65536 | tf_op jit(solution)/shard_map/all_to_all | solution.py:306
  243.1 4.7 %all-to-all-done.8 = f32[8,8,128]{2,1,0:T(8,128)S(1)} async-done(((f32[8,8,128]{2,1,0:T(8,128)}), f32[8,8,128]{2,1,0:T(8,128)S(1)}, u32[]{:S(2)}, u32[]{:S(2)}) %all-to-all-start.8) | async-done | bytes 32800 | tf_op jit(solution)/shard_map/all_to_all | solution.py:306
  248.5 3.9 %all-to-all-start.6 = ((f32[32,8,128]{2,1,0:T(8,128)}), f32[32,8,128]{2,1,0:T(8,128)S(1)}, u32[]{:S(2)}, u32[]{:S(2)}) async-start(f32[32,8,128]{2,1,0:T(8,128)} %broadcast_in_dim.54), calls=%async_computation.8 | async-start | bytes 262144 | tf_op jit(solution)/shard_map/all_to_all | solution.py:247
  253.0 8.8 %all-to-all-done.6 = f32[32,8,128]{2,1,0:T(8,128)S(1)} async-done(((f32[32,8,128]{2,1,0:T(8,128)}), f32[32,8,128]{2,1,0:T(8,128)S(1)}, u32[]{:S(2)}, u32[]{:S(2)}) %all-to-all-start.6) | async-done | bytes 131104 | tf_op jit(solution)/shard_map/all_to_all | solution.py:247
  262.5 2.1 bitcast_convert_fusion.1
  264.6 2.1 bitcast_convert_fusion
  (53 shorter events, 8.4 us)
Async XLA Ops:
  7.2 81.3 %all-gather.5.cloned.1.call-start = ((), (), s32[]{:S(2)}) async-start(), calls=%async_computation.13 | async-start | bytes 4718592 | tf_op jit(solution)/shard_map/all_gather | solution.py:258
  7.9 87.9 %all-gather.7.cloned.1.call-start = ((), (), s32[]{:S(2)}) async-start(), calls=%async_computation.14 | async-start | bytes 4718592 | tf_op jit(solution)/shard_map/all_gather | solution.py:259
  8.6 1.0 copy-start
  9.6 0.7 copy-start.15
  10.3 0.7 copy-start.17
  13.2 40.5 %all-to-all-start = ((bf16[32,16,1152]{2,1,0:T(8,128)(2,1)}), bf16[32,16,1152]{2,1,0:T(8,128)(2,1)S(1)}, u32[]{:S(2)}, u32[]{:S(2)}) async-start(bf16[32,16,1152]{2,1,0:T(8,128)(2,1)} %bitcast.2), calls=%async_computation | async-start | bytes 2359296 | tf_op jit(solution)/shard_map/all_to_all | solution.py:234
  25.1 1.0 copy-start.2
  26.1 0.8 copy-start.13
  26.9 0.7 copy-start.18
  27.6 0.7 copy-start.19
  29.3 1.1 copy-start.4
  30.4 0.6 copy-start.9
  53.7 34.4 %all-to-all-start.2 = ((bf16[32,16,1152]{2,1,0:T(8,128)(2,1)}), bf16[32,16,1152]{2,1,0:T(8,128)(2,1)S(1)}, u32[]{:S(2)}, u32[]{:S(2)}) async-start(bf16[32,16,1152]{2,1,0:T(8,128)(2,1)} %bitcast.56), calls=%async_computation.2 | async-start | bytes 2359296 | tf_op jit(solution)/shard_map/all_to_all | solution.py:234
  60.3 202.2 %reduce-scatter.3.cloned.1.call-start = ((), (), s32[]{:S(2)}) async-start(), calls=%async_computation.11 | async-start | bytes 4718592 | tf_op jit(solution)/shard_map/reduce_scatter | solution.py:288
  60.7 1.0 copy-start.5
  95.8 7.7 %copy-start.6 = (bf16[576,1024]{1,0:T(8,128)(2,1)S(1)}, bf16[576,1024]{1,0:T(8,128)(2,1)}, u32[]{:S(2)}) copy-start(bf16[576,1024]{1,0:T(8,128)(2,1)} %copy-done.5) | copy-start | bytes 3538948
  102.0 1.4 copy-start.21
  108.6 156.0 %reduce-scatter.5.cloned.1.call-start = ((), (), s32[]{:S(2)}) async-start(), calls=%async_computation.12 | async-start | bytes 4718592 | tf_op jit(solution)/shard_map/reduce_scatter | solution.py:283
  124.1 33.8 %all-to-all-start.1 = ((bf16[32,16,1152]{2,1,0:T(8,128)(2,1)}), bf16[32,16,1152]{2,1,0:T(8,128)(2,1)S(1)}, u32[]{:S(2)}, u32[]{:S(2)}) async-start(bf16[32,16,1152]{2,1,0:T(8,128)(2,1)} %bitcast.6), calls=%async_computation.1 | async-start | bytes 2359296 | tf_op jit(solution)/shard_map/all_to_all | solution.py:234
  136.7 29.0 %copy-start.20 = (s32[192]{0:T(256)S(1)}, s32[192]{0:T(256)}, u32[]{:S(2)}) copy-start(s32[192]{0:T(256)} %param.14) | copy-start | bytes 2308
  136.7 29.7 %copy-start.1 = (bf16[192,1024]{1,0:T(8,128)(2,1)S(1)}, bf16[192,1024]{1,0:T(8,128)(2,1)}, u32[]{:S(2)}) copy-start(bf16[192,1024]{1,0:T(8,128)(2,1)} %frames_ref.5) | copy-start | bytes 1179652
  136.7 29.7 %copy-start.3 = (bf16[192,1024]{1,0:T(8,128)(2,1)S(1)}, bf16[192,1024]{1,0:T(8,128)(2,1)}, u32[]{:S(2)}) copy-start(bf16[192,1024]{1,0:T(8,128)(2,1)} %grad_ref.5) | copy-start | bytes 1179652
  136.7 63.6 %copy-start.16 = (f32[1024]{0:T(1024)S(1)}, f32[1024]{0:T(1024)}, u32[]{:S(2)}) copy-start(f32[1024]{0:T(1024)} %param.9) | copy-start | bytes 12292
  157.9 34.5 %all-to-all-start.3 = ((bf16[32,16,1152]{2,1,0:T(8,128)(2,1)}), bf16[32,16,1152]{2,1,0:T(8,128)(2,1)S(1)}, u32[]{:S(2)}, u32[]{:S(2)}) async-start(bf16[32,16,1152]{2,1,0:T(8,128)(2,1)} %bitcast.13), calls=%async_computation.3 | async-start | bytes 2359296 | tf_op jit(solution)/shard_map/all_to_all | solution.py:234
  166.5 0.9 copy-start.10
  167.4 0.9 copy-start.12
  168.3 0.8 copy-start.14
  171.5 0.9 copy-start.7
  192.4 17.2 %all-to-all-start.4 = ((f32[32,8,128]{2,1,0:T(8,128)}), f32[32,8,128]{2,1,0:T(8,128)S(1)}, u32[]{:S(2)}, u32[]{:S(2)}) async-start(f32[32,8,128]{2,1,0:T(8,128)} %bitcast.23), calls=%async_computation.6 | async-start | bytes 262144 | tf_op jit(solution)/shard_map/all_to_all | solution.py:243
  200.3 1.1 copy-start.8
  201.5 0.9 copy-start.11
  210.3 13.3 %all-to-all-start.7 = ((f32[32,8,128]{2,1,0:T(8,128)}), f32[32,8,128]{2,1,0:T(8,128)S(1)}, u32[]{:S(2)}, u32[]{:S(2)}) async-start(f32[32,8,128]{2,1,0:T(8,128)} %broadcast_in_dim.56), calls=%async_computation.9 | async-start | bytes 262144 | tf_op jit(solution)/shard_map/all_to_all | solution.py:304
  224.3 14.2 %all-to-all-start.5 = ((f32[8,8,128]{2,1,0:T(8,128)}), f32[8,8,128]{2,1,0:T(8,128)S(1)}, u32[]{:S(2)}, u32[]{:S(2)}) async-start(f32[8,8,128]{2,1,0:T(8,128)} %broadcast_in_dim.53), calls=%async_computation.7 | async-start | bytes 65536 | tf_op jit(solution)/shard_map/all_to_all | solution.py:245
  239.1 8.7 %all-to-all-start.8 = ((f32[8,8,128]{2,1,0:T(8,128)}), f32[8,8,128]{2,1,0:T(8,128)S(1)}, u32[]{:S(2)}, u32[]{:S(2)}) async-start(f32[8,8,128]{2,1,0:T(8,128)} %broadcast_in_dim.57), calls=%async_computation.10 | async-start | bytes 65536 | tf_op jit(solution)/shard_map/all_to_all | solution.py:306
  248.5 13.3 %all-to-all-start.6 = ((f32[32,8,128]{2,1,0:T(8,128)}), f32[32,8,128]{2,1,0:T(8,128)S(1)}, u32[]{:S(2)}, u32[]{:S(2)}) async-start(f32[32,8,128]{2,1,0:T(8,128)} %broadcast_in_dim.54), calls=%async_computation.8 | async-start | bytes 262144 | tf_op jit(solution)/shard_map/all_to_all | solution.py:247
Sparse Core Ops, SparseCore 0:
  9.9 38.8 all-gather.4
  50.7 34.6 all-gather.6
  108.7 38.1 reduce-scatter.2
  149.4 39.8 reduce-scatter.4

commit v2 on v1

v2 whole, which is shorter than its diff:
```python
import functools

import jax
import jax.numpy as jnp
from jax import lax
from jax.experimental import pallas as pl
from jax.experimental.pallas import tpu as pltpu
from jax.sharding import PartitionSpec as P

CAP = 18
MAIN = 16
EPS = 1e-05
LONG = 10**11
LANES = 128
NC = 2

f32 = jnp.float32
bf16 = jnp.bfloat16


def iota(shape, dim):
    return lax.broadcasted_iota(jnp.int32, shape, dim)


def indicator(condition):
    return jnp.where(condition, 1.0, 0.0).astype(bf16)


def matmul(a, b, **kw):
    return jnp.dot(a, b, preferred_element_type=f32, **kw)


def matmul_nt(a, b, **kw):
    return lax.dot_general(a, b, (((1,), (1,)), ((), ())), preferred_element_type=f32, **kw)


def extra_order(peers, pieces):
    rows = peers * MAIN
    i = iota((rows, rows), 0)
    j = iota((rows, rows), 1)
    return i, j, rows


def pack(rows, out_ref, peers):
    width = rows.shape[1]
    main = peers * MAIN
    out_ref[:, :width] = rows[:main]
    out_ref[:, width : width + LANES] = spread_pieces(rows[main:], peers)


def spread_pieces(extra, peers):
    pieces = extra.shape[1] // LANES
    stacked = jnp.concatenate([extra[:, p * LANES : (p + 1) * LANES] for p in range(pieces)], axis=0)
    i, j, _ = extra_order(peers, pieces)
    source = (i % pieces) * (2 * peers) + ((i // pieces) % 2) * peers + i // MAIN
    return matmul(indicator(j == source), stacked).astype(bf16)


def join_pieces(spread, peers):
    pieces = MAIN // 2
    i, j, _ = extra_order(peers, pieces)
    target = (i % peers) * MAIN + ((i // peers) % 2) * pieces + i // (2 * peers)
    stacked = matmul(indicator(j == target), spread).astype(bf16)
    return jnp.concatenate(
        [stacked[p * 2 * peers : (p + 1) * 2 * peers] for p in range(pieces)], axis=1
    )


def unpack(ref, peers):
    width = MAIN // 2 * LANES
    return ref[:, :width], join_pieces(ref[:, width : width + LANES], peers)


def unpack_into(packed_ref, rows_ref, peers):
    main, extra = unpack(packed_ref, peers)
    rows_ref[: peers * MAIN] = main
    rows_ref[peers * MAIN :] = extra


def layer_norm(frames_ref):
    floats = frames_ref[...].astype(f32)
    average = jnp.mean(floats, axis=1, keepdims=True)
    centered = floats - average
    inverse = lax.rsqrt(jnp.mean(centered * centered, axis=1, keepdims=True) + EPS)
    return floats, centered * inverse, inverse


def dispatch_kernel(peers, frames_ref, gain_ref, ids_ref, out_ref, normed_ref, place_ref):
    _, standardized, _ = layer_norm(frames_ref)
    normed = (standardized * gain_ref[...]).astype(bf16)
    normed_ref[...] = normed
    count = normed.shape[0]
    ids = ids_ref[...]
    expert = iota((peers, count), 0)
    first, second = expert == ids[0:1], expert == ids[1:2]
    earlier = indicator(iota((count, count), 0) < iota((count, count), 1))
    before = matmul(indicator(first | second), earlier)
    places = []
    for k, chosen in enumerate((first, second)):
        slot = jnp.sum(jnp.where(chosen, before, 0.0), axis=0, keepdims=True).astype(jnp.int32)
        e = ids[k : k + 1]
        places.append(
            jnp.where(slot < MAIN, e * MAIN + slot, peers * MAIN + (slot - MAIN) * peers + e)
        )
    place = jnp.concatenate(places, axis=0)
    place_ref[...] = place
    row = iota((peers * CAP, count), 0)
    select = indicator((row == place[0:1]) | (row == place[1:2]))
    pack(matmul(select, normed).astype(bf16), out_ref, peers)


def grads_kernel(peers, normed_ref, router_ref, ids_ref, mask_ref, place_ref, grad_ref, out_ref, meta_ref):
    logits = matmul_nt(router_ref[...], normed_ref[...])
    count = logits.shape[1]
    ids = ids_ref[...]
    place = place_ref[...]
    expert = iota((peers, count), 0)
    scores = [
        jax.nn.sigmoid(
            jnp.sum(jnp.where(expert == ids[k : k + 1], logits, 0.0), axis=0, keepdims=True)
        )
        for k in range(2)
    ]
    total = scores[0] + scores[1]
    live = mask_ref[...].astype(f32)
    weights = [live * s / total for s in scores]
    row = iota((peers * CAP, count), 0)
    here = [row == place[k : k + 1] for k in range(2)]
    scale = jnp.sum(
        jnp.where(here[0], weights[0], 0.0) + jnp.where(here[1], weights[1], 0.0),
        axis=1,
        keepdims=True,
    )
    rows = matmul(indicator(here[0] | here[1]), grad_ref[...])
    pack((rows * scale).astype(bf16), out_ref, peers)
    facts = jnp.concatenate(
        [
            place.astype(f32),
            ids.astype(f32),
            weights[0],
            weights[1],
            scores[0],
            scores[1],
            live,
            jnp.zeros((7, count), f32),
        ],
        axis=0,
    )
    padded = jnp.concatenate([facts, jnp.zeros((16, 256 - count), f32)], axis=1)
    meta_ref[...] = padded.T[:count]


def assemble(order_ref, pieces, out_ref):
    depth = pieces[0].shape[0]
    for j, piece in enumerate(pieces):
        out_ref[pl.ds(pl.multiple_of(order_ref[j] * depth, depth), depth)] = piece[...]


def first_kernel(peers, order_ref, packed_ref, *refs):
    pieces, (rows_ref, hidden_ref, derivative_ref, turned_ref, weights_ref) = refs[:-5], refs[-5:]
    depth = pieces[0].shape[0]

    @pl.when(pl.program_id(0) == 0)
    def _():
        unpack_into(packed_ref, rows_ref, peers)

    @pl.when(pl.program_id(0) == pl.num_programs(0) - 1)
    def _():
        for j in range(len(pieces)):
            columns = pl.ds(pl.multiple_of(order_ref[j] * depth, depth), depth)
            turned_ref[j * depth : (j + 1) * depth] = rows_ref[:, columns].T

    assemble(order_ref, pieces, weights_ref)
    pre = matmul(rows_ref[...], weights_ref[...])
    logistic = jax.nn.sigmoid(pre)
    hidden_ref[...] = (pre * logistic).astype(bf16)
    derivative_ref[...] = logistic * (1.0 + pre * (1.0 - logistic))


def second_kernel(peers, order_ref, hidden_ref, *refs):
    pieces, (out_ref, weights_ref, rows_ref) = refs[:-3], refs[-3:]
    step = pl.program_id(0)
    block = weights_ref.shape[1]
    columns = pl.ds(pl.multiple_of(step * block, block), block)
    assemble(order_ref, pieces, weights_ref)
    rows_ref[:, columns] = matmul(hidden_ref[...], weights_ref[...]).astype(bf16)

    @pl.when(step == pl.num_programs(0) - 1)
    def _():
        pack(rows_ref[...], out_ref, peers)


def outer_kernel(peers, order_ref, core_ref, packed_ref, hidden_ref, grads_ref, out_theirs_ref, out_mine_ref):
    block = out_mine_ref.shape[1]

    @pl.when(pl.program_id(0) == 0)
    def _():
        unpack_into(packed_ref, grads_ref, peers)

    product = matmul(hidden_ref[...].T, grads_ref[...]).astype(bf16)

    @pl.when(core_ref[0] == 0)
    def _():
        out_mine_ref[0] = product[:block]
        out_theirs_ref[0] = product[block:]

    @pl.when(core_ref[0] == 1)
    def _():
        out_theirs_ref[0] = product[:block]
        out_mine_ref[0] = product[block:]


def backward_kernel(
    peers, order_ref, holders_ref, grads_ref, derivative_ref, out_weights_ref, turned_ref, incoming_ref, gain_ref, *refs
):
    pieces, (in_theirs_ref, in_mine_ref, back_ref, gain_part_ref, rows_ref, in_ref) = refs[:-6], refs[-6:]
    step = pl.program_id(0)
    half, depth = in_mine_ref.shape[0], in_mine_ref.shape[1]
    assemble(holders_ref, pieces, in_ref)
    grads = grads_ref[...]
    grad_pre = (matmul_nt(grads, out_weights_ref[...]) * derivative_ref[...]).astype(bf16)
    product = matmul(turned_ref[...], grad_pre).astype(bf16)
    for j in range(half):
        in_mine_ref[j] = product[j * depth : (j + 1) * depth]
        in_theirs_ref[j] = product[(half + j) * depth : (half + j + 1) * depth]
    rows = matmul_nt(grad_pre, in_ref[...])

    @pl.when(step == 0)
    def _():
        rows_ref[...] = rows

    @pl.when(step > 0)
    def _():
        rows_ref[...] += rows

    @pl.when(step == pl.num_programs(0) - 1)
    def _():
        done = rows_ref[...].astype(bf16)
        pack(done, back_ref, peers)
        total = jnp.sum(done.astype(f32) * incoming_ref[...].astype(f32), axis=0, keepdims=True)
        gain_part_ref[...] = total / gain_ref[...]


def tally_kernel(peers, packed_ref, out_ref):
    rows = join_pieces(packed_ref[...], peers).astype(f32)
    out_ref[0:1] = jnp.sum(rows[:peers], axis=0, keepdims=True)
    out_ref[1:2] = jnp.sum(rows[peers:], axis=0, keepdims=True)


def pair_kernel(mine_ref, theirs_ref, kept_ref, *out_refs):
    kept_ref[...] = mine_ref[0].astype(f32) + theirs_ref[0].astype(f32)
    for k, out_ref in enumerate(out_refs):
        out_ref[...] = (mine_ref[k + 1].astype(f32) + theirs_ref[k + 1].astype(f32)).astype(bf16)


def total_kernel(first_ref, second_ref, *refs):
    ins, outs = refs[:-2], refs[-2:]
    count = len(ins) // 2
    for kept_ref, parts, out_ref in ((first_ref, ins[:count], outs[0]), (second_ref, ins[count:], outs[1])):
        total = kept_ref[...]
        for ref in parts:
            total += ref[...].astype(f32)
        out_ref[...] = total


def mix_kernel(
    peers, packed_ref, frames_ref, normed_ref, grad_ref, meta_ref, router_ref,
    packed_grads_ref, gain_expert_ref, mixed_ref, base_ref, out_ref,
):
    main, extra = unpack(packed_ref, peers)
    meta = meta_ref[...]
    column = [meta[:, k : k + 1] for k in range(9)]
    count = meta.shape[0]
    places = [c.astype(jnp.int32) for c in column[0:2]]
    experts = [c.astype(jnp.int32) for c in column[2:4]]
    weights, scores = column[4:6], column[6:8]
    cut = peers * MAIN
    lane = iota((count, cut), 1)
    lane_extra = iota((count, 2 * peers), 1) + cut
    grad = grad_ref[...].astype(f32)
    picked = [
        matmul(indicator(lane == p), main) + matmul(indicator(lane_extra == p), extra)
        for p in places
    ]
    floats, standardized, _ = layer_norm(frames_ref)
    mixed = floats + (weights[0] * picked[0] + weights[1] * picked[1])
    mixed_ref[...] = mixed.astype(bf16)
    grad_weight = [jnp.sum(grad * p, axis=1, keepdims=True) for p in picked]
    total = scores[0] + scores[1]
    gap = column[8] * (grad_weight[0] - grad_weight[1]) / (total * total)
    first = gap * scores[1] * scores[0] * (1.0 - scores[0])
    second = -gap * scores[0] * scores[1] * (1.0 - scores[1])
    which = iota((count, peers), 1)
    grad_logits = jnp.where(which == experts[0], first, 0.0) + jnp.where(
        which == experts[1], second, 0.0
    )
    base = matmul(grad_logits, router_ref[...].astype(f32), precision=lax.Precision.HIGHEST)
    base_ref[...] = base
    gain_part = gain_expert_ref[...] + jnp.sum(base * standardized, axis=0, keepdims=True)
    router_part = lax.dot_general(
        grad_logits,
        normed_ref[...].astype(f32),
        (((0,), (0,)), ((), ())),
        precision=lax.Precision.HIGHEST,
        preferred_element_type=f32,
    )
    sums = jnp.concatenate([router_part, jnp.broadcast_to(gain_part, router_part.shape)], axis=0)
    start = packed_grads_ref.shape[1]
    out_ref[:, :start] = packed_grads_ref[...]
    out_ref[:, start:] = spread_pieces(sums.astype(bf16), peers)


def finish_kernel(
    peers, packed_ref, frames_ref, gain_ref, grad_ref, meta_ref, base_ref, out_ref
):
    main, extra = unpack(packed_ref, peers)
    meta = meta_ref[...]
    count = meta.shape[0]
    places = [meta[:, k : k + 1].astype(jnp.int32) for k in range(2)]
    cut = peers * MAIN
    lane = iota((count, cut), 1)
    lane_extra = iota((count, 2 * peers), 1) + cut
    grad_moe = matmul(indicator((lane == places[0]) | (lane == places[1])), main) + matmul(
        indicator((lane_extra == places[0]) | (lane_extra == places[1])), extra
    )
    _, standardized, inverse = layer_norm(frames_ref)
    grad_normed = grad_moe + base_ref[...]
    g = grad_normed * gain_ref[...]
    statistic = inverse * (
        g
        - jnp.mean(g, axis=1, keepdims=True)
        - standardized * jnp.mean(g * standardized, axis=1, keepdims=True)
    )
    out_ref[...] = (grad_ref[...].astype(f32) + statistic).astype(bf16)


def call(kernel, name, *outs, grid=None, in_blocks=None, out_blocks=None, scratch=(), mib=58, order=(), cost=1):
    def spec(block, array):
        if block is None:
            dims = array.shape
            return pl.BlockSpec(dims, lambda i, *_: (0,) * len(dims))
        if block == "any":
            return pl.BlockSpec(memory_space=pl.ANY)
        return pl.BlockSpec(*block)

    def run(*args):
        ins = in_blocks if in_blocks is not None else [None] * len(args)
        ends = out_blocks if out_blocks is not None else [None] * len(outs)
        out_specs = [spec(b, o) for b, o in zip(ends, outs)]
        return pl.pallas_call(
            kernel,
            out_shape=outs if len(outs) > 1 else outs[0],
            grid_spec=pltpu.PrefetchScalarGridSpec(
                num_scalar_prefetch=len(order),
                grid=(grid or 1,),
                in_specs=[spec(b, a) for b, a in zip(ins, args)],
                out_specs=out_specs if len(outs) > 1 else out_specs[0],
                scratch_shapes=scratch,
            ),
            compiler_params=pltpu.CompilerParams(vmem_limit_bytes=mib * 1024 * 1024),
            cost_estimate=pl.CostEstimate(flops=cost, bytes_accessed=1, transcendentals=0),
            name=name,
        )(*order, *args)

    return run


def shape(*dims, dtype=bf16):
    return jax.ShapeDtypeStruct(dims, dtype)


def exchange(packed, peers):
    out = lax.all_to_all(
        packed.reshape(peers, MAIN, packed.shape[1]), "expert", split_axis=0, concat_axis=0, tiled=True
    )
    return out.reshape(packed.shape)


class Ring:
    def __init__(self, name, size, inner, fast):
        self.name, self.size, self.inner, self.fast = name, size, inner, fast
        self.length = inner if fast else size // inner
        place = lax.axis_index(name)
        self.place = place % inner if fast else place // inner

    def step(self, i, k):
        outer, within = i // self.inner, i % self.inner
        if self.fast:
            return outer * self.inner + (within + k) % self.inner
        return (outer + k) % self.length * self.inner + within

    def send(self, array, k):
        if k % self.length == 0:
            return array
        return lax.ppermute(array, self.name, [(i, self.step(i, k)) for i in range(self.size)])

    def behind(self):
        steps = jnp.arange(self.length, dtype=jnp.int32)
        return ((self.place - steps) % self.length).astype(jnp.int32)

    def ahead(self):
        steps = jnp.arange(self.length, dtype=jnp.int32)
        return ((self.place + steps) % self.length).astype(jnp.int32)


def pair_sums(mine, theirs, y, name, cost=1):
    count, depth, width = mine.shape
    steps = 2
    block = ((count, depth // steps, width), lambda i: (0, i, 0))
    flat = ((depth // steps, width), lambda i: (i, 0))
    kept, *sums = call(
        pair_kernel,
        name,
        shape(depth, width, dtype=f32),
        *[shape(depth, width)] * (count - 1),
        grid=steps,
        in_blocks=(block, block),
        out_blocks=(flat,) * count,
        cost=cost,
    )(mine, theirs)
    return kept, [y.send(part, -k - 1) for k, part in enumerate(sums)]


def total_sums(kept, parts):
    steps = 4
    flat = [((k.shape[0] // steps, k.shape[1]), lambda i: (i, 0)) for k in kept]
    count = len(parts[0])
    return call(
        total_kernel,
        "total",
        *[shape(*k.shape, dtype=f32) for k in kept],
        grid=steps,
        in_blocks=flat + [flat[0]] * count + [flat[1]] * count,
        out_blocks=flat,
    )(*kept, *parts[0], *parts[1])


def everyones(mine, axis, size):
    return lax.all_to_all(jnp.broadcast_to(mine[None], (size,) + mine.shape), axis, 0, 0, tiled=True)


def on_device(groups, frames, gain, router, w_in, w_out, expert_ids, frame_mask, out_grad):
    count, width = frames.shape
    peers = router.shape[1]
    rows = peers * CAP
    packed = shape(peers * MAIN, width + LANES)
    part = functools.partial
    gain = gain[None]
    router_rows = router.T
    ids = expert_ids.T
    core, y = Ring("dp", groups, NC, True), Ring("dp", groups, NC, False)
    behind = y.behind() * NC
    holders = jnp.concatenate([behind + core.place, behind + 1 - core.place])
    half = groups // 2

    sent, normed, place = call(
        part(dispatch_kernel, peers), "dispatch", packed, shape(count, width), shape(2, count, dtype=jnp.int32)
    )(frames, gain, ids)
    arrived = exchange(sent, peers)
    sent_grads, meta = call(
        part(grads_kernel, peers), "grads", packed, shape(count, 16, dtype=f32), cost=LONG
    )(normed, router_rows, ids, frame_mask[None], place, out_grad)
    pieces_in = [y.send(w_in[0], k) for k in range(half)]
    pieces_out = [y.send(w_out[0], k) if k != 2 else None for k in range(half)]
    later, _ = lax.optimization_barrier((w_out[0], pieces_in[2]))
    pieces_out[2] = y.send(later, 2)
    sent_grads, pieces_in, pieces_out[1], pieces_out[3] = lax.optimization_barrier(
        (sent_grads, pieces_in, pieces_out[1], pieces_out[3])
    )
    pieces_in += [core.send(piece, 1) for piece in pieces_in]
    arrived_grads = exchange(sent_grads, peers)

    inner = w_in.shape[2]
    block = 512
    column = ((rows, block), lambda i, order: (0, i))
    incoming, hidden, derivative, turned = call(
        part(first_kernel, peers),
        "first",
        shape(rows, width),
        shape(rows, inner),
        shape(rows, inner, dtype=f32),
        shape(width, rows),
        grid=inner // block,
        in_blocks=(None,) + (((width // groups, block), lambda i, order: (0, i)),) * groups,
        out_blocks=(None, column, column, None),
        scratch=[pltpu.VMEM((width, block), bf16)],
        order=(holders,),
    )(arrived, *pieces_in)
    hidden, pieces_out[2] = lax.optimization_barrier((hidden, pieces_out[2]))
    pieces_out += [core.send(piece, 1) for piece in pieces_out]
    block = 256
    expert_packed, weights_out = call(
        part(second_kernel, peers),
        "second",
        packed,
        shape(inner, width),
        grid=width // block,
        in_blocks=(None,) + (((inner // groups, block), lambda i, order: (0, i)),) * groups,
        out_blocks=(None, ((inner, block), lambda i, order: (0, i))),
        scratch=[pltpu.VMEM((rows, width), bf16)],
        order=(holders,),
    )(hidden, *pieces_out)
    expert_packed, arrived_grads = lax.optimization_barrier((expert_packed, arrived_grads))
    returned = exchange(expert_packed, peers)

    block = NC * inner // groups
    column = ((rows, block), lambda i, order, *_: (0, order[i]))
    split = ((half, width // groups, block), lambda i, order, *_: (0, 0, order[i]))
    whole = ((1, inner // groups, width), lambda i, *_: (i, 0, 0))
    grad_incoming, out_theirs, out_mine = call(
        part(outer_kernel, peers),
        "outer",
        shape(rows, width),
        *[shape(half, inner // groups, width)] * 2,
        grid=half,
        in_blocks=(None, column),
        out_blocks=(None, whole, whole),
        order=(y.behind(), core.place[None].astype(jnp.int32)),
    )(arrived_grads, hidden)
    in_theirs, in_mine, packed_grads, gain_expert = call(
        part(backward_kernel, peers),
        "backward",
        *[shape(half, width // groups, inner)] * 2,
        packed,
        shape(1, width, dtype=f32),
        grid=half,
        in_blocks=(
            None,
            column,
            ((block, width), lambda i, order, *_: (order[i], 0)),
            None,
            None,
            None,
        )
        + (((width // groups, block), lambda i, order, *_: (0, order[i])),) * groups,
        out_blocks=(split, split, None, None),
        scratch=[pltpu.VMEM((rows, width), f32), pltpu.VMEM((width, block), bf16)],
        order=(y.behind(), holders),
    )(grad_incoming, derivative, weights_out, turned, incoming, gain, *pieces_in)
    out_kept, out_parts = pair_sums(out_mine, core.send(out_theirs, 1), y, "out_pair")
    arrived_in, out_parts = lax.optimization_barrier((core.send(in_theirs, 1), out_parts))
    in_kept, in_parts = pair_sums(in_mine, arrived_in, y, "in_pair", cost=LONG)
    returned, packed_grads, out_kept = lax.optimization_barrier((returned, packed_grads, out_kept))

    mixed, base, sent_back = call(
        part(mix_kernel, peers),
        "mix",
        shape(count, width),
        shape(count, width, dtype=f32),
        shape(peers * MAIN, width + 2 * LANES),
        cost=LONG,
    )(returned, frames, normed, out_grad, meta, router_rows, packed_grads, gain_expert)
    back = exchange(sent_back, peers)
    back, out_parts, in_kept = lax.optimization_barrier((back, out_parts, in_kept))
    last = ((peers * MAIN, LANES), lambda i: (0, 1 + width // LANES))
    sums = call(part(tally_kernel, peers), "tally", shape(2, width, dtype=f32), in_blocks=(last,), mib=4)(back)
    sums = jnp.sum(everyones(sums.reshape(8, 2 * width // 8), "dp", groups), axis=0).reshape(2, width)
    grad_frames = call(part(finish_kernel, peers), "finish", shape(count, width))(
        back, frames, gain, out_grad, meta, base
    )
    sums, in_parts, grad_frames = lax.optimization_barrier((sums, in_parts, grad_frames))
    router_mine, gain_gradient = sums[0], sums[1]
    grad_router = everyones(router_mine.reshape(8, width // 8), "expert", peers).reshape(peers, width).T
    grad_w_out, grad_w_in = total_sums((out_kept, in_kept), (out_parts, in_parts))
    return (mixed, grad_frames, grad_w_in[None], grad_w_out[None], grad_router, gain_gradient)


def solution(mesh):
    return jax.shard_map(
        functools.partial(on_device, mesh.shape["dp"]),
        mesh=mesh,
        in_specs=(
            P(("dp", "expert"), None),
            P(),
            P(),
            P("expert", "dp", None),
            P("expert", "dp", None),
            P(("dp", "expert"), None),
            P(("dp", "expert")),
            P(("dp", "expert"), None),
        ),
        out_specs=(
            P(("dp", "expert"), None),
            P(("dp", "expert"), None),
            P("expert", "dp", None),
            P("expert", "dp", None),
            P(),
            P(),
        ),
        check_vma=False,
    )
```

time: 275 us -> 212 us (0.77)
  Pallas kernels: 11 us -> 72.6 us
  waiting for transfers between devices: 122 us -> 61.2 us
  matrix products: 38.2 us -> 0 us
  local copies, waits for them, and re-layouts: 20 us -> 6.04 us
  between operations: 14 us -> 0.91 us
  starting transfers between devices: 62.7 us -> 68.9 us
  other arithmetic: 4.93 us -> 1.2 us
    pallas_call x8 -> x12, Pallas kernels: 11 us -> 72.6 us  [run(): pl.pallas_call(kernel, out_shape=outs if len(outs) > 1 else outs[0], grid...]
    all_to_all x4, waiting for transfers between devices: 88.2 us -> 29.6 us  [exchange(): lax.all_to_all(packed.reshape(peers, MAIN, packed.shape[1]), 'expert', sp...]
    dot_general x6 -> x0, matrix products: 38.2 us -> none  [the longest x2 13.6 us: matmul(): return jnp.dot(a, b, preferred_element_type=f32, **kw)]
    all_to_all x5 -> x2, waiting for transfers between devices: 32.8 us -> 5.93 us  [everyones(): lax.all_to_all(jnp.broadcast_to(mine[None], (size,) + mine.shape), axis,...]
    ppermute x0 -> x22, waiting for transfers between devices: none -> 25.7 us  [send(): lax.ppermute(array, self.name, [(i, self.step(i, k)) for i in range(self....]
    ppermute x0 -> x22, starting transfers between devices: none -> 17.9 us  [send(): lax.ppermute(array, self.name, [(i, self.step(i, k)) for i in range(self....]
    all_to_all x5 -> x2, starting transfers between devices: 29.2 us -> 14 us  [everyones(): lax.all_to_all(jnp.broadcast_to(mine[None], (size,) + mine.shape), axis,...]
    unnamed x46 -> x35, local copies, waits for them, and re-layouts: 16.6 us -> 3.93 us
  transfers between devices with their start and end apart: 13 -> 28, of which waited for: 9 -> 13; matrix products, arithmetic and copies ran while one was open for 13% -> 1% of each run, Pallas kernels for 4% -> 34%
where the time goes in v2:
time: 212 us; the launch traced here: 211 us
  Pallas kernels  72.6 us (34%)
  starting transfers between devices  68.9 us (33%)
  waiting for transfers between devices  61.2 us (29%)
  local copies, waits for them, and re-layouts  6.04 us (3%)
    pallas_call x12, Pallas kernels, run(): pl.pallas_call(kernel, out_shape=outs if len(outs) > 1 else outs[0], grid...  72.6 us
    all_to_all x4, starting transfers between devices, exchange(): lax.all_to_all(packed.reshape(peers, MAIN, packed.shape[1]), 'expert', sp...  37 us
    all_to_all x4, waiting for transfers between devices, exchange(): lax.all_to_all(packed.reshape(peers, MAIN, packed.shape[1]), 'expert', sp...  29.6 us
    ppermute x22, waiting for transfers between devices, send(): lax.ppermute(array, self.name, [(i, self.step(i, k)) for i in range(self....  25.7 us
    ppermute x22, starting transfers between devices, send(): lax.ppermute(array, self.name, [(i, self.step(i, k)) for i in range(self....  17.9 us
    all_to_all x2, starting transfers between devices, everyones(): lax.all_to_all(jnp.broadcast_to(mine[None], (size,) + mine.shape), axis,...  14 us
    all_to_all x2, waiting for transfers between devices, everyones(): lax.all_to_all(jnp.broadcast_to(mine[None], (size,) + mine.shape), axis,...  5.93 us
  transfers between devices with their start and end apart: 28, of which 13 were waited for; matrix products, arithmetic and copies ran while one was open for 1% of the time, Pallas kernels for 34%

profile of v2, /device:TPU:1, one launch (start us, length us, event | category | flops | bytes accessed | tf_op | source)
XLA Modules:
  0.0 210.9 jit_solution(5769552361640361652)
XLA Ops:
  0.6 2.2 %collective-permute-start.3 = (bf16[256,1024]{1,0:T(8,128)(2,1)}, bf16[256,1024]{1,0:T(8,128)(2,1)}, u32[]{:S(2)}, u32[]{:S(2)}) collective-permute-start(bf16[256,1024]{1,0:T(8,128)(2,1)} %bitcast.42), channel_id=1, source_target_pairs={{0,64},{32,96},{64,128},{96,160},{128,192},{160,224},{192,0},{224,... | collective-permute-start | bytes 1572872 | tf_op jit(solution)/shard_map/ppermute | solution.py:395
  2.8 1.5 collective-permute-start.4
  4.4 1.6 collective-permute-start.1
  6.3 2.3 %collective-permute-start.2 = (bf16[128,2048]{1,0:T(8,128)(2,1)}, bf16[128,2048]{1,0:T(8,128)(2,1)S(1)}, u32[]{:S(2)}, u32[]{:S(2)}) collective-permute-start(bf16[128,2048]{1,0:T(8,128)(2,1)} %bitcast.32), channel_id=1, source_target_pairs={{0,192},{32,224},{64,0},{96,32},{128,64},{160,96},{192,128},{224,1... | collective-permute-start | bytes 1572872 | tf_op jit(solution)/shard_map/ppermute | solution.py:395
  8.6 3.2 %dispatch.1 = (bf16[512,1152]{1,0:T(8,128)(2,1)}, bf16[192,1024]{1,0:T(8,128)(2,1)}, s32[2,192]{1,0:T(2,128)}) custom-call(bf16[192,1024]{1,0:T(8,128)(2,1)} %frames_ref.5, f32[1,1024]{1,0:T(1,128)} %bitcast.48, s32[2,192]{1,0:T(2,128)} %bitcast.53), custom_call_target="tpu_custom_call" | custom-call | flops 1 | bytes 1 | tf_op jit(solution)/shard_map/dispatch/pallas_call | solution.py:350
  11.8 11.0 %all-to-all-start = ((bf16[32,16,1152]{2,1,0:T(8,128)(2,1)}), bf16[32,16,1152]{2,1,0:T(8,128)(2,1)S(1)}, u32[]{:S(2)}, u32[]{:S(2)}) async-start(bf16[32,16,1152]{2,1,0:T(8,128)(2,1)} %bitcast.40), calls=%async_computation | async-start | bytes 2359296 | tf_op jit(solution)/shard_map/all_to_all | solution.py:373
  22.9 3.3 %grads.1 = (bf16[512,1152]{1,0:T(8,128)(2,1)}, f32[192,16]{1,0:T(8,128)}) custom-call(bf16[192,1024]{1,0:T(8,128)(2,1)} %get-tuple-element.67.normed_ref, bf16[32,1024]{1,0:T(8,128)(2,1)} %bitcast.57, s32[2,192]{1,0:T(2,128)} %bitcast.54, s32[1,192]{1,0:T(1,128)} %bitcast.59, s32[2,192]{1,0:T(2,128)} %get-tuple-element.68.place_ref, bf16[192,1024]{1,0:T(8,128)(2,1)} %grad_ref.5), custom_call_target="tpu_custom_call" | custom-call | flops 99999997952 | bytes 1 | tf_op jit(solution)/shard_map/grads/pallas_call | solution.py:350
  26.2 2.1 collective-permute-done.1.refs_2_
  28.3 8.3 %collective-permute-done.refs_1_ = bf16[128,2048]{1,0:T(8,128)(2,1)S(1)} collective-permute-done((bf16[128,2048]{1,0:T(8,128)(2,1)}, bf16[128,2048]{1,0:T(8,128)(2,1)S(1)}, u32[]{:S(2)}, u32[]{:S(2)}) %collective-permute-start) | collective-permute-done | bytes 524320 | tf_op jit(solution)/shard_map/ppermute | solution.py:395
  36.6 1.2 collective-permute-done.2.refs_3_
  37.8 12.7 %all-to-all-done = bf16[32,16,1152]{2,1,0:T(8,128)(2,1)S(1)} async-done(((bf16[32,16,1152]{2,1,0:T(8,128)(2,1)}), bf16[32,16,1152]{2,1,0:T(8,128)(2,1)S(1)}, u32[]{:S(2)}, u32[]{:S(2)}) %all-to-all-start) | async-done | bytes 1179680 | tf_op jit(solution)/shard_map/all_to_all | solution.py:373
  50.5 7.0 %all-to-all-start.1 = ((bf16[32,16,1152]{2,1,0:T(8,128)(2,1)}), bf16[32,16,1152]{2,1,0:T(8,128)(2,1)S(1)}, u32[]{:S(2)}, u32[]{:S(2)}) async-start(bf16[32,16,1152]{2,1,0:T(8,128)(2,1)} %bitcast.37), calls=%async_computation.1 | async-start | bytes 2359296 | tf_op jit(solution)/shard_map/all_to_all | solution.py:373
  57.5 2.9 %collective-permute-start.5 = (bf16[128,2048]{1,0:T(8,128)(2,1)S(1)}, bf16[128,2048]{1,0:T(8,128)(2,1)}, u32[]{:S(2)}, u32[]{:S(2)}) collective-permute-start(bf16[128,2048]{1,0:T(8,128)(2,1)S(1)} %bitcast.35), channel_id=1, source_target_pairs={{0,32},{32,0},{64,96},{96,64},{128,160},{160,128},{192,224},{224,1... | collective-permute-start | bytes 1572872 | tf_op jit(solution)/shard_map/ppermute | solution.py:395
  61.2 0.6 pad_add_fusion.order_ref.holders_ref
  62.5 1.3 collective-permute-done.6.refs_5_
  64.3 1.0 collective-permute-done.8.refs_7_
  65.3 9.7 %first.1 = (bf16[576,1024]{1,0:T(8,128)(2,1)}, bf16[576,2048]{1,0:T(8,128)(2,1)}, f32[576,2048]{1,0:T(8,128)}, bf16[1024,576]{1,0:T(8,128)(2,1)}) custom-call(s32[8]{0:T(128)} %pad_add_fusion.order_ref.holders_ref, bf16[512,1152]{1,0:T(8,128)(2,1)} %bitcast.29, bf16[128,2048]{1,0:T(8,128)(2,1)} %bitcast.33, bf16[128,2048]{1,0:T(8,128)(2,1)} %copy-done.6, ...), custom_call_target="tpu_custom_call" | custom-call | flops 1 | bytes 1 | tf_op jit(solution)/shard_map/first/pallas_call | solution.py:350
  75.0 0.9 collective-permute-done.9.refs_2_
  75.9 1.2 collective-permute-start.12
  77.2 1.7 collective-permute-done.12.refs_6_
  78.9 0.8 copy-done.16
  79.7 9.1 %second.1 = (bf16[512,1152]{1,0:T(8,128)(2,1)}, bf16[2048,1024]{1,0:T(8,128)(2,1)}) custom-call(s32[8]{0:T(128)} %pad_add_fusion.order_ref.holders_ref, bf16[576,2048]{1,0:T(8,128)(2,1)} %get-tuple-element.76.hidden_ref, bf16[256,1024]{1,0:T(8,128)(2,1)} %bitcast.46, bf16[256,1024]{1,0:T(8,128)(2,1)} %collective-permute-done.3.refs_1_, ...), custom_call_target="tpu_custom_call" | custom-call | flops 1 | bytes 1 | tf_op jit(solution)/shard_map/second/pallas_call | solution.py:350
  88.8 9.5 %all-to-all-start.2 = ((bf16[32,16,1152]{2,1,0:T(8,128)(2,1)}), bf16[32,16,1152]{2,1,0:T(8,128)(2,1)S(1)}, u32[]{:S(2)}, u32[]{:S(2)}) async-start(bf16[32,16,1152]{2,1,0:T(8,128)(2,1)} %bitcast.38), calls=%async_computation.2 | async-start | bytes 2359296 | tf_op jit(solution)/shard_map/all_to_all | solution.py:373
  98.4 0.6 and_select_fusion.order_ref
  98.9 8.7 %outer.1 = (bf16[576,1024]{1,0:T(8,128)(2,1)}, bf16[4,256,1024]{2,1,0:T(8,128)(2,1)}, bf16[4,256,1024]{2,1,0:T(8,128)(2,1)}) custom-call(s32[4]{0:T(128)} %and_select_fusion.order_ref, s32[1]{0:T(128)} %bitcast.12.core_ref, bf16[512,1152]{1,0:T(8,128)(2,1)} %bitcast.28, bf16[576,2048]{1,0:T(8,128)(2,1)} %get-tuple-element.76.hidden_ref), custom_call_target="tpu_custom_call" | custom-call | flops 1 | bytes 1 | tf_op jit(solution)/shard_map/outer/pallas_call | solution.py:350
  107.7 0.7 collective-permute-start.14
  108.4 17.2 %backward.1 = (bf16[4,128,2048]{2,1,0:T(8,128)(2,1)}, bf16[4,128,2048]{2,1,0:T(8,128)(2,1)}, bf16[512,1152]{1,0:T(8,128)(2,1)}, f32[1,1024]{1,0:T(1,128)}) custom-call(s32[4]{0:T(128)} %and_select_fusion.order_ref, s32[8]{0:T(128)} %pad_add_fusion.order_ref.holders_ref, bf16[576,1024]{1,0:T(8,128)(2,1)} %get-tuple-element.84.grads_ref, ...), custom_call_target="tpu_custom_call" | custom-call | flops 1 | bytes 1 | tf_op jit(solution)/shard_map/backward/pallas_call | solution.py:350
  125.6 1.4 copy-done.3
  127.0 3.4 %out_pair.1 = (f32[256,1024]{1,0:T(8,128)}, bf16[256,1024]{1,0:T(8,128)(2,1)}, bf16[256,1024]{1,0:T(8,128)(2,1)}, bf16[256,1024]{1,0:T(8,128)(2,1)}) custom-call(bf16[4,256,1024]{2,1,0:T(8,128)(2,1)} %get-tuple-element.90.mine_ref, bf16[4,256,1024]{2,1,0:T(8,128)(2,1)} %copy-done.3), custom_call_target="tpu_custom_call" | custom-call | flops 1 | bytes 1 | tf_op jit(solution)/shard_map/out_pair/pallas_call | solution.py:350
  130.5 0.9 collective-permute-start.17
  131.9 1.0 copy-done.8
  132.9 6.0 %mix.1 = (bf16[192,1024]{1,0:T(8,128)(2,1)}, f32[192,1024]{1,0:T(8,128)}, bf16[512,1280]{1,0:T(8,128)(2,1)}) custom-call(bf16[512,1152]{1,0:T(8,128)(2,1)} %bitcast.39, bf16[192,1024]{1,0:T(8,128)(2,1)} %frames_ref.5, bf16[192,1024]{1,0:T(8,128)(2,1)} %get-tuple-element.67.normed_ref, bf16[192,1024]{1,0:T(8,128)(2,1)} %grad_ref.5, ...), custom_call_target="tpu_custom_call" | custom-call | flops 99999997952 | bytes 1 | tf_op jit(solution)/shard_map/mix/pallas_call | solution.py:350
  138.9 9.5 %all-to-all-start.3 = ((bf16[32,16,1280]{2,1,0:T(8,128)(2,1)}), bf16[32,16,1280]{2,1,0:T(8,128)(2,1)S(1)}, u32[]{:S(2)}, u32[]{:S(2)}) async-start(bf16[32,16,1280]{2,1,0:T(8,128)(2,1)} %bitcast.36), calls=%async_computation.3 | async-start | bytes 2621440 | tf_op jit(solution)/shard_map/all_to_all | solution.py:373
  148.4 8.9 %collective-permute-done.18.refs_2_ = bf16[256,1024]{1,0:T(8,128)(2,1)} collective-permute-done((bf16[256,1024]{1,0:T(8,128)(2,1)}, bf16[256,1024]{1,0:T(8,128)(2,1)}, u32[]{:S(2)}, u32[]{:S(2)}) %collective-permute-start.18) | collective-permute-done | bytes 524320 | tf_op jit(solution)/shard_map/ppermute | solution.py:395
  157.4 3.4 %in_pair.1 = (f32[128,2048]{1,0:T(8,128)}, bf16[128,2048]{1,0:T(8,128)(2,1)}, bf16[128,2048]{1,0:T(8,128)(2,1)}, bf16[128,2048]{1,0:T(8,128)(2,1)}) custom-call(bf16[4,128,2048]{2,1,0:T(8,128)(2,1)} %get-tuple-element.106.mine_ref, bf16[4,128,2048]{2,1,0:T(8,128)(2,1)} %collective-permute-done.15.theirs_ref), custom_call_target="tpu_custom_call" | custom-call | flops 99999997952 | bytes 1 | tf_op jit(solution)/shard_map/in_pair/pallas_call | solution.py:350
  160.8 0.9 collective-permute-start.20
  161.8 0.8 collective-permute-start.21
  162.5 16.9 %all-to-all-done.3 = bf16[32,16,1280]{2,1,0:T(8,128)(2,1)S(1)} async-done(((bf16[32,16,1280]{2,1,0:T(8,128)(2,1)}), bf16[32,16,1280]{2,1,0:T(8,128)(2,1)S(1)}, u32[]{:S(2)}, u32[]{:S(2)}) %all-to-all-start.3) | async-done | bytes 1310752 | tf_op jit(solution)/shard_map/all_to_all | solution.py:373
  179.8 0.8 broadcast_in_dim.33
  180.5 8.6 %all-to-all-start.4 = ((f32[8,8,256]{2,1,0:T(8,128)}), f32[8,8,256]{2,1,0:T(8,128)S(1)}, u32[]{:S(2)}, u32[]{:S(2)}) async-start(f32[8,8,256]{2,1,0:T(8,128)} %broadcast_in_dim.33), calls=%async_computation.4 | async-start | bytes 131072 | tf_op jit(solution)/shard_map/all_to_all | solution.py:439
  189.2 3.9 %finish.1 = bf16[192,1024]{1,0:T(8,128)(2,1)} custom-call(bf16[512,1280]{1,0:T(8,128)(2,1)} %bitcast.27, bf16[192,1024]{1,0:T(8,128)(2,1)} %frames_ref.5, f32[1,1024]{1,0:T(1,128)} %bitcast.50, bf16[192,1024]{1,0:T(8,128)(2,1)} %grad_ref.5, f32[192,16]{1,0:T(8,128)} %get-tuple-element.94.meta_ref, f32[192,1024]{1,0:T(8,128)} %get-tuple-element.113.base_ref), custom_call_target="tpu_custom_call" | custom-call | flops 1 | bytes 1 | tf_op jit(solution)/shard_map/finish/pallas_call | solution.py:350
  193.1 1.0 all-to-all-done.4
  194.1 0.7 fusion.1
  194.8 0.7 broadcast_in_dim.37
  195.4 5.4 %all-to-all-start.5 = ((f32[32,8,128]{2,1,0:T(8,128)}), f32[32,8,128]{2,1,0:T(8,128)S(1)}, u32[]{:S(2)}, u32[]{:S(2)}) async-start(f32[32,8,128]{2,1,0:T(8,128)} %broadcast_in_dim.37), calls=%async_computation.5 | async-start | bytes 262144 | tf_op jit(solution)/shard_map/all_to_all | solution.py:439
  200.9 4.4 %total.1 = (f32[256,1024]{1,0:T(8,128)}, f32[128,2048]{1,0:T(8,128)}) custom-call(f32[256,1024]{1,0:T(8,128)} %get-tuple-element.115.first_ref, f32[128,2048]{1,0:T(8,128)} %get-tuple-element.116.second_ref, bf16[256,1024]{1,0:T(8,128)(2,1)} %copy-done.9, bf16[256,1024]{1,0:T(8,128)(2,1)} %collective-permute-done.17.refs_1_, ...), custom_call_target="tpu_custom_call" | custom-call | flops 1 | bytes 1 | tf_op jit(solution)/shard_map/total/pallas_call | solution.py:350
  205.2 5.0 %all-to-all-done.5 = f32[32,8,128]{2,1,0:T(8,128)S(1)} async-done(((f32[32,8,128]{2,1,0:T(8,128)}), f32[32,8,128]{2,1,0:T(8,128)S(1)}, u32[]{:S(2)}, u32[]{:S(2)}) %all-to-all-start.5) | async-done | bytes 131104 | tf_op jit(solution)/shard_map/all_to_all | solution.py:439
  210.2 0.7 copy.16
  (64 shorter events, 3.6 us)
Async XLA Ops:
  0.6 27.6 %collective-permute-start.3 = (bf16[256,1024]{1,0:T(8,128)(2,1)}, bf16[256,1024]{1,0:T(8,128)(2,1)}, u32[]{:S(2)}, u32[]{:S(2)}) collective-permute-start(bf16[256,1024]{1,0:T(8,128)(2,1)} %bitcast.42), channel_id=1, source_target_pairs={{0,64},{32,96},{64,128},{96,160},{128,192},{160,224},{192,0},{224,... | collective-permute-start | bytes 1572872 | tf_op jit(solution)/shard_map/ppermute | solution.py:395
  2.8 25.4 %collective-permute-start.4 = (bf16[256,1024]{1,0:T(8,128)(2,1)}, bf16[256,1024]{1,0:T(8,128)(2,1)}, u32[]{:S(2)}, u32[]{:S(2)}) collective-permute-start(bf16[256,1024]{1,0:T(8,128)(2,1)} %bitcast.43), channel_id=1, source_target_pairs={{0,192},{32,224},{64,0},{96,32},{128,64},{160,96},{192,128},{224,1... | collective-permute-start | bytes 1572872 | tf_op jit(solution)/shard_map/ppermute | solution.py:395
  4.4 23.9 %collective-permute-start.1 = (bf16[128,2048]{1,0:T(8,128)(2,1)}, bf16[128,2048]{1,0:T(8,128)(2,1)S(1)}, u32[]{:S(2)}, u32[]{:S(2)}) collective-permute-start(bf16[128,2048]{1,0:T(8,128)(2,1)} %bitcast.30), channel_id=1, source_target_pairs={{0,128},{32,160},{64,192},{96,224},{128,0},{160,32},{192,64},{224,... | collective-permute-start | bytes 1572872 | tf_op jit(solution)/shard_map/ppermute | solution.py:395
  5.9 30.6 %collective-permute-start = (bf16[128,2048]{1,0:T(8,128)(2,1)}, bf16[128,2048]{1,0:T(8,128)(2,1)S(1)}, u32[]{:S(2)}, u32[]{:S(2)}) collective-permute-start(bf16[128,2048]{1,0:T(8,128)(2,1)} %bitcast.31), channel_id=1, source_target_pairs={{0,64},{32,96},{64,128},{96,160},{128,192},{160,224},{192,0},{224,... | collective-permute-start | bytes 1572872 | tf_op jit(solution)/shard_map/ppermute | solution.py:395
  6.3 31.5 %collective-permute-start.2 = (bf16[128,2048]{1,0:T(8,128)(2,1)}, bf16[128,2048]{1,0:T(8,128)(2,1)S(1)}, u32[]{:S(2)}, u32[]{:S(2)}) collective-permute-start(bf16[128,2048]{1,0:T(8,128)(2,1)} %bitcast.32), channel_id=1, source_target_pairs={{0,192},{32,224},{64,0},{96,32},{128,64},{160,96},{192,128},{224,1... | collective-permute-start | bytes 1572872 | tf_op jit(solution)/shard_map/ppermute | solution.py:395
  11.8 38.7 %all-to-all-start = ((bf16[32,16,1152]{2,1,0:T(8,128)(2,1)}), bf16[32,16,1152]{2,1,0:T(8,128)(2,1)S(1)}, u32[]{:S(2)}, u32[]{:S(2)}) async-start(bf16[32,16,1152]{2,1,0:T(8,128)(2,1)} %bitcast.40), calls=%async_computation | async-start | bytes 2359296 | tf_op jit(solution)/shard_map/all_to_all | solution.py:373
  26.2 31.3 %copy-start.4 = (bf16[1,128,2048]{2,1,0:T(8,128)(2,1)S(1)}, bf16[1,128,2048]{2,1,0:T(8,128)(2,1)}, u32[]{:S(2)}) copy-start(bf16[1,128,2048]{2,1,0:T(8,128)(2,1)} %param.11) | copy-start | bytes 1572868
  28.3 37.0 %copy-start.5 = (bf16[128,2048]{1,0:T(8,128)(2,1)}, bf16[128,2048]{1,0:T(8,128)(2,1)S(1)}, u32[]{:S(2)}) copy-start(bf16[128,2048]{1,0:T(8,128)(2,1)S(1)} %collective-permute-done.1.refs_2_) | copy-start | bytes 1572868
  36.6 13.9 %copy-start.6 = (bf16[128,2048]{1,0:T(8,128)(2,1)}, bf16[128,2048]{1,0:T(8,128)(2,1)S(1)}, u32[]{:S(2)}) copy-start(bf16[128,2048]{1,0:T(8,128)(2,1)S(1)} %collective-permute-done.refs_1_) | copy-start | bytes 1572868
  37.8 12.7 %copy-start.7 = (bf16[128,2048]{1,0:T(8,128)(2,1)}, bf16[128,2048]{1,0:T(8,128)(2,1)S(1)}, u32[]{:S(2)}) copy-start(bf16[128,2048]{1,0:T(8,128)(2,1)S(1)} %collective-permute-done.2.refs_3_) | copy-start | bytes 1572868
  50.5 14.8 %copy-start.2 = (bf16[32,16,1152]{2,1,0:T(8,128)(2,1)}, bf16[32,16,1152]{2,1,0:T(8,128)(2,1)S(1)}, u32[]{:S(2)}) copy-start(bf16[32,16,1152]{2,1,0:T(8,128)(2,1)S(1)} %all-to-all-done) | copy-start | bytes 3538948
  50.5 38.3 %all-to-all-start.1 = ((bf16[32,16,1152]{2,1,0:T(8,128)(2,1)}), bf16[32,16,1152]{2,1,0:T(8,128)(2,1)S(1)}, u32[]{:S(2)}, u32[]{:S(2)}) async-start(bf16[32,16,1152]{2,1,0:T(8,128)(2,1)} %bitcast.37), calls=%async_computation.1 | async-start | bytes 2359296 | tf_op jit(solution)/shard_map/all_to_all | solution.py:373
  57.5 4.5 %collective-permute-start.5 = (bf16[128,2048]{1,0:T(8,128)(2,1)S(1)}, bf16[128,2048]{1,0:T(8,128)(2,1)}, u32[]{:S(2)}, u32[]{:S(2)}) collective-permute-start(bf16[128,2048]{1,0:T(8,128)(2,1)S(1)} %bitcast.35), channel_id=1, source_target_pairs={{0,32},{32,0},{64,96},{96,64},{128,160},{160,128},{192,224},{224,1... | collective-permute-start | bytes 1572872 | tf_op jit(solution)/shard_map/ppermute | solution.py:395
  60.4 3.4 %collective-permute-start.6 = (bf16[128,2048]{1,0:T(8,128)(2,1)}, bf16[128,2048]{1,0:T(8,128)(2,1)}, u32[]{:S(2)}, u32[]{:S(2)}) collective-permute-start(bf16[128,2048]{1,0:T(8,128)(2,1)} %copy-done.6), channel_id=1, source_target_pairs={{0,32},{32,0},{64,96},{96,64},{128,160},{160,128},{192,224},{224,1... | collective-permute-start | bytes 1572872 | tf_op jit(solution)/shard_map/ppermute | solution.py:395
  60.5 3.7 %collective-permute-start.7 = (bf16[128,2048]{1,0:T(8,128)(2,1)S(1)}, bf16[128,2048]{1,0:T(8,128)(2,1)}, u32[]{:S(2)}, u32[]{:S(2)}) collective-permute-start(bf16[128,2048]{1,0:T(8,128)(2,1)S(1)} %collective-permute-done.1.refs_2_), channel_id=1, source_target_pairs={{0,32},{32,0},{64,96},{96,64},{128,160},{160,128},{192,224},{224,1... | collective-permute-start | bytes 1572872 | tf_op jit(solution)/shard_map/ppermute | solution.py:395
  60.9 4.4 %collective-permute-start.8 = (bf16[128,2048]{1,0:T(8,128)(2,1)}, bf16[128,2048]{1,0:T(8,128)(2,1)}, u32[]{:S(2)}, u32[]{:S(2)}) collective-permute-start(bf16[128,2048]{1,0:T(8,128)(2,1)} %copy-done.7), channel_id=1, source_target_pairs={{0,32},{32,0},{64,96},{96,64},{128,160},{160,128},{192,224},{224,1... | collective-permute-start | bytes 1572872 | tf_op jit(solution)/shard_map/ppermute | solution.py:395
  61.0 14.9 %collective-permute-start.9 = (bf16[256,1024]{1,0:T(8,128)(2,1)}, bf16[256,1024]{1,0:T(8,128)(2,1)}, u32[]{:S(2)}, u32[]{:S(2)}) collective-permute-start(bf16[256,1024]{1,0:T(8,128)(2,1)} %bitcast.44), channel_id=1, source_target_pairs={{0,128},{32,160},{64,192},{96,224},{128,0},{160,32},{192,64},{224,... | collective-permute-start | bytes 1572872 | tf_op jit(solution)/shard_map/ppermute | solution.py:395
  62.0 15.1 %collective-permute-start.10 = (bf16[256,1024]{1,0:T(8,128)(2,1)}, bf16[256,1024]{1,0:T(8,128)(2,1)S(1)}, u32[]{:S(2)}, u32[]{:S(2)}) collective-permute-start(bf16[256,1024]{1,0:T(8,128)(2,1)} %bitcast.45), channel_id=1, source_target_pairs={{0,32},{32,0},{64,96},{96,64},{128,160},{160,128},{192,224},{224,1... | collective-permute-start | bytes 1572872 | tf_op jit(solution)/shard_map/ppermute | solution.py:395
  63.8 13.4 %collective-permute-start.11 = (bf16[256,1024]{1,0:T(8,128)(2,1)}, bf16[256,1024]{1,0:T(8,128)(2,1)S(1)}, u32[]{:S(2)}, u32[]{:S(2)}) collective-permute-start(bf16[256,1024]{1,0:T(8,128)(2,1)} %collective-permute-done.3.refs_1_), channel_id=1, source_target_pairs={{0,32},{32,0},{64,96},{96,64},{128,160},{160,128},{192,224},{224,1... | collective-permute-start | bytes 1572872 | tf_op jit(solution)/shard_map/ppermute | solution.py:395
  64.1 13.0 %collective-permute-start.13 = (bf16[256,1024]{1,0:T(8,128)(2,1)}, bf16[256,1024]{1,0:T(8,128)(2,1)S(1)}, u32[]{:S(2)}, u32[]{:S(2)}) collective-permute-start(bf16[256,1024]{1,0:T(8,128)(2,1)} %collective-permute-done.4.refs_3_), channel_id=1, source_target_pairs={{0,32},{32,0},{64,96},{96,64},{128,160},{160,128},{192,224},{224,1... | collective-permute-start | bytes 1572872 | tf_op jit(solution)/shard_map/ppermute | solution.py:395
  75.9 3.0 %collective-permute-start.12 = (bf16[256,1024]{1,0:T(8,128)(2,1)}, bf16[256,1024]{1,0:T(8,128)(2,1)S(1)}, u32[]{:S(2)}, u32[]{:S(2)}) collective-permute-start(bf16[256,1024]{1,0:T(8,128)(2,1)} %collective-permute-done.9.refs_2_), channel_id=1, source_target_pairs={{0,32},{32,0},{64,96},{96,64},{128,160},{160,128},{192,224},{224,1... | collective-permute-start | bytes 1572872 | tf_op jit(solution)/shard_map/ppermute | solution.py:395
  77.2 1.7 copy-start.13
  77.2 1.7 copy-start.14
  77.2 1.7 copy-start.15
  78.9 0.8 copy-start.16
  88.8 10.1 %copy-start.1 = (bf16[32,16,1152]{2,1,0:T(8,128)(2,1)}, bf16[32,16,1152]{2,1,0:T(8,128)(2,1)S(1)}, u32[]{:S(2)}) copy-start(bf16[32,16,1152]{2,1,0:T(8,128)(2,1)S(1)} %all-to-all-done.1) | copy-start | bytes 3538948
  88.8 43.0 %all-to-all-start.2 = ((bf16[32,16,1152]{2,1,0:T(8,128)(2,1)}), bf16[32,16,1152]{2,1,0:T(8,128)(2,1)S(1)}, u32[]{:S(2)}, u32[]{:S(2)}) async-start(bf16[32,16,1152]{2,1,0:T(8,128)(2,1)} %bitcast.38), calls=%async_computation.2 | async-start | bytes 2359296 | tf_op jit(solution)/shard_map/all_to_all | solution.py:373
  107.7 17.9 %collective-permute-start.14 = (bf16[4,256,1024]{2,1,0:T(8,128)(2,1)}, bf16[4,256,1024]{2,1,0:T(8,128)(2,1)S(1)}, u32[]{:S(2)}, u32[]{:S(2)}) collective-permute-start(bf16[4,256,1024]{2,1,0:T(8,128)(2,1)} %get-tuple-element.91), channel_id=1, source_target_pairs={{0,32},{32,0},{64,96},{96,64},{128,160},{160,128},{192,224},{224,1... | collective-permute-start | bytes 6291464 | tf_op jit(solution)/shard_map/ppermute | solution.py:395
  125.5 22.9 %collective-permute-start.15 = (bf16[4,128,2048]{2,1,0:T(8,128)(2,1)}, bf16[4,128,2048]{2,1,0:T(8,128)(2,1)}, u32[]{:S(2)}, u32[]{:S(2)}) collective-permute-start(bf16[4,128,2048]{2,1,0:T(8,128)(2,1)} %get-tuple-element.99), channel_id=1, source_target_pairs={{0,32},{32,0},{64,96},{96,64},{128,160},{160,128},{192,224},{224,1... | collective-permute-start | bytes 6291464 | tf_op jit(solution)/shard_map/ppermute | solution.py:395
  125.6 1.4 copy-start.3
  130.4 18.0 %collective-permute-start.16 = (bf16[256,1024]{1,0:T(8,128)(2,1)}, bf16[256,1024]{1,0:T(8,128)(2,1)S(1)}, u32[]{:S(2)}, u32[]{:S(2)}) collective-permute-start(bf16[256,1024]{1,0:T(8,128)(2,1)} %get-tuple-element.100), channel_id=1, source_target_pairs={{0,192},{32,224},{64,0},{96,32},{128,64},{160,96},{192,128},{224,1... | collective-permute-start | bytes 1572872 | tf_op jit(solution)/shard_map/ppermute | solution.py:395
  130.5 18.0 %collective-permute-start.17 = (bf16[256,1024]{1,0:T(8,128)(2,1)}, bf16[256,1024]{1,0:T(8,128)(2,1)}, u32[]{:S(2)}, u32[]{:S(2)}) collective-permute-start(bf16[256,1024]{1,0:T(8,128)(2,1)} %get-tuple-element.101), channel_id=1, source_target_pairs={{0,128},{32,160},{64,192},{96,224},{128,0},{160,32},{192,64},{224,... | collective-permute-start | bytes 1572872 | tf_op jit(solution)/shard_map/ppermute | solution.py:395
  131.3 26.0 %collective-permute-start.18 = (bf16[256,1024]{1,0:T(8,128)(2,1)}, bf16[256,1024]{1,0:T(8,128)(2,1)}, u32[]{:S(2)}, u32[]{:S(2)}) collective-permute-start(bf16[256,1024]{1,0:T(8,128)(2,1)} %get-tuple-element.102), channel_id=1, source_target_pairs={{0,64},{32,96},{64,128},{96,160},{128,192},{160,224},{192,0},{224,... | collective-permute-start | bytes 1572872 | tf_op jit(solution)/shard_map/ppermute | solution.py:395
  131.9 1.0 copy-start.8
  138.9 40.5 %all-to-all-start.3 = ((bf16[32,16,1280]{2,1,0:T(8,128)(2,1)}), bf16[32,16,1280]{2,1,0:T(8,128)(2,1)S(1)}, u32[]{:S(2)}, u32[]{:S(2)}) async-start(bf16[32,16,1280]{2,1,0:T(8,128)(2,1)} %bitcast.36), calls=%async_computation.3 | async-start | bytes 2621440 | tf_op jit(solution)/shard_map/all_to_all | solution.py:373
  148.4 12.4 %copy-start.9 = (bf16[256,1024]{1,0:T(8,128)(2,1)}, bf16[256,1024]{1,0:T(8,128)(2,1)S(1)}, u32[]{:S(2)}) copy-start(bf16[256,1024]{1,0:T(8,128)(2,1)S(1)} %collective-permute-done.16.refs_0_) | copy-start | bytes 1572868
  160.8 33.3 %collective-permute-start.19 = (bf16[128,2048]{1,0:T(8,128)(2,1)}, bf16[128,2048]{1,0:T(8,128)(2,1)S(1)}, u32[]{:S(2)}, u32[]{:S(2)}) collective-permute-start(bf16[128,2048]{1,0:T(8,128)(2,1)} %get-tuple-element.110), channel_id=1, source_target_pairs={{0,192},{32,224},{64,0},{96,32},{128,64},{160,96},{192,128},{224,1... | collective-permute-start | bytes 1572872 | tf_op jit(solution)/shard_map/ppermute | solution.py:395
  160.8 33.2 %collective-permute-start.20 = (bf16[128,2048]{1,0:T(8,128)(2,1)}, bf16[128,2048]{1,0:T(8,128)(2,1)S(1)}, u32[]{:S(2)}, u32[]{:S(2)}) collective-permute-start(bf16[128,2048]{1,0:T(8,128)(2,1)} %get-tuple-element.111), channel_id=1, source_target_pairs={{0,128},{32,160},{64,192},{96,224},{128,0},{160,32},{192,64},{224,... | collective-permute-start | bytes 1572872 | tf_op jit(solution)/shard_map/ppermute | solution.py:395
  161.8 32.3 %collective-permute-start.21 = (bf16[128,2048]{1,0:T(8,128)(2,1)}, bf16[128,2048]{1,0:T(8,128)(2,1)S(1)}, u32[]{:S(2)}, u32[]{:S(2)}) collective-permute-start(bf16[128,2048]{1,0:T(8,128)(2,1)} %get-tuple-element.112), channel_id=1, source_target_pairs={{0,64},{32,96},{64,128},{96,160},{128,192},{160,224},{192,0},{224,... | collective-permute-start | bytes 1572872 | tf_op jit(solution)/shard_map/ppermute | solution.py:395
  179.4 9.7 %copy-start = (bf16[32,16,1280]{2,1,0:T(8,128)(2,1)}, bf16[32,16,1280]{2,1,0:T(8,128)(2,1)S(1)}, u32[]{:S(2)}) copy-start(bf16[32,16,1280]{2,1,0:T(8,128)(2,1)S(1)} %all-to-all-done.3) | copy-start | bytes 3932164
  180.5 13.5 %all-to-all-start.4 = ((f32[8,8,256]{2,1,0:T(8,128)}), f32[8,8,256]{2,1,0:T(8,128)S(1)}, u32[]{:S(2)}, u32[]{:S(2)}) async-start(f32[8,8,256]{2,1,0:T(8,128)} %broadcast_in_dim.33), calls=%async_computation.4 | async-start | bytes 131072 | tf_op jit(solution)/shard_map/all_to_all | solution.py:439
  194.1 6.8 %copy-start.10 = (bf16[128,2048]{1,0:T(8,128)(2,1)}, bf16[128,2048]{1,0:T(8,128)(2,1)S(1)}, u32[]{:S(2)}) copy-start(bf16[128,2048]{1,0:T(8,128)(2,1)S(1)} %collective-permute-done.19.refs_3_) | copy-start | bytes 1572868
  194.1 6.8 %copy-start.11 = (bf16[128,2048]{1,0:T(8,128)(2,1)}, bf16[128,2048]{1,0:T(8,128)(2,1)S(1)}, u32[]{:S(2)}) copy-start(bf16[128,2048]{1,0:T(8,128)(2,1)S(1)} %collective-permute-done.20.refs_4_) | copy-start | bytes 1572868
  194.1 6.8 %copy-start.12 = (bf16[128,2048]{1,0:T(8,128)(2,1)}, bf16[128,2048]{1,0:T(8,128)(2,1)S(1)}, u32[]{:S(2)}) copy-start(bf16[128,2048]{1,0:T(8,128)(2,1)S(1)} %collective-permute-done.21.refs_5_) | copy-start | bytes 1572868
  195.4 14.8 %all-to-all-start.5 = ((f32[32,8,128]{2,1,0:T(8,128)}), f32[32,8,128]{2,1,0:T(8,128)S(1)}, u32[]{:S(2)}, u32[]{:S(2)}) async-start(f32[32,8,128]{2,1,0:T(8,128)} %broadcast_in_dim.37), calls=%async_computation.5 | async-start | bytes 262144 | tf_op jit(solution)/shard_map/all_to_all | solution.py:439

commit v3 on v2

--- a/solution.py
+++ b/solution.py
@@ -46,6 +46,14 @@
     main = peers * MAIN
     out_ref[:, :width] = rows[:main]
     out_ref[:, width : width + LANES] = spread_pieces(rows[main:], peers)
+
+
+def pack_halves(rows, left_ref, right_ref, peers):
+    main, cut = peers * MAIN, left_ref.shape[1]
+    rest = rows.shape[1] - cut
+    left_ref[...] = rows[:main, :cut]
+    right_ref[:, :rest] = rows[:main, cut:]
+    right_ref[:, rest : rest + LANES] = spread_pieces(rows[main:], peers)
 
 
 def spread_pieces(extra, peers):
@@ -213,7 +221,7 @@
 def backward_kernel(
     peers, order_ref, holders_ref, grads_ref, derivative_ref, out_weights_ref, turned_ref, incoming_ref, gain_ref, *refs
 ):
-    pieces, (in_theirs_ref, in_mine_ref, back_ref, gain_part_ref, rows_ref, in_ref) = refs[:-6], refs[-6:]
+    pieces, (in_theirs_ref, in_mine_ref, left_ref, right_ref, gain_part_ref, rows_ref, in_ref) = refs[:-7], refs[-7:]
     step = pl.program_id(0)
     half, depth = in_mine_ref.shape[0], in_mine_ref.shape[1]
     assemble(holders_ref, pieces, in_ref)
@@ -236,15 +244,30 @@
     @pl.when(step == pl.num_programs(0) - 1)
     def _():
         done = rows_ref[...].astype(bf16)
-        pack(done, back_ref, peers)
+        pack_halves(done, left_ref, right_ref, peers)
         total = jnp.sum(done.astype(f32) * incoming_ref[...].astype(f32), axis=0, keepdims=True)
         gain_part_ref[...] = total / gain_ref[...]
 
 
 def tally_kernel(peers, packed_ref, out_ref):
     rows = join_pieces(packed_ref[...], peers).astype(f32)
-    out_ref[0:1] = jnp.sum(rows[:peers], axis=0, keepdims=True)
-    out_ref[1:2] = jnp.sum(rows[peers:], axis=0, keepdims=True)
+    width = out_ref.shape[2]
+    for k in range(2):
+        total = jnp.sum(rows[k * peers : (k + 1) * peers], axis=0, keepdims=True)
+        for j in range(4):
+            out_ref[:, 4 * k + j] = jnp.broadcast_to(
+                total[:, j * width : (j + 1) * width], (out_ref.shape[0], width)
+            )
+
+
+def sum_kernel(sums_ref, router_ref, gain_ref):
+    total = jnp.sum(sums_ref[...], axis=0)
+    width = total.shape[1]
+    for j in range(4):
+        gain_ref[:, j * width : (j + 1) * width] = total[4 + j : 5 + j]
+    for j in range(8):
+        row = total[j // 2 : j // 2 + 1, (j % 2) * LANES : (j % 2 + 1) * LANES]
+        router_ref[:, j] = jnp.broadcast_to(row, (router_ref.shape[0], LANES))
 
 
 def pair_kernel(mine_ref, theirs_ref, kept_ref, *out_refs):
@@ -263,40 +286,34 @@
         out_ref[...] = total
 
 
-def mix_kernel(
-    peers, packed_ref, frames_ref, normed_ref, grad_ref, meta_ref, router_ref,
-    packed_grads_ref, gain_expert_ref, mixed_ref, base_ref, out_ref,
+def picks(packed_ref, meta, peers):
+    main, extra = unpack(packed_ref, peers)
+    cut = peers * MAIN
+    lane = iota((meta.shape[0], cut), 1)
+    lane_extra = iota((meta.shape[0], 2 * peers), 1) + cut
+    return [
+        matmul(indicator(lane == place), main) + matmul(indicator(lane_extra == place), extra)
+        for place in (meta[:, k : k + 1].astype(jnp.int32) for k in range(2))
+    ]
+
+
+def route_kernel(
+    peers, packed_ref, normed_ref, grad_ref, meta_ref, router_ref, gain_ref, gain_expert_ref, _, out_ref, logits_ref
 ):
-    main, extra = unpack(packed_ref, peers)
     meta = meta_ref[...]
-    column = [meta[:, k : k + 1] for k in range(9)]
-    count = meta.shape[0]
-    places = [c.astype(jnp.int32) for c in column[0:2]]
-    experts = [c.astype(jnp.int32) for c in column[2:4]]
-    weights, scores = column[4:6], column[6:8]
-    cut = peers * MAIN
-    lane = iota((count, cut), 1)
-    lane_extra = iota((count, 2 * peers), 1) + cut
+    experts = [meta[:, k : k + 1].astype(jnp.int32) for k in (2, 3)]
+    scores, live = [meta[:, k : k + 1] for k in (6, 7)], meta[:, 8:9]
     grad = grad_ref[...].astype(f32)
-    picked = [
-        matmul(indicator(lane == p), main) + matmul(indicator(lane_extra == p), extra)
-        for p in places
-    ]
-    floats, standardized, _ = layer_norm(frames_ref)
-    mixed = floats + (weights[0] * picked[0] + weights[1] * picked[1])
-    mixed_ref[...] = mixed.astype(bf16)
-    grad_weight = [jnp.sum(grad * p, axis=1, keepdims=True) for p in picked]
+    grad_weight = [jnp.sum(grad * p, axis=1, keepdims=True) for p in picks(packed_ref, meta, peers)]
     total = scores[0] + scores[1]
-    gap = column[8] * (grad_weight[0] - grad_weight[1]) / (total * total)
+    gap = live * (grad_weight[0] - grad_weight[1]) / (total * total)
     first = gap * scores[1] * scores[0] * (1.0 - scores[0])
     second = -gap * scores[0] * scores[1] * (1.0 - scores[1])
-    which = iota((count, peers), 1)
+    which = iota((meta.shape[0], peers), 1)
     grad_logits = jnp.where(which == experts[0], first, 0.0) + jnp.where(
         which == experts[1], second, 0.0
     )
-    base = matmul(grad_logits, router_ref[...].astype(f32), precision=lax.Precision.HIGHEST)
-    base_ref[...] = base
-    gain_part = gain_expert_ref[...] + jnp.sum(base * standardized, axis=0, keepdims=True)
+    logits_ref[...] = grad_logits
     router_part = lax.dot_general(
         grad_logits,
         normed_ref[...].astype(f32),
@@ -304,16 +321,26 @@
         precision=lax.Precision.HIGHEST,
         preferred_element_type=f32,
     )
+    gain_part = jnp.sum(router_part * router_ref[...].astype(f32), axis=0, keepdims=True) / gain_ref[...]
+    gain_part += gain_expert_ref[...]
     sums = jnp.concatenate([router_part, jnp.broadcast_to(gain_part, router_part.shape)], axis=0)
-    start = packed_grads_ref.shape[1]
-    out_ref[:, :start] = packed_grads_ref[...]
-    out_ref[:, start:] = spread_pieces(sums.astype(bf16), peers)
+    out_ref[...] = spread_pieces(sums.astype(bf16), peers)
+
+
+def mixed_kernel(peers, packed_ref, frames_ref, meta_ref, mixed_ref):
+    meta = meta_ref[...]
+    picked = picks(packed_ref, meta, peers)
+    mixed_ref[...] = (
+        frames_ref[...].astype(f32) + (meta[:, 4:5] * picked[0] + meta[:, 5:6] * picked[1])
+    ).astype(bf16)
 
 
 def finish_kernel(
-    peers, packed_ref, frames_ref, gain_ref, grad_ref, meta_ref, base_ref, out_ref
+    peers, left_ref, right_ref, frames_ref, gain_ref, grad_ref, meta_ref, logits_ref, router_ref, out_ref
 ):
-    main, extra = unpack(packed_ref, peers)
+    rest = frames_ref.shape[1] - left_ref.shape[1]
+    main = jnp.concatenate([left_ref[...], right_ref[:, :rest]], axis=1)
+    extra = join_pieces(right_ref[:, rest : rest + LANES], peers)
     meta = meta_ref[...]
     count = meta.shape[0]
     places = [meta[:, k : k + 1].astype(jnp.int32) for k in range(2)]
@@ -324,7 +351,9 @@
         indicator((lane_extra == places[0]) | (lane_extra == places[1])), extra
     )
     _, standardized, inverse = layer_norm(frames_ref)
-    grad_normed = grad_moe + base_ref[...]
+    grad_normed = grad_moe + matmul(
+        logits_ref[...], router_ref[...].astype(f32), precision=lax.Precision.HIGHEST
+    )
     g = grad_normed * gain_ref[...]
     statistic = inverse * (
         g
@@ -334,7 +363,7 @@
     out_ref[...] = (grad_ref[...].astype(f32) + statistic).astype(bf16)
 
 
-def call(kernel, name, *outs, grid=None, in_blocks=None, out_blocks=None, scratch=(), mib=58, order=(), cost=1):
+def call(kernel, name, *outs, grid=None, in_blocks=None, out_blocks=None, scratch=(), mib=58, order=(), cost=1, aliases=None):
     def spec(block, array):
         if block is None:
             dims = array.shape
@@ -360,6 +389,7 @@
             compiler_params=pltpu.CompilerParams(vmem_limit_bytes=mib * 1024 * 1024),
             cost_estimate=pl.CostEstimate(flops=cost, bytes_accessed=1, transcendentals=0),
             name=name,
+            input_output_aliases=aliases or {},
         )(*order, *args)
 
     return run
@@ -435,10 +465,6 @@
     )(*kept, *parts[0], *parts[1])
 
 
-def everyones(mine, axis, size):
-    return lax.all_to_all(jnp.broadcast_to(mine[None], (size,) + mine.shape), axis, 0, 0, tiled=True)
-
-
 def on_device(groups, frames, gain, router, w_in, w_out, expert_ids, frame_mask, out_grad):
     count, width = frames.shape
     peers = router.shape[1]
@@ -454,20 +480,21 @@
     half = groups // 2
 
     sent, normed, place = call(
-        part(dispatch_kernel, peers), "dispatch", packed, shape(count, width), shape(2, count, dtype=jnp.int32)
+        part(dispatch_kernel, peers), "dispatch", packed, shape(count, width), shape(2, count, dtype=jnp.int32), cost=LONG
     )(frames, gain, ids)
     arrived = exchange(sent, peers)
     sent_grads, meta = call(
         part(grads_kernel, peers), "grads", packed, shape(count, 16, dtype=f32), cost=LONG
     )(normed, router_rows, ids, frame_mask[None], place, out_grad)
     pieces_in = [y.send(w_in[0], k) for k in range(half)]
-    pieces_out = [y.send(w_out[0], k) if k != 2 else None for k in range(half)]
-    later, _ = lax.optimization_barrier((w_out[0], pieces_in[2]))
-    pieces_out[2] = y.send(later, 2)
+    shard, _, pieces_in = lax.optimization_barrier((w_out[0], meta, pieces_in))
+    pieces_in += [core.send(piece, 1) for piece in pieces_in]
+    pieces_out = [y.send(shard, k) if k != 2 else None for k in range(half)]
+    shard, _ = lax.optimization_barrier((shard, pieces_out[1]))
+    pieces_out[2] = y.send(shard, 2)
     sent_grads, pieces_in, pieces_out[1], pieces_out[3] = lax.optimization_barrier(
         (sent_grads, pieces_in, pieces_out[1], pieces_out[3])
     )
-    pieces_in += [core.send(piece, 1) for piece in pieces_in]
     arrived_grads = exchange(sent_grads, peers)
 
     inner = w_in.shape[2]
@@ -517,11 +544,12 @@
         out_blocks=(None, whole, whole),
         order=(y.behind(), core.place[None].astype(jnp.int32)),
     )(arrived_grads, hidden)
-    in_theirs, in_mine, packed_grads, gain_expert = call(
+    cut = width // 2 + LANES
+    in_theirs, in_mine, left, right, gain_expert = call(
         part(backward_kernel, peers),
         "backward",
         *[shape(half, width // groups, inner)] * 2,
-        packed,
+        *[shape(peers * MAIN, cut)] * 2,
         shape(1, width, dtype=f32),
         grid=half,
         in_blocks=(
@@ -533,36 +561,46 @@
             None,
         )
         + (((width // groups, block), lambda i, order, *_: (0, order[i])),) * groups,
-        out_blocks=(split, split, None, None),
+        out_blocks=(split, split, None, None, None),
         scratch=[pltpu.VMEM((rows, width), f32), pltpu.VMEM((width, block), bf16)],
         order=(y.behind(), holders),
     )(grad_incoming, derivative, weights_out, turned, incoming, gain, *pieces_in)
-    out_kept, out_parts = pair_sums(out_mine, core.send(out_theirs, 1), y, "out_pair")
-    arrived_in, out_parts = lax.optimization_barrier((core.send(in_theirs, 1), out_parts))
-    in_kept, in_parts = pair_sums(in_mine, arrived_in, y, "in_pair", cost=LONG)
-    returned, packed_grads, out_kept = lax.optimization_barrier((returned, packed_grads, out_kept))
-
-    mixed, base, sent_back = call(
-        part(mix_kernel, peers),
-        "mix",
-        shape(count, width),
-        shape(count, width, dtype=f32),
-        shape(peers * MAIN, width + 2 * LANES),
+    arrived_out, _ = lax.optimization_barrier((core.send(out_theirs, 1), returned))
+    out_kept, out_parts = pair_sums(out_mine, arrived_out, y, "out_pair")
+    arrived_in, _ = lax.optimization_barrier((core.send(in_theirs, 1), out_kept))
+    in_kept, in_parts = pair_sums(in_mine, arrived_in, y, "in_pair")
+    back_left = exchange(left, peers)
+
+    last = ((peers * MAIN, LANES), lambda i: (0, cut // LANES - 1))
+    sent_back, grad_logits = call(
+        part(route_kernel, peers),
+        "route",
+        shape(peers * MAIN, cut),
+        shape(count, peers, dtype=f32),
+        in_blocks=(None,) * 7 + ("any",),
+        out_blocks=(last, None),
         cost=LONG,
-    )(returned, frames, normed, out_grad, meta, router_rows, packed_grads, gain_expert)
+        aliases={7: 0},
+    )(returned, normed, out_grad, meta, router_rows, gain, gain_expert, right)
+    sent_back, back_left, in_kept = lax.optimization_barrier((sent_back, back_left, in_kept))
     back = exchange(sent_back, peers)
-    back, out_parts, in_kept = lax.optimization_barrier((back, out_parts, in_kept))
-    last = ((peers * MAIN, LANES), lambda i: (0, 1 + width // LANES))
-    sums = call(part(tally_kernel, peers), "tally", shape(2, width, dtype=f32), in_blocks=(last,), mib=4)(back)
-    sums = jnp.sum(everyones(sums.reshape(8, 2 * width // 8), "dp", groups), axis=0).reshape(2, width)
+    returned, out_parts = lax.optimization_barrier((returned, out_parts))
+    mixed = call(part(mixed_kernel, peers), "mixed", shape(count, width), cost=LONG)(returned, frames, meta)
+    back, out_parts, mixed = lax.optimization_barrier((back, out_parts, mixed))
+    sums = call(
+        part(tally_kernel, peers), "tally", shape(groups, 8, width // 4, dtype=f32), in_blocks=(last,), mib=4
+    )(back)
+    sums = lax.all_to_all(sums, "dp", 0, 0, tiled=True)
     grad_frames = call(part(finish_kernel, peers), "finish", shape(count, width))(
-        back, frames, gain, out_grad, meta, base
+        back_left, back, frames, gain, out_grad, meta, grad_logits, router_rows
     )
     sums, in_parts, grad_frames = lax.optimization_barrier((sums, in_parts, grad_frames))
-    router_mine, gain_gradient = sums[0], sums[1]
-    grad_router = everyones(router_mine.reshape(8, width // 8), "expert", peers).reshape(peers, width).T
+    router_mine, gain_gradient = call(
+        sum_kernel, "sum", shape(peers, 8, width // 8, dtype=f32), shape(1, width, dtype=f32), mib=4
+    )(sums)
+    grad_router = lax.all_to_all(router_mine, "expert", 0, 0, tiled=True).reshape(peers, width).T
     grad_w_out, grad_w_in = total_sums((out_kept, in_kept), (out_parts, in_parts))
-    return (mixed, grad_frames, grad_w_in[None], grad_w_out[None], grad_router, gain_gradient)
+    return (mixed, grad_frames, grad_w_in[None], grad_w_out[None], grad_router, gain_gradient[0])
 
 
 def solution(mesh):

time: 212 us -> 208 us (0.981)
  waiting for transfers between devices: 61.2 us -> 43.2 us
  starting transfers between devices: 68.9 us -> 81.6 us
  Pallas kernels: 72.6 us -> 75.9 us
  local copies, waits for them, and re-layouts: 6.04 us -> 3.74 us
    all_to_all x4 -> x5, waiting for transfers between devices: 29.6 us -> 16.4 us  [exchange(): lax.all_to_all(packed.reshape(peers, MAIN, packed.shape[1]), 'expert', sp...]
    ppermute x22, starting transfers between devices: 17.9 us -> 24.7 us  [send(): lax.ppermute(array, self.name, [(i, self.step(i, k)) for i in range(self....]
    ppermute x22, waiting for transfers between devices: 25.7 us -> 20.9 us  [send(): lax.ppermute(array, self.name, [(i, self.step(i, k)) for i in range(self....]
    all_to_all x4 -> x5, starting transfers between devices: 37 us -> 40.7 us  [exchange(): lax.all_to_all(packed.reshape(peers, MAIN, packed.shape[1]), 'expert', sp...]
    pallas_call x12 -> x14, Pallas kernels: 72.6 us -> 75.9 us  [run(): pl.pallas_call(kernel, out_shape=outs if len(outs) > 1 else outs[0], grid...]
    all_to_all x2, starting transfers between devices: 14 us -> 16.3 us  [the longest x1 8.22 us: on_device(): lax.all_to_all(router_mine, 'expert', 0, 0, tiled=True)]
  transfers between devices with their start and end apart: 28 -> 29, of which waited for: 13 -> 13; matrix products, arithmetic and copies ran while one was open for 1% -> 1% of each run, Pallas kernels for 34% -> 36%
where the time goes in v3:
time: 208 us; the launch traced here: 207 us
  starting transfers between devices  81.6 us (39%)
  Pallas kernels  75.9 us (36%)
  waiting for transfers between devices  43.2 us (21%)
  local copies, waits for them, and re-layouts  3.74 us (2%)
    pallas_call x14, Pallas kernels, run(): pl.pallas_call(kernel, out_shape=outs if len(outs) > 1 else outs[0], grid...  75.9 us
    all_to_all x5, starting transfers between devices, exchange(): lax.all_to_all(packed.reshape(peers, MAIN, packed.shape[1]), 'expert', sp...  40.7 us
    ppermute x22, starting transfers between devices, send(): lax.ppermute(array, self.name, [(i, self.step(i, k)) for i in range(self....  24.7 us
    ppermute x22, waiting for transfers between devices, send(): lax.ppermute(array, self.name, [(i, self.step(i, k)) for i in range(self....  20.9 us
    all_to_all x5, waiting for transfers between devices, exchange(): lax.all_to_all(packed.reshape(peers, MAIN, packed.shape[1]), 'expert', sp...  16.4 us
    all_to_all x1, starting transfers between devices, on_device(): lax.all_to_all(router_mine, 'expert', 0, 0, tiled=True)  8.22 us
    all_to_all x1, starting transfers between devices, on_device(): sums = lax.all_to_all(sums, 'dp', 0, 0, tiled=True)  8.04 us
    all_to_all x1, waiting for transfers between devices, on_device(): lax.all_to_all(router_mine, 'expert', 0, 0, tiled=True)  4.99 us
  transfers between devices with their start and end apart: 29, of which 13 were waited for; matrix products, arithmetic and copies ran while one was open for 1% of the time, Pallas kernels for 36%

profile of v3, /device:TPU:1, one launch (start us, length us, event | category | flops | bytes accessed | tf_op | source)
XLA Modules:
  0.0 206.5 jit_solution(15966018958987768332)
XLA Ops:
  0.6 2.2 %collective-permute-start = (bf16[128,2048]{1,0:T(8,128)(2,1)}, bf16[128,2048]{1,0:T(8,128)(2,1)}, u32[]{:S(2)}, u32[]{:S(2)}) collective-permute-start(bf16[128,2048]{1,0:T(8,128)(2,1)} %bitcast.32), channel_id=1, source_target_pairs={{0,64},{32,96},{64,128},{96,160},{128,192},{160,224},{192,0},{224,... | collective-permute-start | bytes 1572872 | tf_op jit(solution)/shard_map/ppermute | solution.py:425
  2.8 2.6 %collective-permute-start.1 = (bf16[128,2048]{1,0:T(8,128)(2,1)}, bf16[128,2048]{1,0:T(8,128)(2,1)}, u32[]{:S(2)}, u32[]{:S(2)}) collective-permute-start(bf16[128,2048]{1,0:T(8,128)(2,1)} %bitcast.33), channel_id=1, source_target_pairs={{0,128},{32,160},{64,192},{96,224},{128,0},{160,32},{192,64},{224,... | collective-permute-start | bytes 1572872 | tf_op jit(solution)/shard_map/ppermute | solution.py:425
  5.5 1.1 collective-permute-start.2
  6.5 3.2 %dispatch.1 = (bf16[512,1152]{1,0:T(8,128)(2,1)}, bf16[192,1024]{1,0:T(8,128)(2,1)}, s32[2,192]{1,0:T(2,128)}) custom-call(bf16[192,1024]{1,0:T(8,128)(2,1)} %frames_ref.5, f32[1,1024]{1,0:T(1,128)} %bitcast.52, s32[2,192]{1,0:T(2,128)} %bitcast.59), custom_call_target="tpu_custom_call" | custom-call | flops 99999997952 | bytes 1 | tf_op jit(solution)/shard_map/dispatch/pallas_call | solution.py:379
  9.7 11.0 %all-to-all-start = ((bf16[32,16,1152]{2,1,0:T(8,128)(2,1)}), bf16[32,16,1152]{2,1,0:T(8,128)(2,1)S(1)}, u32[]{:S(2)}, u32[]{:S(2)}) async-start(bf16[32,16,1152]{2,1,0:T(8,128)(2,1)} %bitcast.39), calls=%async_computation | async-start | bytes 2359296 | tf_op jit(solution)/shard_map/all_to_all | solution.py:403
  20.8 3.4 %grads.1 = (bf16[512,1152]{1,0:T(8,128)(2,1)}, f32[192,16]{1,0:T(8,128)}) custom-call(bf16[192,1024]{1,0:T(8,128)(2,1)} %get-tuple-element.80.normed_ref, bf16[32,1024]{1,0:T(8,128)(2,1)} %bitcast.49, s32[2,192]{1,0:T(2,128)} %bitcast.60, s32[1,192]{1,0:T(1,128)} %bitcast.61, s32[2,192]{1,0:T(2,128)} %get-tuple-element.81.place_ref, bf16[192,1024]{1,0:T(8,128)(2,1)} %grad_ref.5), custom_call_target="tpu_custom_call" | custom-call | flops 99999997952 | bytes 1 | tf_op jit(solution)/shard_map/grads/pallas_call | solution.py:379
  24.2 4.1 %collective-permute-done.1.refs_2_ = bf16[128,2048]{1,0:T(8,128)(2,1)} collective-permute-done((bf16[128,2048]{1,0:T(8,128)(2,1)}, bf16[128,2048]{1,0:T(8,128)(2,1)}, u32[]{:S(2)}, u32[]{:S(2)}) %collective-permute-start.1) | collective-permute-done | bytes 524320 | tf_op jit(solution)/shard_map/ppermute | solution.py:425
  28.3 1.3 collective-permute-start.7
  29.6 1.7 collective-permute-start.8
  31.3 1.8 collective-permute-start.3
  33.6 8.3 %collective-permute-done.7.refs_1_ = bf16[256,1024]{1,0:T(8,128)(2,1)S(1)} collective-permute-done((bf16[256,1024]{1,0:T(8,128)(2,1)S(1)}, bf16[256,1024]{1,0:T(8,128)(2,1)S(1)}, u32[]{:S(2)}, u32[]{:S(2)}) %collective-permute-start.7) | collective-permute-done | bytes 524320 | tf_op jit(solution)/shard_map/ppermute | solution.py:425
  42.0 2.2 %collective-permute-start.6 = (bf16[128,2048]{1,0:T(8,128)(2,1)}, bf16[128,2048]{1,0:T(8,128)(2,1)S(1)}, u32[]{:S(2)}, u32[]{:S(2)}) collective-permute-start(bf16[128,2048]{1,0:T(8,128)(2,1)} %collective-permute-done.2.refs_3_), channel_id=1, source_target_pairs={{0,32},{32,0},{64,96},{96,64},{128,160},{160,128},{192,224},{224,1... | collective-permute-start | bytes 1572872 | tf_op jit(solution)/shard_map/ppermute | solution.py:425
  44.2 1.7 collective-permute-done.6.refs_7_
  45.9 0.8 copy-done.9
  46.7 2.1 %all-to-all-done = bf16[32,16,1152]{2,1,0:T(8,128)(2,1)S(1)} async-done(((bf16[32,16,1152]{2,1,0:T(8,128)(2,1)}), bf16[32,16,1152]{2,1,0:T(8,128)(2,1)S(1)}, u32[]{:S(2)}, u32[]{:S(2)}) %all-to-all-start) | async-done | bytes 1179680 | tf_op jit(solution)/shard_map/all_to_all | solution.py:403
  48.8 9.0 %all-to-all-start.1 = ((bf16[32,16,1152]{2,1,0:T(8,128)(2,1)}), bf16[32,16,1152]{2,1,0:T(8,128)(2,1)S(1)}, u32[]{:S(2)}, u32[]{:S(2)}) async-start(bf16[32,16,1152]{2,1,0:T(8,128)(2,1)} %bitcast.38), calls=%async_computation.1 | async-start | bytes 2359296 | tf_op jit(solution)/shard_map/all_to_all | solution.py:403
  59.0 2.1 %collective-permute-start.10 = (bf16[256,1024]{1,0:T(8,128)(2,1)}, bf16[256,1024]{1,0:T(8,128)(2,1)S(1)}, u32[]{:S(2)}, u32[]{:S(2)}) collective-permute-start(bf16[256,1024]{1,0:T(8,128)(2,1)} %bitcast.44), channel_id=1, source_target_pairs={{0,32},{32,0},{64,96},{96,64},{128,160},{160,128},{192,224},{224,1... | collective-permute-start | bytes 1572872 | tf_op jit(solution)/shard_map/ppermute | solution.py:425
  61.6 9.7 %first.1 = (bf16[576,1024]{1,0:T(8,128)(2,1)}, bf16[576,2048]{1,0:T(8,128)(2,1)}, f32[576,2048]{1,0:T(8,128)}, bf16[1024,576]{1,0:T(8,128)(2,1)}) custom-call(s32[8]{0:T(128)} %pad_add_fusion.order_ref.holders_ref, bf16[512,1152]{1,0:T(8,128)(2,1)} %bitcast.29, bf16[128,2048]{1,0:T(8,128)(2,1)} %bitcast.35, bf16[128,2048]{1,0:T(8,128)(2,1)} %collective-permute-done.refs_1_, ...), custom_call_target="tpu_custom_call" | custom-call | flops 1 | bytes 1 | tf_op jit(solution)/shard_map/first/pallas_call | solution.py:379
  71.4 1.1 collective-permute-done.9.refs_2_
  72.4 1.5 collective-permute-start.12
  74.0 1.5 collective-permute-done.12.refs_6_
  75.5 0.8 copy-done.20
  76.3 9.2 %second.1 = (bf16[512,1152]{1,0:T(8,128)(2,1)}, bf16[2048,1024]{1,0:T(8,128)(2,1)}) custom-call(s32[8]{0:T(128)} %pad_add_fusion.order_ref.holders_ref, bf16[576,2048]{1,0:T(8,128)(2,1)} %get-tuple-element.99.hidden_ref, bf16[256,1024]{1,0:T(8,128)(2,1)} %bitcast.45, bf16[256,1024]{1,0:T(8,128)(2,1)} %copy-done.14, bf16[256,1024]{1,0:T(8,128)(2,1)} %copy-done.16, ...), custom_call_target="tpu_custom_call" | custom-call | flops 1 | bytes 1 | tf_op jit(solution)/shard_map/second/pallas_call | solution.py:379
  85.6 1.7 all-to-all-done.1
  87.3 7.6 %all-to-all-start.2 = ((bf16[32,16,1152]{2,1,0:T(8,128)(2,1)}), bf16[32,16,1152]{2,1,0:T(8,128)(2,1)}, u32[]{:S(2)}, u32[]{:S(2)}) async-start(bf16[32,16,1152]{2,1,0:T(8,128)(2,1)} %bitcast.40), calls=%async_computation.2 | async-start | bytes 2359296 | tf_op jit(solution)/shard_map/all_to_all | solution.py:403
  95.5 8.9 %outer.1 = (bf16[576,1024]{1,0:T(8,128)(2,1)}, bf16[4,256,1024]{2,1,0:T(8,128)(2,1)}, bf16[4,256,1024]{2,1,0:T(8,128)(2,1)}) custom-call(s32[4]{0:T(128)} %and_select_fusion.order_ref, s32[1]{0:T(128)} %bitcast.12.core_ref, bf16[512,1152]{1,0:T(8,128)(2,1)} %bitcast.30, bf16[576,2048]{1,0:T(8,128)(2,1)} %get-tuple-element.99.hidden_ref), custom_call_target="tpu_custom_call" | custom-call | flops 1 | bytes 1 | tf_op jit(solution)/shard_map/outer/pallas_call | solution.py:379
  105.0 17.1 %backward.1 = (bf16[4,128,2048]{2,1,0:T(8,128)(2,1)}, bf16[4,128,2048]{2,1,0:T(8,128)(2,1)}, bf16[512,640]{1,0:T(8,128)(2,1)}, bf16[512,640]{1,0:T(8,128)(2,1)}, f32[1,1024]{1,0:T(1,128)}) custom-call(s32[4]{0:T(128)} %and_select_fusion.order_ref, s32[8]{0:T(128)} %pad_add_fusion.order_ref.holders_ref, bf16[576,1024]{1,0:T(8,128)(2,1)} %get-tuple-element.107.grads_ref, ...), custom_call_target="tpu_custom_call" | custom-call | flops 1 | bytes 1 | tf_op jit(solution)/shard_map/backward/pallas_call | solution.py:379
  122.3 2.1 %all-to-all-done.2 = bf16[32,16,1152]{2,1,0:T(8,128)(2,1)} async-done(((bf16[32,16,1152]{2,1,0:T(8,128)(2,1)}), bf16[32,16,1152]{2,1,0:T(8,128)(2,1)}, u32[]{:S(2)}, u32[]{:S(2)}) %all-to-all-start.2) | async-done | bytes 1179680 | tf_op jit(solution)/shard_map/all_to_all | solution.py:403
  124.4 7.3 %all-to-all-start.3 = ((bf16[32,16,640]{2,1,0:T(8,128)(2,1)}), bf16[32,16,640]{2,1,0:T(8,128)(2,1)S(1)}, u32[]{:S(2)}, u32[]{:S(2)}) async-start(bf16[32,16,640]{2,1,0:T(8,128)(2,1)} %bitcast.41), calls=%async_computation.3 | async-start | bytes 1310720 | tf_op jit(solution)/shard_map/all_to_all | solution.py:403
  131.7 3.5 %out_pair.1 = (f32[256,1024]{1,0:T(8,128)}, bf16[256,1024]{1,0:T(8,128)(2,1)}, bf16[256,1024]{1,0:T(8,128)(2,1)}, bf16[256,1024]{1,0:T(8,128)(2,1)}) custom-call(bf16[4,256,1024]{2,1,0:T(8,128)(2,1)} %get-tuple-element.118.mine_ref, bf16[4,256,1024]{2,1,0:T(8,128)(2,1)} %collective-permute-done.15.theirs_ref), custom_call_target="tpu_custom_call" | custom-call | flops 1 | bytes 1 | tf_op jit(solution)/shard_map/out_pair/pallas_call | solution.py:379
  135.2 1.5 collective-permute-start.16
  137.4 4.4 %route.1 = (bf16[512,640]{1,0:T(8,128)(2,1)}, f32[192,32]{1,0:T(8,128)}) custom-call(bf16[512,1152]{1,0:T(8,128)(2,1)} %bitcast.11.packed_ref, bf16[192,1024]{1,0:T(8,128)(2,1)} %get-tuple-element.80.normed_ref, bf16[192,1024]{1,0:T(8,128)(2,1)} %grad_ref.5, f32[192,16]{1,0:T(8,128)} %get-tuple-element.83.meta_ref, ...), custom_call_target="tpu_custom_call", output_to_operand_aliasing={{0}: (7, {})} | custom-call | flops 99999997952 | bytes 1 | tf_op jit(solution)/shard_map/route/pallas_call | solution.py:379
  141.8 1.3 copy-done.4
  143.1 3.4 %in_pair.1 = (f32[128,2048]{1,0:T(8,128)}, bf16[128,2048]{1,0:T(8,128)(2,1)}, bf16[128,2048]{1,0:T(8,128)(2,1)}, bf16[128,2048]{1,0:T(8,128)(2,1)}) custom-call(bf16[4,128,2048]{2,1,0:T(8,128)(2,1)} %get-tuple-element.116.mine_ref, bf16[4,128,2048]{2,1,0:T(8,128)(2,1)} %copy-done.4), custom_call_target="tpu_custom_call" | custom-call | flops 1 | bytes 1 | tf_op jit(solution)/shard_map/in_pair/pallas_call | solution.py:379
  146.5 3.8 %all-to-all-done.3 = bf16[32,16,640]{2,1,0:T(8,128)(2,1)S(1)} async-done(((bf16[32,16,640]{2,1,0:T(8,128)(2,1)}), bf16[32,16,640]{2,1,0:T(8,128)(2,1)S(1)}, u32[]{:S(2)}, u32[]{:S(2)}) %all-to-all-start.3) | async-done | bytes 655392 | tf_op jit(solution)/shard_map/all_to_all | solution.py:403
  150.4 5.7 %all-to-all-start.4 = ((bf16[32,16,640]{2,1,0:T(8,128)(2,1)}), bf16[32,16,640]{2,1,0:T(8,128)(2,1)S(1)}, u32[]{:S(2)}, u32[]{:S(2)}) async-start(bf16[32,16,640]{2,1,0:T(8,128)(2,1)} %bitcast.15), calls=%async_computation.4 | async-start | bytes 1310720 | tf_op jit(solution)/shard_map/all_to_all | solution.py:403
  156.1 1.9 collective-permute-start.19
  158.0 1.7 collective-permute-start.20
  159.7 4.1 %collective-permute-done.18.refs_2_ = bf16[256,1024]{1,0:T(8,128)(2,1)} collective-permute-done((bf16[256,1024]{1,0:T(8,128)(2,1)}, bf16[256,1024]{1,0:T(8,128)(2,1)}, u32[]{:S(2)}, u32[]{:S(2)}) %collective-permute-start.18) | collective-permute-done | bytes 524320 | tf_op jit(solution)/shard_map/ppermute | solution.py:425
  163.8 3.1 %mixed.1 = bf16[192,1024]{1,0:T(8,128)(2,1)} custom-call(bf16[512,1152]{1,0:T(8,128)(2,1)} %bitcast.11.packed_ref, bf16[192,1024]{1,0:T(8,128)(2,1)} %frames_ref.5, f32[192,16]{1,0:T(8,128)} %get-tuple-element.83.meta_ref), custom_call_target="tpu_custom_call" | custom-call | flops 99999997952 | bytes 1 | tf_op jit(solution)/shard_map/mixed/pallas_call | solution.py:379
  166.9 6.7 %all-to-all-done.4 = bf16[32,16,640]{2,1,0:T(8,128)(2,1)S(1)} async-done(((bf16[32,16,640]{2,1,0:T(8,128)(2,1)}), bf16[32,16,640]{2,1,0:T(8,128)(2,1)S(1)}, u32[]{:S(2)}, u32[]{:S(2)}) %all-to-all-start.4) | async-done | bytes 655392 | tf_op jit(solution)/shard_map/all_to_all | solution.py:403
  173.6 1.0 tally.1
  174.6 8.0 %all-to-all-start.5 = ((f32[8,8,256]{2,1,0:T(8,128)}), f32[8,8,256]{2,1,0:T(8,128)S(1)}, u32[]{:S(2)}, u32[]{:S(2)}) async-start(f32[8,8,256]{2,1,0:T(8,128)} %tally.1), calls=%async_computation.5 | async-start | bytes 131072 | tf_op jit(solution)/shard_map/all_to_all | solution.py:593
  182.6 3.9 %finish.1 = bf16[192,1024]{1,0:T(8,128)(2,1)} custom-call(bf16[512,640]{1,0:T(8,128)(2,1)} %bitcast.31, bf16[512,640]{1,0:T(8,128)(2,1)} %bitcast.28, bf16[192,1024]{1,0:T(8,128)(2,1)} %frames_ref.5, f32[1,1024]{1,0:T(1,128)} %bitcast.55, bf16[192,1024]{1,0:T(8,128)(2,1)} %grad_ref.5, f32[192,16]{1,0:T(8,128)} %get-tuple-element.83.meta_ref, ...), custom_call_target="tpu_custom_call" | custom-call | flops 1 | bytes 1 | tf_op jit(solution)/shard_map/finish/pallas_call | solution.py:379
  186.6 0.9 all-to-all-done.5.sums_ref
  188.2 8.2 %all-to-all-start.6 = ((f32[32,8,128]{2,1,0:T(8,128)}), f32[32,8,128]{2,1,0:T(8,128)S(1)}, u32[]{:S(2)}, u32[]{:S(2)}) async-start(f32[32,8,128]{2,1,0:T(8,128)} %get-tuple-element.150), calls=%async_computation.6 | async-start | bytes 262144 | tf_op jit(solution)/shard_map/all_to_all | solution.py:601
  196.5 4.4 %total.1 = (f32[256,1024]{1,0:T(8,128)}, f32[128,2048]{1,0:T(8,128)}) custom-call(f32[256,1024]{1,0:T(8,128)} %get-tuple-element.121.first_ref, f32[128,2048]{1,0:T(8,128)} %get-tuple-element.140.second_ref, bf16[256,1024]{1,0:T(8,128)(2,1)} %copy-done.10, bf16[256,1024]{1,0:T(8,128)(2,1)} %collective-permute-done.17.refs_1_, ...), custom_call_target="tpu_custom_call" | custom-call | flops 1 | bytes 1 | tf_op jit(solution)/shard_map/total/pallas_call | solution.py:379
  200.8 5.0 %all-to-all-done.6 = f32[32,8,128]{2,1,0:T(8,128)S(1)} async-done(((f32[32,8,128]{2,1,0:T(8,128)}), f32[32,8,128]{2,1,0:T(8,128)S(1)}, u32[]{:S(2)}, u32[]{:S(2)}) %all-to-all-start.6) | async-done | bytes 131104 | tf_op jit(solution)/shard_map/all_to_all | solution.py:601
  (70 shorter events, 5.8 us)
Async XLA Ops:
  0.6 23.6 %collective-permute-start = (bf16[128,2048]{1,0:T(8,128)(2,1)}, bf16[128,2048]{1,0:T(8,128)(2,1)}, u32[]{:S(2)}, u32[]{:S(2)}) collective-permute-start(bf16[128,2048]{1,0:T(8,128)(2,1)} %bitcast.32), channel_id=1, source_target_pairs={{0,64},{32,96},{64,128},{96,160},{128,192},{160,224},{192,0},{224,... | collective-permute-start | bytes 1572872 | tf_op jit(solution)/shard_map/ppermute | solution.py:425
  2.8 25.5 %collective-permute-start.1 = (bf16[128,2048]{1,0:T(8,128)(2,1)}, bf16[128,2048]{1,0:T(8,128)(2,1)}, u32[]{:S(2)}, u32[]{:S(2)}) collective-permute-start(bf16[128,2048]{1,0:T(8,128)(2,1)} %bitcast.33), channel_id=1, source_target_pairs={{0,128},{32,160},{64,192},{96,224},{128,0},{160,32},{192,64},{224,... | collective-permute-start | bytes 1572872 | tf_op jit(solution)/shard_map/ppermute | solution.py:425
  5.5 22.9 %collective-permute-start.2 = (bf16[128,2048]{1,0:T(8,128)(2,1)}, bf16[128,2048]{1,0:T(8,128)(2,1)}, u32[]{:S(2)}, u32[]{:S(2)}) collective-permute-start(bf16[128,2048]{1,0:T(8,128)(2,1)} %bitcast.34), channel_id=1, source_target_pairs={{0,192},{32,224},{64,0},{96,32},{128,64},{160,96},{192,128},{224,1... | collective-permute-start | bytes 1572872 | tf_op jit(solution)/shard_map/ppermute | solution.py:425
  9.7 39.1 %all-to-all-start = ((bf16[32,16,1152]{2,1,0:T(8,128)(2,1)}), bf16[32,16,1152]{2,1,0:T(8,128)(2,1)S(1)}, u32[]{:S(2)}, u32[]{:S(2)}) async-start(bf16[32,16,1152]{2,1,0:T(8,128)(2,1)} %bitcast.39), calls=%async_computation | async-start | bytes 2359296 | tf_op jit(solution)/shard_map/all_to_all | solution.py:403
  20.8 7.5 %copy-start.13 = (bf16[1,256,1024]{2,1,0:T(8,128)(2,1)S(1)}, bf16[1,256,1024]{2,1,0:T(8,128)(2,1)}, u32[]{:S(2)}) copy-start(bf16[1,256,1024]{2,1,0:T(8,128)(2,1)} %param.12) | copy-start | bytes 1572868
  20.8 10.5 %copy-start.5 = (bf16[1,128,2048]{2,1,0:T(8,128)(2,1)S(1)}, bf16[1,128,2048]{2,1,0:T(8,128)(2,1)}, u32[]{:S(2)}) copy-start(bf16[1,128,2048]{2,1,0:T(8,128)(2,1)} %param.11) | copy-start | bytes 1572868
  28.3 13.6 %collective-permute-start.7 = (bf16[256,1024]{1,0:T(8,128)(2,1)S(1)}, bf16[256,1024]{1,0:T(8,128)(2,1)S(1)}, u32[]{:S(2)}, u32[]{:S(2)}) collective-permute-start(bf16[256,1024]{1,0:T(8,128)(2,1)S(1)} %bitcast.46), channel_id=1, source_target_pairs={{0,64},{32,96},{64,128},{96,160},{128,192},{160,224},{192,0},{224,... | collective-permute-start | bytes 1572872 | tf_op jit(solution)/shard_map/ppermute | solution.py:425
  29.6 14.6 %collective-permute-start.8 = (bf16[256,1024]{1,0:T(8,128)(2,1)S(1)}, bf16[256,1024]{1,0:T(8,128)(2,1)S(1)}, u32[]{:S(2)}, u32[]{:S(2)}) collective-permute-start(bf16[256,1024]{1,0:T(8,128)(2,1)S(1)} %bitcast.47), channel_id=1, source_target_pairs={{0,192},{32,224},{64,0},{96,32},{128,64},{160,96},{192,128},{224,1... | collective-permute-start | bytes 1572872 | tf_op jit(solution)/shard_map/ppermute | solution.py:425
  31.3 12.9 %collective-permute-start.3 = (bf16[128,2048]{1,0:T(8,128)(2,1)S(1)}, bf16[128,2048]{1,0:T(8,128)(2,1)S(1)}, u32[]{:S(2)}, u32[]{:S(2)}) collective-permute-start(bf16[128,2048]{1,0:T(8,128)(2,1)S(1)} %bitcast.37), channel_id=1, source_target_pairs={{0,32},{32,0},{64,96},{96,64},{128,160},{160,128},{192,224},{224,1... | collective-permute-start | bytes 1572872 | tf_op jit(solution)/shard_map/ppermute | solution.py:425
  33.1 11.1 %collective-permute-start.4 = (bf16[128,2048]{1,0:T(8,128)(2,1)}, bf16[128,2048]{1,0:T(8,128)(2,1)S(1)}, u32[]{:S(2)}, u32[]{:S(2)}) collective-permute-start(bf16[128,2048]{1,0:T(8,128)(2,1)} %collective-permute-done.refs_1_), channel_id=1, source_target_pairs={{0,32},{32,0},{64,96},{96,64},{128,160},{160,128},{192,224},{224,1... | collective-permute-start | bytes 1572872 | tf_op jit(solution)/shard_map/ppermute | solution.py:425
  33.1 11.1 %collective-permute-start.5 = (bf16[128,2048]{1,0:T(8,128)(2,1)}, bf16[128,2048]{1,0:T(8,128)(2,1)S(1)}, u32[]{:S(2)}, u32[]{:S(2)}) collective-permute-start(bf16[128,2048]{1,0:T(8,128)(2,1)} %collective-permute-done.1.refs_2_), channel_id=1, source_target_pairs={{0,32},{32,0},{64,96},{96,64},{128,160},{160,128},{192,224},{224,1... | collective-permute-start | bytes 1572872 | tf_op jit(solution)/shard_map/ppermute | solution.py:425
  42.0 4.0 %copy-start.14 = (bf16[256,1024]{1,0:T(8,128)(2,1)}, bf16[256,1024]{1,0:T(8,128)(2,1)S(1)}, u32[]{:S(2)}) copy-start(bf16[256,1024]{1,0:T(8,128)(2,1)S(1)} %collective-permute-done.7.refs_1_) | copy-start | bytes 1572868
  42.0 4.0 %collective-permute-start.6 = (bf16[128,2048]{1,0:T(8,128)(2,1)}, bf16[128,2048]{1,0:T(8,128)(2,1)S(1)}, u32[]{:S(2)}, u32[]{:S(2)}) collective-permute-start(bf16[128,2048]{1,0:T(8,128)(2,1)} %collective-permute-done.2.refs_3_), channel_id=1, source_target_pairs={{0,32},{32,0},{64,96},{96,64},{128,160},{160,128},{192,224},{224,1... | collective-permute-start | bytes 1572872 | tf_op jit(solution)/shard_map/ppermute | solution.py:425
  44.2 1.7 copy-start.15
  44.2 17.5 %copy-start.6 = (bf16[128,2048]{1,0:T(8,128)(2,1)}, bf16[128,2048]{1,0:T(8,128)(2,1)S(1)}, u32[]{:S(2)}) copy-start(bf16[128,2048]{1,0:T(8,128)(2,1)S(1)} %collective-permute-done.3.refs_4_) | copy-start | bytes 1572868
  44.2 4.6 %copy-start.7 = (bf16[128,2048]{1,0:T(8,128)(2,1)}, bf16[128,2048]{1,0:T(8,128)(2,1)S(1)}, u32[]{:S(2)}) copy-start(bf16[128,2048]{1,0:T(8,128)(2,1)S(1)} %collective-permute-done.4.refs_5_) | copy-start | bytes 1572868
  44.2 4.6 %copy-start.8 = (bf16[128,2048]{1,0:T(8,128)(2,1)}, bf16[128,2048]{1,0:T(8,128)(2,1)S(1)}, u32[]{:S(2)}) copy-start(bf16[128,2048]{1,0:T(8,128)(2,1)S(1)} %collective-permute-done.5.refs_6_) | copy-start | bytes 1572868
  48.8 12.8 %copy-start.1 = (bf16[32,16,1152]{2,1,0:T(8,128)(2,1)}, bf16[32,16,1152]{2,1,0:T(8,128)(2,1)S(1)}, u32[]{:S(2)}) copy-start(bf16[32,16,1152]{2,1,0:T(8,128)(2,1)S(1)} %all-to-all-done) | copy-start | bytes 3538948
  48.8 38.4 %all-to-all-start.1 = ((bf16[32,16,1152]{2,1,0:T(8,128)(2,1)}), bf16[32,16,1152]{2,1,0:T(8,128)(2,1)S(1)}, u32[]{:S(2)}, u32[]{:S(2)}) async-start(bf16[32,16,1152]{2,1,0:T(8,128)(2,1)} %bitcast.38), calls=%async_computation.1 | async-start | bytes 2359296 | tf_op jit(solution)/shard_map/all_to_all | solution.py:403
  57.8 14.6 %collective-permute-start.9 = (bf16[256,1024]{1,0:T(8,128)(2,1)}, bf16[256,1024]{1,0:T(8,128)(2,1)S(1)}, u32[]{:S(2)}, u32[]{:S(2)}) collective-permute-start(bf16[256,1024]{1,0:T(8,128)(2,1)} %bitcast.43), channel_id=1, source_target_pairs={{0,128},{32,160},{64,192},{96,224},{128,0},{160,32},{192,64},{224,... | collective-permute-start | bytes 1572872 | tf_op jit(solution)/shard_map/ppermute | solution.py:425
  59.0 14.9 %collective-permute-start.10 = (bf16[256,1024]{1,0:T(8,128)(2,1)}, bf16[256,1024]{1,0:T(8,128)(2,1)S(1)}, u32[]{:S(2)}, u32[]{:S(2)}) collective-permute-start(bf16[256,1024]{1,0:T(8,128)(2,1)} %bitcast.44), channel_id=1, source_target_pairs={{0,32},{32,0},{64,96},{96,64},{128,160},{160,128},{192,224},{224,1... | collective-permute-start | bytes 1572872 | tf_op jit(solution)/shard_map/ppermute | solution.py:425
  61.1 12.8 %collective-permute-start.11 = (bf16[256,1024]{1,0:T(8,128)(2,1)}, bf16[256,1024]{1,0:T(8,128)(2,1)S(1)}, u32[]{:S(2)}, u32[]{:S(2)}) collective-permute-start(bf16[256,1024]{1,0:T(8,128)(2,1)} %copy-done.14), channel_id=1, source_target_pairs={{0,32},{32,0},{64,96},{96,64},{128,160},{160,128},{192,224},{224,1... | collective-permute-start | bytes 1572872 | tf_op jit(solution)/shard_map/ppermute | solution.py:425
  61.1 12.9 %collective-permute-start.13 = (bf16[256,1024]{1,0:T(8,128)(2,1)}, bf16[256,1024]{1,0:T(8,128)(2,1)S(1)}, u32[]{:S(2)}, u32[]{:S(2)}) collective-permute-start(bf16[256,1024]{1,0:T(8,128)(2,1)} %copy-done.15), channel_id=1, source_target_pairs={{0,32},{32,0},{64,96},{96,64},{128,160},{160,128},{192,224},{224,1... | collective-permute-start | bytes 1572872 | tf_op jit(solution)/shard_map/ppermute | solution.py:425
  72.4 3.1 %copy-start.16 = (bf16[256,1024]{1,0:T(8,128)(2,1)}, bf16[256,1024]{1,0:T(8,128)(2,1)S(1)}, u32[]{:S(2)}) copy-start(bf16[256,1024]{1,0:T(8,128)(2,1)S(1)} %collective-permute-done.9.refs_2_) | copy-start | bytes 1572868
  72.4 3.1 %collective-permute-start.12 = (bf16[256,1024]{1,0:T(8,128)(2,1)S(1)}, bf16[256,1024]{1,0:T(8,128)(2,1)S(1)}, u32[]{:S(2)}, u32[]{:S(2)}) collective-permute-start(bf16[256,1024]{1,0:T(8,128)(2,1)S(1)} %collective-permute-done.9.refs_2_), channel_id=1, source_target_pairs={{0,32},{32,0},{64,96},{96,64},{128,160},{160,128},{192,224},{224,1... | collective-permute-start | bytes 1572872 | tf_op jit(solution)/shard_map/ppermute | solution.py:425
  74.0 1.5 copy-start.17
  74.0 1.5 copy-start.18
  74.0 1.5 copy-start.19
  87.3 8.2 %copy-start.2 = (bf16[32,16,1152]{2,1,0:T(8,128)(2,1)}, bf16[32,16,1152]{2,1,0:T(8,128)(2,1)S(1)}, u32[]{:S(2)}) copy-start(bf16[32,16,1152]{2,1,0:T(8,128)(2,1)S(1)} %all-to-all-done.1) | copy-start | bytes 3538948
  87.3 37.1 %all-to-all-start.2 = ((bf16[32,16,1152]{2,1,0:T(8,128)(2,1)}), bf16[32,16,1152]{2,1,0:T(8,128)(2,1)}, u32[]{:S(2)}, u32[]{:S(2)}) async-start(bf16[32,16,1152]{2,1,0:T(8,128)(2,1)} %bitcast.40), calls=%async_computation.2 | async-start | bytes 2359296 | tf_op jit(solution)/shard_map/all_to_all | solution.py:403
  104.4 27.4 %collective-permute-start.15 = (bf16[4,256,1024]{2,1,0:T(8,128)(2,1)}, bf16[4,256,1024]{2,1,0:T(8,128)(2,1)}, u32[]{:S(2)}, u32[]{:S(2)}) collective-permute-start(bf16[4,256,1024]{2,1,0:T(8,128)(2,1)} %get-tuple-element.119), channel_id=1, source_target_pairs={{0,32},{32,0},{64,96},{96,64},{128,160},{160,128},{192,224},{224,1... | collective-permute-start | bytes 6291464 | tf_op jit(solution)/shard_map/ppermute | solution.py:425
  122.2 19.6 %collective-permute-start.14 = (bf16[4,128,2048]{2,1,0:T(8,128)(2,1)}, bf16[4,128,2048]{2,1,0:T(8,128)(2,1)S(1)}, u32[]{:S(2)}, u32[]{:S(2)}) collective-permute-start(bf16[4,128,2048]{2,1,0:T(8,128)(2,1)} %get-tuple-element.117), channel_id=1, source_target_pairs={{0,32},{32,0},{64,96},{96,64},{128,160},{160,128},{192,224},{224,1... | collective-permute-start | bytes 6291464 | tf_op jit(solution)/shard_map/ppermute | solution.py:425
  124.4 26.0 %all-to-all-start.3 = ((bf16[32,16,640]{2,1,0:T(8,128)(2,1)}), bf16[32,16,640]{2,1,0:T(8,128)(2,1)S(1)}, u32[]{:S(2)}, u32[]{:S(2)}) async-start(bf16[32,16,640]{2,1,0:T(8,128)(2,1)} %bitcast.41), calls=%async_computation.3 | async-start | bytes 1310720 | tf_op jit(solution)/shard_map/all_to_all | solution.py:403
  135.2 24.4 %collective-permute-start.16 = (bf16[256,1024]{1,0:T(8,128)(2,1)}, bf16[256,1024]{1,0:T(8,128)(2,1)S(1)}, u32[]{:S(2)}, u32[]{:S(2)}) collective-permute-start(bf16[256,1024]{1,0:T(8,128)(2,1)} %get-tuple-element.125), channel_id=1, source_target_pairs={{0,192},{32,224},{64,0},{96,32},{128,64},{160,96},{192,128},{224,1... | collective-permute-start | bytes 1572872 | tf_op jit(solution)/shard_map/ppermute | solution.py:425
  136.7 22.9 %collective-permute-start.17 = (bf16[256,1024]{1,0:T(8,128)(2,1)}, bf16[256,1024]{1,0:T(8,128)(2,1)}, u32[]{:S(2)}, u32[]{:S(2)}) collective-permute-start(bf16[256,1024]{1,0:T(8,128)(2,1)} %get-tuple-element.126), channel_id=1, source_target_pairs={{0,128},{32,160},{64,192},{96,224},{128,0},{160,32},{192,64},{224,... | collective-permute-start | bytes 1572872 | tf_op jit(solution)/shard_map/ppermute | solution.py:425
  136.8 27.0 %collective-permute-start.18 = (bf16[256,1024]{1,0:T(8,128)(2,1)}, bf16[256,1024]{1,0:T(8,128)(2,1)}, u32[]{:S(2)}, u32[]{:S(2)}) collective-permute-start(bf16[256,1024]{1,0:T(8,128)(2,1)} %get-tuple-element.127), channel_id=1, source_target_pairs={{0,64},{32,96},{64,128},{96,160},{128,192},{160,224},{192,0},{224,... | collective-permute-start | bytes 1572872 | tf_op jit(solution)/shard_map/ppermute | solution.py:425
  141.8 1.3 copy-start.4
  150.4 16.6 %copy-start.3 = (bf16[32,16,640]{2,1,0:T(8,128)(2,1)}, bf16[32,16,640]{2,1,0:T(8,128)(2,1)S(1)}, u32[]{:S(2)}) copy-start(bf16[32,16,640]{2,1,0:T(8,128)(2,1)S(1)} %all-to-all-done.3) | copy-start | bytes 1966084
  150.4 23.3 %all-to-all-start.4 = ((bf16[32,16,640]{2,1,0:T(8,128)(2,1)}), bf16[32,16,640]{2,1,0:T(8,128)(2,1)S(1)}, u32[]{:S(2)}, u32[]{:S(2)}) async-start(bf16[32,16,640]{2,1,0:T(8,128)(2,1)} %bitcast.15), calls=%async_computation.4 | async-start | bytes 1310720 | tf_op jit(solution)/shard_map/all_to_all | solution.py:403
  156.1 30.5 %collective-permute-start.19 = (bf16[128,2048]{1,0:T(8,128)(2,1)}, bf16[128,2048]{1,0:T(8,128)(2,1)S(1)}, u32[]{:S(2)}, u32[]{:S(2)}) collective-permute-start(bf16[128,2048]{1,0:T(8,128)(2,1)} %get-tuple-element.134), channel_id=1, source_target_pairs={{0,192},{32,224},{64,0},{96,32},{128,64},{160,96},{192,128},{224,1... | collective-permute-start | bytes 1572872 | tf_op jit(solution)/shard_map/ppermute | solution.py:425
  158.0 28.6 %collective-permute-start.20 = (bf16[128,2048]{1,0:T(8,128)(2,1)}, bf16[128,2048]{1,0:T(8,128)(2,1)S(1)}, u32[]{:S(2)}, u32[]{:S(2)}) collective-permute-start(bf16[128,2048]{1,0:T(8,128)(2,1)} %get-tuple-element.135), channel_id=1, source_target_pairs={{0,128},{32,160},{64,192},{96,224},{128,0},{160,32},{192,64},{224,... | collective-permute-start | bytes 1572872 | tf_op jit(solution)/shard_map/ppermute | solution.py:425
  159.6 7.3 %copy-start.10 = (bf16[256,1024]{1,0:T(8,128)(2,1)}, bf16[256,1024]{1,0:T(8,128)(2,1)S(1)}, u32[]{:S(2)}) copy-start(bf16[256,1024]{1,0:T(8,128)(2,1)S(1)} %collective-permute-done.16.refs_0_) | copy-start | bytes 1572868
  159.6 26.9 %collective-permute-start.21 = (bf16[128,2048]{1,0:T(8,128)(2,1)}, bf16[128,2048]{1,0:T(8,128)(2,1)}, u32[]{:S(2)}, u32[]{:S(2)}) collective-permute-start(bf16[128,2048]{1,0:T(8,128)(2,1)} %get-tuple-element.136), channel_id=1, source_target_pairs={{0,64},{32,96},{64,128},{96,160},{128,192},{160,224},{192,0},{224,... | collective-permute-start | bytes 1572872 | tf_op jit(solution)/shard_map/ppermute | solution.py:425
  173.6 9.0 %copy-start = (bf16[32,16,640]{2,1,0:T(8,128)(2,1)}, bf16[32,16,640]{2,1,0:T(8,128)(2,1)S(1)}, u32[]{:S(2)}) copy-start(bf16[32,16,640]{2,1,0:T(8,128)(2,1)S(1)} %all-to-all-done.4) | copy-start | bytes 1966084
  174.6 12.9 %all-to-all-start.5 = ((f32[8,8,256]{2,1,0:T(8,128)}), f32[8,8,256]{2,1,0:T(8,128)S(1)}, u32[]{:S(2)}, u32[]{:S(2)}) async-start(f32[8,8,256]{2,1,0:T(8,128)} %tally.1), calls=%async_computation.5 | async-start | bytes 131072 | tf_op jit(solution)/shard_map/all_to_all | solution.py:593
  186.5 9.9 %copy-start.11 = (bf16[128,2048]{1,0:T(8,128)(2,1)}, bf16[128,2048]{1,0:T(8,128)(2,1)S(1)}, u32[]{:S(2)}) copy-start(bf16[128,2048]{1,0:T(8,128)(2,1)S(1)} %collective-permute-done.19.refs_3_) | copy-start | bytes 1572868
  186.5 9.9 %copy-start.12 = (bf16[128,2048]{1,0:T(8,128)(2,1)}, bf16[128,2048]{1,0:T(8,128)(2,1)S(1)}, u32[]{:S(2)}) copy-start(bf16[128,2048]{1,0:T(8,128)(2,1)S(1)} %collective-permute-done.20.refs_4_) | copy-start | bytes 1572868
  188.2 17.6 %all-to-all-start.6 = ((f32[32,8,128]{2,1,0:T(8,128)}), f32[32,8,128]{2,1,0:T(8,128)S(1)}, u32[]{:S(2)}, u32[]{:S(2)}) async-start(f32[32,8,128]{2,1,0:T(8,128)} %get-tuple-element.150), calls=%async_computation.6 | async-start | bytes 262144 | tf_op jit(solution)/shard_map/all_to_all | solution.py:601
  (2 other events, 1.7 us)

commit v4 on v3

--- a/solution.py
+++ b/solution.py
@@ -46,14 +46,6 @@
     main = peers * MAIN
     out_ref[:, :width] = rows[:main]
     out_ref[:, width : width + LANES] = spread_pieces(rows[main:], peers)
-
-
-def pack_halves(rows, left_ref, right_ref, peers):
-    main, cut = peers * MAIN, left_ref.shape[1]
-    rest = rows.shape[1] - cut
-    left_ref[...] = rows[:main, :cut]
-    right_ref[:, :rest] = rows[:main, cut:]
-    right_ref[:, rest : rest + LANES] = spread_pieces(rows[main:], peers)
 
 
 def spread_pieces(extra, peers):
@@ -198,39 +190,39 @@
         pack(rows_ref[...], out_ref, peers)
 
 
-def outer_kernel(peers, order_ref, core_ref, packed_ref, hidden_ref, grads_ref, out_theirs_ref, out_mine_ref):
-    block = out_mine_ref.shape[1]
-
-    @pl.when(pl.program_id(0) == 0)
+def outer_kernel(order_ref, core_ref, grads_ref, hidden_ref, *refs):
+    theirs, mine_ref = refs[:-1], refs[-1]
+    block = mine_ref.shape[1]
+    step = pl.program_id(0)
+    product = matmul(hidden_ref[...].T, grads_ref[...]).astype(bf16)
+    first, second = product[:block], product[block:]
+    mine_ref[0] = jnp.where(core_ref[0] == 0, first, second)
+    other = jnp.where(core_ref[0] == 0, second, first)
+    for k, ref in enumerate(theirs):
+
+        @pl.when(step == k)
+        def _(ref=ref):
+            ref[...] = other
+
+
+def backward_kernel(
+    peers, order_ref, holders_ref, packed_ref, derivative_ref, out_weights_ref, turned_ref, incoming_ref, gain_ref, *refs
+):
+    pieces, (grads_ref, *in_theirs, in_mine_ref, back_ref, gain_part_ref, rows_ref, in_ref) = refs[:-10], refs[-10:]
+    step = pl.program_id(0)
+    half, depth = in_mine_ref.shape[0], in_mine_ref.shape[1]
+
+    @pl.when(step == 0)
     def _():
         unpack_into(packed_ref, grads_ref, peers)
 
-    product = matmul(hidden_ref[...].T, grads_ref[...]).astype(bf16)
-
-    @pl.when(core_ref[0] == 0)
-    def _():
-        out_mine_ref[0] = product[:block]
-        out_theirs_ref[0] = product[block:]
-
-    @pl.when(core_ref[0] == 1)
-    def _():
-        out_theirs_ref[0] = product[:block]
-        out_mine_ref[0] = product[block:]
-
-
-def backward_kernel(
-    peers, order_ref, holders_ref, grads_ref, derivative_ref, out_weights_ref, turned_ref, incoming_ref, gain_ref, *refs
-):
-    pieces, (in_theirs_ref, in_mine_ref, left_ref, right_ref, gain_part_ref, rows_ref, in_ref) = refs[:-7], refs[-7:]
-    step = pl.program_id(0)
-    half, depth = in_mine_ref.shape[0], in_mine_ref.shape[1]
     assemble(holders_ref, pieces, in_ref)
     grads = grads_ref[...]
     grad_pre = (matmul_nt(grads, out_weights_ref[...]) * derivative_ref[...]).astype(bf16)
     product = matmul(turned_ref[...], grad_pre).astype(bf16)
     for j in range(half):
         in_mine_ref[j] = product[j * depth : (j + 1) * depth]
-        in_theirs_ref[j] = product[(half + j) * depth : (half + j + 1) * depth]
+        in_theirs[j][...] = product[(half + j) * depth : (half + j + 1) * depth]
     rows = matmul_nt(grad_pre, in_ref[...])
 
     @pl.when(step == 0)
@@ -244,7 +236,7 @@
     @pl.when(step == pl.num_programs(0) - 1)
     def _():
         done = rows_ref[...].astype(bf16)
-        pack_halves(done, left_ref, right_ref, peers)
+        pack(done, back_ref, peers)
         total = jnp.sum(done.astype(f32) * incoming_ref[...].astype(f32), axis=0, keepdims=True)
         gain_part_ref[...] = total / gain_ref[...]
 
@@ -270,10 +262,11 @@
         router_ref[:, j] = jnp.broadcast_to(row, (router_ref.shape[0], LANES))
 
 
-def pair_kernel(mine_ref, theirs_ref, kept_ref, *out_refs):
-    kept_ref[...] = mine_ref[0].astype(f32) + theirs_ref[0].astype(f32)
-    for k, out_ref in enumerate(out_refs):
-        out_ref[...] = (mine_ref[k + 1].astype(f32) + theirs_ref[k + 1].astype(f32)).astype(bf16)
+def pair_kernel(count, mine_ref, *refs):
+    theirs, kept_ref, outs = refs[:count], refs[count], refs[count + 1 :]
+    kept_ref[...] = mine_ref[0].astype(f32) + theirs[0][...].astype(f32)
+    for k, out_ref in enumerate(outs):
+        out_ref[...] = (mine_ref[k + 1].astype(f32) + theirs[k + 1][...].astype(f32)).astype(bf16)
 
 
 def total_kernel(first_ref, second_ref, *refs):
@@ -336,11 +329,9 @@
 
 
 def finish_kernel(
-    peers, left_ref, right_ref, frames_ref, gain_ref, grad_ref, meta_ref, logits_ref, router_ref, out_ref
+    peers, packed_ref, frames_ref, gain_ref, grad_ref, meta_ref, logits_ref, router_ref, out_ref
 ):
-    rest = frames_ref.shape[1] - left_ref.shape[1]
-    main = jnp.concatenate([left_ref[...], right_ref[:, :rest]], axis=1)
-    extra = join_pieces(right_ref[:, rest : rest + LANES], peers)
+    main, extra = unpack(packed_ref, peers)
     meta = meta_ref[...]
     count = meta.shape[0]
     places = [meta[:, k : k + 1].astype(jnp.int32) for k in range(2)]
@@ -439,15 +430,15 @@
     block = ((count, depth // steps, width), lambda i: (0, i, 0))
     flat = ((depth // steps, width), lambda i: (i, 0))
     kept, *sums = call(
-        pair_kernel,
+        functools.partial(pair_kernel, count),
         name,
         shape(depth, width, dtype=f32),
         *[shape(depth, width)] * (count - 1),
         grid=steps,
-        in_blocks=(block, block),
+        in_blocks=(block,) + (flat,) * count,
         out_blocks=(flat,) * count,
         cost=cost,
-    )(mine, theirs)
+    )(mine, *theirs)
     return kept, [y.send(part, -k - 1) for k, part in enumerate(sums)]
 
 
@@ -534,22 +525,13 @@
     column = ((rows, block), lambda i, order, *_: (0, order[i]))
     split = ((half, width // groups, block), lambda i, order, *_: (0, 0, order[i]))
     whole = ((1, inner // groups, width), lambda i, *_: (i, 0, 0))
-    grad_incoming, out_theirs, out_mine = call(
-        part(outer_kernel, peers),
-        "outer",
-        shape(rows, width),
-        *[shape(half, inner // groups, width)] * 2,
-        grid=half,
-        in_blocks=(None, column),
-        out_blocks=(None, whole, whole),
-        order=(y.behind(), core.place[None].astype(jnp.int32)),
-    )(arrived_grads, hidden)
-    cut = width // 2 + LANES
-    in_theirs, in_mine, left, right, gain_expert = call(
+    grad_incoming, *in_theirs, in_mine, packed_grads, gain_expert = call(
         part(backward_kernel, peers),
         "backward",
-        *[shape(half, width // groups, inner)] * 2,
-        *[shape(peers * MAIN, cut)] * 2,
+        shape(rows, width),
+        *[shape(width // groups, inner)] * half,
+        shape(half, width // groups, inner),
+        shape(peers * MAIN, width + 2 * LANES),
         shape(1, width, dtype=f32),
         grid=half,
         in_blocks=(
@@ -561,40 +543,49 @@
             None,
         )
         + (((width // groups, block), lambda i, order, *_: (0, order[i])),) * groups,
-        out_blocks=(split, split, None, None, None),
+        out_blocks=(None,) + (((width // groups, block), lambda i, order, *_: (0, order[i])),) * half + (split, (packed.shape, lambda i, *_: (0, 0)), None),
         scratch=[pltpu.VMEM((rows, width), f32), pltpu.VMEM((width, block), bf16)],
         order=(y.behind(), holders),
-    )(grad_incoming, derivative, weights_out, turned, incoming, gain, *pieces_in)
-    arrived_out, _ = lax.optimization_barrier((core.send(out_theirs, 1), returned))
-    out_kept, out_parts = pair_sums(out_mine, arrived_out, y, "out_pair")
-    arrived_in, _ = lax.optimization_barrier((core.send(in_theirs, 1), out_kept))
-    in_kept, in_parts = pair_sums(in_mine, arrived_in, y, "in_pair")
-    back_left = exchange(left, peers)
-
-    last = ((peers * MAIN, LANES), lambda i: (0, cut // LANES - 1))
+    )(arrived_grads, derivative, weights_out, turned, incoming, gain, *pieces_in)
+    in_kept, in_parts = pair_sums(in_mine, [core.send(part, 1) for part in in_theirs], y, "in_pair")
+    returned, packed_grads, in_kept = lax.optimization_barrier((returned, packed_grads, in_kept))
+
+    last = ((peers * MAIN, LANES), lambda i: (0, 1 + width // LANES))
     sent_back, grad_logits = call(
         part(route_kernel, peers),
         "route",
-        shape(peers * MAIN, cut),
+        shape(peers * MAIN, width + 2 * LANES),
         shape(count, peers, dtype=f32),
         in_blocks=(None,) * 7 + ("any",),
         out_blocks=(last, None),
+        aliases={7: 0},
+    )(returned, normed, out_grad, meta, router_rows, gain, gain_expert, packed_grads)
+    returned, sent_back = lax.optimization_barrier((returned, sent_back))
+    back = exchange(sent_back, peers)
+    grad_incoming, _ = lax.optimization_barrier((grad_incoming, grad_logits))
+    *out_theirs, out_mine = call(
+        outer_kernel,
+        "outer",
+        *[shape(inner // groups, width)] * half,
+        shape(half, inner // groups, width),
+        grid=half,
+        in_blocks=(None, column),
+        out_blocks=(None,) * half + (whole,),
+        order=(y.behind(), core.place[None].astype(jnp.int32)),
         cost=LONG,
-        aliases={7: 0},
-    )(returned, normed, out_grad, meta, router_rows, gain, gain_expert, right)
-    sent_back, back_left, in_kept = lax.optimization_barrier((sent_back, back_left, in_kept))
-    back = exchange(sent_back, peers)
-    returned, out_parts = lax.optimization_barrier((returned, out_parts))
-    mixed = call(part(mixed_kernel, peers), "mixed", shape(count, width), cost=LONG)(returned, frames, meta)
-    back, out_parts, mixed = lax.optimization_barrier((back, out_parts, mixed))
+    )(grad_incoming, hidden)
+    arrived_out, in_parts = lax.optimization_barrier(([core.send(part, 1) for part in out_theirs], in_parts))
+    out_kept, out_parts = pair_sums(out_mine, arrived_out, y, "out_pair")
+    mixed = call(part(mixed_kernel, peers), "mixed", shape(count, width))(returned, frames, meta)
+    back, out_kept, mixed = lax.optimization_barrier((back, out_kept, mixed))
     sums = call(
         part(tally_kernel, peers), "tally", shape(groups, 8, width // 4, dtype=f32), in_blocks=(last,), mib=4
     )(back)
     sums = lax.all_to_all(sums, "dp", 0, 0, tiled=True)
     grad_frames = call(part(finish_kernel, peers), "finish", shape(count, width))(
-        back_left, back, frames, gain, out_grad, meta, grad_logits, router_rows
-    )
-    sums, in_parts, grad_frames = lax.optimization_barrier((sums, in_parts, grad_frames))
+        back, frames, gain, out_grad, meta, grad_logits, router_rows
+    )
+    sums, grad_frames = lax.optimization_barrier((sums, grad_frames))
     router_mine, gain_gradient = call(
         sum_kernel, "sum", shape(peers, 8, width // 8, dtype=f32), shape(1, width, dtype=f32), mib=4
     )(sums)

time: 208 us -> 209 us (level)
  local copies, waits for them, and re-layouts: 3.74 us -> 7.52 us
  waiting for transfers between devices: 43.2 us -> 39.6 us
    all_to_all x5 -> x4, waiting for transfers between devices: 16.4 us -> 9.13 us  [exchange(): lax.all_to_all(packed.reshape(peers, MAIN, packed.shape[1]), 'expert', sp...]
    unnamed x43 -> x61, local copies, waits for them, and re-layouts: 3.74 us -> 7.52 us
    ppermute x22 -> x28, starting transfers between devices: 24.7 us -> 27.6 us  [send(): lax.ppermute(array, self.name, [(i, self.step(i, k)) for i in range(self....]
    all_to_all x1, waiting for transfers between devices: 0.92 us -> 3.73 us  [on_device(): sums = lax.all_to_all(sums, 'dp', 0, 0, tiled=True)]
    all_to_all x5 -> x4, starting transfers between devices: 40.7 us -> 37.9 us  [exchange(): lax.all_to_all(packed.reshape(peers, MAIN, packed.shape[1]), 'expert', sp...]
    ppermute x22 -> x28, waiting for transfers between devices: 20.9 us -> 23.6 us  [send(): lax.ppermute(array, self.name, [(i, self.step(i, k)) for i in range(self....]
  transfers between devices with their start and end apart: 29 -> 34, of which waited for: 13 -> 18; matrix products, arithmetic and copies ran while one was open for 1% -> 1% of each run, Pallas kernels for 36% -> 37%
where the time goes in v4:
time: 209 us; the launch traced here: 208 us
  starting transfers between devices  82.3 us (39%)
  Pallas kernels  76.2 us (36%)
  waiting for transfers between devices  39.6 us (19%)
  local copies, waits for them, and re-layouts  7.52 us (4%)
    pallas_call x14, Pallas kernels, run(): pl.pallas_call(kernel, out_shape=outs if len(outs) > 1 else outs[0], grid...  76.2 us
    all_to_all x4, starting transfers between devices, exchange(): lax.all_to_all(packed.reshape(peers, MAIN, packed.shape[1]), 'expert', sp...  37.9 us
    ppermute x28, starting transfers between devices, send(): lax.ppermute(array, self.name, [(i, self.step(i, k)) for i in range(self....  27.6 us
    ppermute x28, waiting for transfers between devices, send(): lax.ppermute(array, self.name, [(i, self.step(i, k)) for i in range(self....  23.6 us
    all_to_all x1, starting transfers between devices, on_device(): lax.all_to_all(router_mine, 'expert', 0, 0, tiled=True)  9.5 us
    all_to_all x4, waiting for transfers between devices, exchange(): lax.all_to_all(packed.reshape(peers, MAIN, packed.shape[1]), 'expert', sp...  9.13 us
    unnamed x61, local copies, waits for them, and re-layouts  7.52 us
    all_to_all x1, starting transfers between devices, on_device(): sums = lax.all_to_all(sums, 'dp', 0, 0, tiled=True)  7.27 us
  transfers between devices with their start and end apart: 34, of which 18 were waited for; matrix products, arithmetic and copies ran while one was open for 1% of the time, Pallas kernels for 37%

profile of v4, /device:TPU:1, one launch (start us, length us, event | category | flops | bytes accessed | tf_op | source)
XLA Modules:
  0.0 207.7 jit_solution(11467843579364444242)
XLA Ops:
  0.6 2.2 %collective-permute-start = (bf16[128,2048]{1,0:T(8,128)(2,1)}, bf16[128,2048]{1,0:T(8,128)(2,1)}, u32[]{:S(2)}, u32[]{:S(2)}) collective-permute-start(bf16[128,2048]{1,0:T(8,128)(2,1)} %bitcast.32), channel_id=1, source_target_pairs={{0,64},{32,96},{64,128},{96,160},{128,192},{160,224},{192,0},{224,... | collective-permute-start | bytes 1572872 | tf_op jit(solution)/shard_map/ppermute | solution.py:416
  2.8 2.6 %collective-permute-start.1 = (bf16[128,2048]{1,0:T(8,128)(2,1)}, bf16[128,2048]{1,0:T(8,128)(2,1)}, u32[]{:S(2)}, u32[]{:S(2)}) collective-permute-start(bf16[128,2048]{1,0:T(8,128)(2,1)} %bitcast.33), channel_id=1, source_target_pairs={{0,128},{32,160},{64,192},{96,224},{128,0},{160,32},{192,64},{224,... | collective-permute-start | bytes 1572872 | tf_op jit(solution)/shard_map/ppermute | solution.py:416
  5.5 1.1 collective-permute-start.2
  6.5 3.2 %dispatch.1 = (bf16[512,1152]{1,0:T(8,128)(2,1)}, bf16[192,1024]{1,0:T(8,128)(2,1)}, s32[2,192]{1,0:T(2,128)}) custom-call(bf16[192,1024]{1,0:T(8,128)(2,1)} %frames_ref.5, f32[1,1024]{1,0:T(1,128)} %bitcast.51, s32[2,192]{1,0:T(2,128)} %bitcast.58), custom_call_target="tpu_custom_call" | custom-call | flops 99999997952 | bytes 1 | tf_op jit(solution)/shard_map/dispatch/pallas_call | solution.py:370
  9.7 11.0 %all-to-all-start = ((bf16[32,16,1152]{2,1,0:T(8,128)(2,1)}), bf16[32,16,1152]{2,1,0:T(8,128)(2,1)S(1)}, u32[]{:S(2)}, u32[]{:S(2)}) async-start(bf16[32,16,1152]{2,1,0:T(8,128)(2,1)} %bitcast.40), calls=%async_computation | async-start | bytes 2359296 | tf_op jit(solution)/shard_map/all_to_all | solution.py:394
  20.8 3.4 %grads.1 = (bf16[512,1152]{1,0:T(8,128)(2,1)}, f32[192,16]{1,0:T(8,128)}) custom-call(bf16[192,1024]{1,0:T(8,128)(2,1)} %get-tuple-element.84.normed_ref, bf16[32,1024]{1,0:T(8,128)(2,1)} %bitcast.47, s32[2,192]{1,0:T(2,128)} %bitcast.59, s32[1,192]{1,0:T(1,128)} %bitcast.60, s32[2,192]{1,0:T(2,128)} %get-tuple-element.85.place_ref, bf16[192,1024]{1,0:T(8,128)(2,1)} %grad_ref.5), custom_call_target="tpu_custom_call" | custom-call | flops 99999997952 | bytes 1 | tf_op jit(solution)/shard_map/grads/pallas_call | solution.py:370
  24.2 4.2 %collective-permute-done.1.refs_2_ = bf16[128,2048]{1,0:T(8,128)(2,1)} collective-permute-done((bf16[128,2048]{1,0:T(8,128)(2,1)}, bf16[128,2048]{1,0:T(8,128)(2,1)}, u32[]{:S(2)}, u32[]{:S(2)}) %collective-permute-start.1) | collective-permute-done | bytes 524320 | tf_op jit(solution)/shard_map/ppermute | solution.py:416
  28.3 1.5 collective-permute-start.3
  30.5 0.9 collective-permute-start.7
  31.4 2.5 %collective-permute-start.8 = (bf16[256,1024]{1,0:T(8,128)(2,1)S(1)}, bf16[256,1024]{1,0:T(8,128)(2,1)S(1)}, u32[]{:S(2)}, u32[]{:S(2)}) collective-permute-start(bf16[256,1024]{1,0:T(8,128)(2,1)S(1)} %bitcast.44), channel_id=1, source_target_pairs={{0,192},{32,224},{64,0},{96,32},{128,64},{160,96},{192,128},{224,1... | collective-permute-start | bytes 1572872 | tf_op jit(solution)/shard_map/ppermute | solution.py:416
  33.9 10.9 %collective-permute-done.7.refs_1_ = bf16[256,1024]{1,0:T(8,128)(2,1)S(1)} collective-permute-done((bf16[256,1024]{1,0:T(8,128)(2,1)S(1)}, bf16[256,1024]{1,0:T(8,128)(2,1)S(1)}, u32[]{:S(2)}, u32[]{:S(2)}) %collective-permute-start.7) | collective-permute-done | bytes 524320 | tf_op jit(solution)/shard_map/ppermute | solution.py:416
  44.8 0.8 copy-done.16
  45.6 0.8 copy-done.17
  46.4 2.4 %all-to-all-done = bf16[32,16,1152]{2,1,0:T(8,128)(2,1)S(1)} async-done(((bf16[32,16,1152]{2,1,0:T(8,128)(2,1)}), bf16[32,16,1152]{2,1,0:T(8,128)(2,1)S(1)}, u32[]{:S(2)}, u32[]{:S(2)}) %all-to-all-start) | async-done | bytes 1179680 | tf_op jit(solution)/shard_map/all_to_all | solution.py:394
  48.8 8.6 %all-to-all-start.1 = ((bf16[32,16,1152]{2,1,0:T(8,128)(2,1)}), bf16[32,16,1152]{2,1,0:T(8,128)(2,1)S(1)}, u32[]{:S(2)}, u32[]{:S(2)}) async-start(bf16[32,16,1152]{2,1,0:T(8,128)(2,1)} %bitcast.38), calls=%async_computation.1 | async-start | bytes 2359296 | tf_op jit(solution)/shard_map/all_to_all | solution.py:394
  57.4 2.1 collective-permute-start.9
  60.2 1.8 collective-permute-start.10
  62.5 9.8 %first.1 = (bf16[576,1024]{1,0:T(8,128)(2,1)}, bf16[576,2048]{1,0:T(8,128)(2,1)}, f32[576,2048]{1,0:T(8,128)}, bf16[1024,576]{1,0:T(8,128)(2,1)}) custom-call(s32[8]{0:T(128)} %pad_add_fusion.order_ref.holders_ref, bf16[512,1152]{1,0:T(8,128)(2,1)} %bitcast.31, bf16[128,2048]{1,0:T(8,128)(2,1)} %bitcast.35, bf16[128,2048]{1,0:T(8,128)(2,1)} %collective-permute-done.refs_1_, ...), custom_call_target="tpu_custom_call" | custom-call | flops 1 | bytes 1 | tf_op jit(solution)/shard_map/first/pallas_call | solution.py:370
  72.3 1.2 collective-permute-start.12
  73.5 1.7 collective-permute-done.12.refs_6_
  75.2 0.8 copy-done.29
  76.1 9.1 %second.1 = (bf16[512,1152]{1,0:T(8,128)(2,1)}, bf16[2048,1024]{1,0:T(8,128)(2,1)}) custom-call(s32[8]{0:T(128)} %pad_add_fusion.order_ref.holders_ref, bf16[576,2048]{1,0:T(8,128)(2,1)} %get-tuple-element.103.hidden_ref, bf16[256,1024]{1,0:T(8,128)(2,1)} %bitcast.42, bf16[256,1024]{1,0:T(8,128)(2,1)} %copy-done.16, ...), custom_call_target="tpu_custom_call" | custom-call | flops 1 | bytes 1 | tf_op jit(solution)/shard_map/second/pallas_call | solution.py:370
  85.7 8.8 %all-to-all-start.2 = ((bf16[32,16,1152]{2,1,0:T(8,128)(2,1)}), bf16[32,16,1152]{2,1,0:T(8,128)(2,1)S(1)}, u32[]{:S(2)}, u32[]{:S(2)}) async-start(bf16[32,16,1152]{2,1,0:T(8,128)(2,1)} %bitcast.39), calls=%async_computation.2 | async-start | bytes 2359296 | tf_op jit(solution)/shard_map/all_to_all | solution.py:394
  95.0 18.1 %backward.1 = (bf16[576,1024]{1,0:T(8,128)(2,1)}, bf16[128,2048]{1,0:T(8,128)(2,1)}, bf16[128,2048]{1,0:T(8,128)(2,1)}, bf16[128,2048]{1,0:T(8,128)(2,1)}, bf16[...) custom-call(s32[4]{0:T(128)} %and_select_fusion.order_ref, ...), custom_call_target="tpu_custom_call" | custom-call | flops 1 | bytes 1 | tf_op jit(solution)/shard_map/backward/pallas_call | solution.py:370
  114.5 1.1 collective-permute-done.14.refs_0_
  115.6 0.7 collective-permute-done.15.refs_1_
  117.9 0.8 copy-done.28
  118.7 3.3 %in_pair.1 = (f32[128,2048]{1,0:T(8,128)}, bf16[128,2048]{1,0:T(8,128)(2,1)}, bf16[128,2048]{1,0:T(8,128)(2,1)}, bf16[128,2048]{1,0:T(8,128)(2,1)}) custom-call(bf16[4,128,2048]{2,1,0:T(8,128)(2,1)} %get-tuple-element.116.mine_ref, bf16[128,2048]{1,0:T(8,128)(2,1)} %copy-done.23, bf16[128,2048]{1,0:T(8,128)(2,1)} %copy-done.25, ...), custom_call_target="tpu_custom_call" | custom-call | flops 1 | bytes 1 | tf_op jit(solution)/shard_map/in_pair/pallas_call | solution.py:370
  122.0 2.7 %collective-permute-start.22 = (bf16[128,2048]{1,0:T(8,128)(2,1)}, bf16[128,2048]{1,0:T(8,128)(2,1)S(1)}, u32[]{:S(2)}, u32[]{:S(2)}) collective-permute-start(bf16[128,2048]{1,0:T(8,128)(2,1)} %get-tuple-element.135), channel_id=1, source_target_pairs={{0,192},{32,224},{64,0},{96,32},{128,64},{160,96},{192,128},{224,1... | collective-permute-start | bytes 1572872 | tf_op jit(solution)/shard_map/ppermute | solution.py:416
  125.4 1.0 copy-done.1
  126.4 4.4 %route.1 = (bf16[512,1280]{1,0:T(8,128)(2,1)}, f32[192,32]{1,0:T(8,128)}) custom-call(bf16[512,1152]{1,0:T(8,128)(2,1)} %bitcast.27, bf16[192,1024]{1,0:T(8,128)(2,1)} %get-tuple-element.84.normed_ref, bf16[192,1024]{1,0:T(8,128)(2,1)} %grad_ref.5, f32[192,16]{1,0:T(8,128)} %get-tuple-element.87.meta_ref, ...), custom_call_target="tpu_custom_call", output_to_operand_aliasing={{0}: (7, {})} | custom-call | flops 1 | bytes 1 | tf_op jit(solution)/shard_map/route/pallas_call | solution.py:370
  130.8 9.5 %all-to-all-start.3 = ((bf16[32,16,1280]{2,1,0:T(8,128)(2,1)}), bf16[32,16,1280]{2,1,0:T(8,128)(2,1)S(1)}, u32[]{:S(2)}, u32[]{:S(2)}) async-start(bf16[32,16,1280]{2,1,0:T(8,128)(2,1)} %bitcast.29), calls=%async_computation.3 | async-start | bytes 2621440 | tf_op jit(solution)/shard_map/all_to_all | solution.py:394
  140.3 8.2 %outer.1 = (bf16[256,1024]{1,0:T(8,128)(2,1)}, bf16[256,1024]{1,0:T(8,128)(2,1)}, bf16[256,1024]{1,0:T(8,128)(2,1)}, bf16[256,1024]{1,0:T(8,128)(2,1)}, bf16[4,256,1024]{2,1,0:T(8,128)(2,1)}) custom-call(s32[4]{0:T(128)} %and_select_fusion.order_ref, s32[1]{0:T(128)} %bitcast.14.core_ref, bf16[576,1024]{1,0:T(8,128)(2,1)} %get-tuple-element.129.grads_ref, ...), custom_call_target="tpu_custom_call" | custom-call | flops 99999997952 | bytes 1 | tf_op jit(solution)/shard_map/outer/pallas_call | solution.py:370
  148.5 1.2 collective-permute-start.18
  154.5 3.4 %out_pair.1 = (f32[256,1024]{1,0:T(8,128)}, bf16[256,1024]{1,0:T(8,128)(2,1)}, bf16[256,1024]{1,0:T(8,128)(2,1)}, bf16[256,1024]{1,0:T(8,128)(2,1)}) custom-call(bf16[4,256,1024]{2,1,0:T(8,128)(2,1)} %get-tuple-element.130.mine_ref, bf16[256,1024]{1,0:T(8,128)(2,1)} %copy-done.18, bf16[256,1024]{1,0:T(8,128)(2,1)} %copy-done.19, ...), custom_call_target="tpu_custom_call" | custom-call | flops 1 | bytes 1 | tf_op jit(solution)/shard_map/out_pair/pallas_call | solution.py:370
  157.9 2.1 %collective-permute-start.25 = (bf16[256,1024]{1,0:T(8,128)(2,1)}, bf16[256,1024]{1,0:T(8,128)(2,1)S(1)}, u32[]{:S(2)}, u32[]{:S(2)}) collective-permute-start(bf16[256,1024]{1,0:T(8,128)(2,1)} %get-tuple-element.149), channel_id=1, source_target_pairs={{0,192},{32,224},{64,0},{96,32},{128,64},{160,96},{192,128},{224,1... | collective-permute-start | bytes 1572872 | tf_op jit(solution)/shard_map/ppermute | solution.py:416
  160.1 2.0 collective-permute-start.26
  162.1 3.1 %mixed.1 = bf16[192,1024]{1,0:T(8,128)(2,1)} custom-call(bf16[512,1152]{1,0:T(8,128)(2,1)} %bitcast.28, bf16[192,1024]{1,0:T(8,128)(2,1)} %frames_ref.5, f32[192,16]{1,0:T(8,128)} %get-tuple-element.87.meta_ref), custom_call_target="tpu_custom_call" | custom-call | flops 1 | bytes 1 | tf_op jit(solution)/shard_map/mixed/pallas_call | solution.py:370
  165.2 6.2 %all-to-all-done.3 = bf16[32,16,1280]{2,1,0:T(8,128)(2,1)S(1)} async-done(((bf16[32,16,1280]{2,1,0:T(8,128)(2,1)}), bf16[32,16,1280]{2,1,0:T(8,128)(2,1)S(1)}, u32[]{:S(2)}, u32[]{:S(2)}) %all-to-all-start.3) | async-done | bytes 1310752 | tf_op jit(solution)/shard_map/all_to_all | solution.py:394
  171.4 1.1 tally.1
  172.5 7.3 %all-to-all-start.4 = ((f32[8,8,256]{2,1,0:T(8,128)}), f32[8,8,256]{2,1,0:T(8,128)S(1)}, u32[]{:S(2)}, u32[]{:S(2)}) async-start(f32[8,8,256]{2,1,0:T(8,128)} %tally.1), calls=%async_computation.4 | async-start | bytes 131072 | tf_op jit(solution)/shard_map/all_to_all | solution.py:584
  179.8 3.9 %finish.1 = bf16[192,1024]{1,0:T(8,128)(2,1)} custom-call(bf16[512,1280]{1,0:T(8,128)(2,1)} %bitcast.26, bf16[192,1024]{1,0:T(8,128)(2,1)} %frames_ref.5, f32[1,1024]{1,0:T(1,128)} %bitcast.54, bf16[192,1024]{1,0:T(8,128)(2,1)} %grad_ref.5, f32[192,16]{1,0:T(8,128)} %get-tuple-element.87.meta_ref, f32[192,32]{1,0:T(8,128)} %get-tuple-element.128.logits_ref, ...), custom_call_target="tpu_custom_call" | custom-call | flops 1 | bytes 1 | tf_op jit(solution)/shard_map/finish/pallas_call | solution.py:370
  183.7 3.7 %all-to-all-done.4.sums_ref = f32[8,8,256]{2,1,0:T(8,128)S(1)} async-done(((f32[8,8,256]{2,1,0:T(8,128)}), f32[8,8,256]{2,1,0:T(8,128)S(1)}, u32[]{:S(2)}, u32[]{:S(2)}) %all-to-all-start.4) | async-done | bytes 65568 | tf_op jit(solution)/shard_map/all_to_all | solution.py:584
  188.1 9.5 %all-to-all-start.5 = ((f32[32,8,128]{2,1,0:T(8,128)}), f32[32,8,128]{2,1,0:T(8,128)S(1)}, u32[]{:S(2)}, u32[]{:S(2)}) async-start(f32[32,8,128]{2,1,0:T(8,128)} %get-tuple-element.158), calls=%async_computation.5 | async-start | bytes 262144 | tf_op jit(solution)/shard_map/all_to_all | solution.py:592
  197.7 0.8 copy-done.12
  198.7 0.8 copy-done.14
  199.5 4.3 %total.1 = (f32[256,1024]{1,0:T(8,128)}, f32[128,2048]{1,0:T(8,128)}) custom-call(f32[256,1024]{1,0:T(8,128)} %get-tuple-element.147.first_ref, f32[128,2048]{1,0:T(8,128)} %get-tuple-element.148.second_ref, bf16[256,1024]{1,0:T(8,128)(2,1)} %copy-done.12, bf16[256,1024]{1,0:T(8,128)(2,1)} %copy-done.13, bf16[256,1024]{1,0:T(8,128)(2,1)} %copy-done.14, ...), custom_call_target="tpu_custom_call" | custom-call | flops 1 | bytes 1 | tf_op jit(solution)/shard_map/total/pallas_call | solution.py:370
  203.8 3.2 %all-to-all-done.5 = f32[32,8,128]{2,1,0:T(8,128)S(1)} async-done(((f32[32,8,128]{2,1,0:T(8,128)}), f32[32,8,128]{2,1,0:T(8,128)S(1)}, u32[]{:S(2)}, u32[]{:S(2)}) %all-to-all-start.5) | async-done | bytes 131104 | tf_op jit(solution)/shard_map/all_to_all | solution.py:592
  (98 shorter events, 12.9 us)
Async XLA Ops:
  0.6 23.5 %collective-permute-start = (bf16[128,2048]{1,0:T(8,128)(2,1)}, bf16[128,2048]{1,0:T(8,128)(2,1)}, u32[]{:S(2)}, u32[]{:S(2)}) collective-permute-start(bf16[128,2048]{1,0:T(8,128)(2,1)} %bitcast.32), channel_id=1, source_target_pairs={{0,64},{32,96},{64,128},{96,160},{128,192},{160,224},{192,0},{224,... | collective-permute-start | bytes 1572872 | tf_op jit(solution)/shard_map/ppermute | solution.py:416
  2.8 25.5 %collective-permute-start.1 = (bf16[128,2048]{1,0:T(8,128)(2,1)}, bf16[128,2048]{1,0:T(8,128)(2,1)}, u32[]{:S(2)}, u32[]{:S(2)}) collective-permute-start(bf16[128,2048]{1,0:T(8,128)(2,1)} %bitcast.33), channel_id=1, source_target_pairs={{0,128},{32,160},{64,192},{96,224},{128,0},{160,32},{192,64},{224,... | collective-permute-start | bytes 1572872 | tf_op jit(solution)/shard_map/ppermute | solution.py:416
  5.5 22.9 %collective-permute-start.2 = (bf16[128,2048]{1,0:T(8,128)(2,1)}, bf16[128,2048]{1,0:T(8,128)(2,1)}, u32[]{:S(2)}, u32[]{:S(2)}) collective-permute-start(bf16[128,2048]{1,0:T(8,128)(2,1)} %bitcast.34), channel_id=1, source_target_pairs={{0,192},{32,224},{64,0},{96,32},{128,64},{160,96},{192,128},{224,1... | collective-permute-start | bytes 1572872 | tf_op jit(solution)/shard_map/ppermute | solution.py:416
  9.7 39.1 %all-to-all-start = ((bf16[32,16,1152]{2,1,0:T(8,128)(2,1)}), bf16[32,16,1152]{2,1,0:T(8,128)(2,1)S(1)}, u32[]{:S(2)}, u32[]{:S(2)}) async-start(bf16[32,16,1152]{2,1,0:T(8,128)(2,1)} %bitcast.40), calls=%async_computation | async-start | bytes 2359296 | tf_op jit(solution)/shard_map/all_to_all | solution.py:394
  20.8 7.6 %copy-start.4 = (bf16[1,128,2048]{2,1,0:T(8,128)(2,1)S(1)}, bf16[1,128,2048]{2,1,0:T(8,128)(2,1)}, u32[]{:S(2)}) copy-start(bf16[1,128,2048]{2,1,0:T(8,128)(2,1)} %param.11) | copy-start | bytes 1572868
  20.8 9.7 %copy-start.15 = (bf16[1,256,1024]{2,1,0:T(8,128)(2,1)S(1)}, bf16[1,256,1024]{2,1,0:T(8,128)(2,1)}, u32[]{:S(2)}) copy-start(bf16[1,256,1024]{2,1,0:T(8,128)(2,1)} %param.12) | copy-start | bytes 1572868
  28.3 3.1 %collective-permute-start.3 = (bf16[128,2048]{1,0:T(8,128)(2,1)S(1)}, bf16[128,2048]{1,0:T(8,128)(2,1)S(1)}, u32[]{:S(2)}, u32[]{:S(2)}) collective-permute-start(bf16[128,2048]{1,0:T(8,128)(2,1)S(1)} %bitcast.37), channel_id=1, source_target_pairs={{0,32},{32,0},{64,96},{96,64},{128,160},{160,128},{192,224},{224,1... | collective-permute-start | bytes 1572872 | tf_op jit(solution)/shard_map/ppermute | solution.py:416
  29.9 4.0 %collective-permute-start.4 = (bf16[128,2048]{1,0:T(8,128)(2,1)}, bf16[128,2048]{1,0:T(8,128)(2,1)S(1)}, u32[]{:S(2)}, u32[]{:S(2)}) collective-permute-start(bf16[128,2048]{1,0:T(8,128)(2,1)} %collective-permute-done.refs_1_), channel_id=1, source_target_pairs={{0,32},{32,0},{64,96},{96,64},{128,160},{160,128},{192,224},{224,1... | collective-permute-start | bytes 1572872 | tf_op jit(solution)/shard_map/ppermute | solution.py:416
  30.0 3.9 %collective-permute-start.5 = (bf16[128,2048]{1,0:T(8,128)(2,1)}, bf16[128,2048]{1,0:T(8,128)(2,1)S(1)}, u32[]{:S(2)}, u32[]{:S(2)}) collective-permute-start(bf16[128,2048]{1,0:T(8,128)(2,1)} %collective-permute-done.1.refs_2_), channel_id=1, source_target_pairs={{0,32},{32,0},{64,96},{96,64},{128,160},{160,128},{192,224},{224,1... | collective-permute-start | bytes 1572872 | tf_op jit(solution)/shard_map/ppermute | solution.py:416
  30.4 3.5 %collective-permute-start.6 = (bf16[128,2048]{1,0:T(8,128)(2,1)}, bf16[128,2048]{1,0:T(8,128)(2,1)S(1)}, u32[]{:S(2)}, u32[]{:S(2)}) collective-permute-start(bf16[128,2048]{1,0:T(8,128)(2,1)} %collective-permute-done.2.refs_3_), channel_id=1, source_target_pairs={{0,32},{32,0},{64,96},{96,64},{128,160},{160,128},{192,224},{224,1... | collective-permute-start | bytes 1572872 | tf_op jit(solution)/shard_map/ppermute | solution.py:416
  30.5 14.3 %collective-permute-start.7 = (bf16[256,1024]{1,0:T(8,128)(2,1)S(1)}, bf16[256,1024]{1,0:T(8,128)(2,1)S(1)}, u32[]{:S(2)}, u32[]{:S(2)}) collective-permute-start(bf16[256,1024]{1,0:T(8,128)(2,1)S(1)} %bitcast.43), channel_id=1, source_target_pairs={{0,64},{32,96},{64,128},{96,160},{128,192},{160,224},{192,0},{224,... | collective-permute-start | bytes 1572872 | tf_op jit(solution)/shard_map/ppermute | solution.py:416
  31.4 31.0 %copy-start.5 = (bf16[128,2048]{1,0:T(8,128)(2,1)}, bf16[128,2048]{1,0:T(8,128)(2,1)S(1)}, u32[]{:S(2)}) copy-start(bf16[128,2048]{1,0:T(8,128)(2,1)S(1)} %collective-permute-done.3.refs_4_) | copy-start | bytes 1572868
  31.4 13.4 %collective-permute-start.8 = (bf16[256,1024]{1,0:T(8,128)(2,1)S(1)}, bf16[256,1024]{1,0:T(8,128)(2,1)S(1)}, u32[]{:S(2)}, u32[]{:S(2)}) collective-permute-start(bf16[256,1024]{1,0:T(8,128)(2,1)S(1)} %bitcast.44), channel_id=1, source_target_pairs={{0,192},{32,224},{64,0},{96,32},{128,64},{160,96},{192,128},{224,1... | collective-permute-start | bytes 1572872 | tf_op jit(solution)/shard_map/ppermute | solution.py:416
  33.9 14.9 %copy-start.6 = (bf16[128,2048]{1,0:T(8,128)(2,1)}, bf16[128,2048]{1,0:T(8,128)(2,1)S(1)}, u32[]{:S(2)}) copy-start(bf16[128,2048]{1,0:T(8,128)(2,1)S(1)} %collective-permute-done.4.refs_5_) | copy-start | bytes 1572868
  33.9 14.9 %copy-start.7 = (bf16[128,2048]{1,0:T(8,128)(2,1)}, bf16[128,2048]{1,0:T(8,128)(2,1)S(1)}, u32[]{:S(2)}) copy-start(bf16[128,2048]{1,0:T(8,128)(2,1)S(1)} %collective-permute-done.5.refs_6_) | copy-start | bytes 1572868
  33.9 10.9 %copy-start.8 = (bf16[128,2048]{1,0:T(8,128)(2,1)}, bf16[128,2048]{1,0:T(8,128)(2,1)S(1)}, u32[]{:S(2)}) copy-start(bf16[128,2048]{1,0:T(8,128)(2,1)S(1)} %collective-permute-done.6.refs_7_) | copy-start | bytes 1572868
  48.8 13.7 %copy-start.3 = (bf16[32,16,1152]{2,1,0:T(8,128)(2,1)}, bf16[32,16,1152]{2,1,0:T(8,128)(2,1)S(1)}, u32[]{:S(2)}) copy-start(bf16[32,16,1152]{2,1,0:T(8,128)(2,1)S(1)} %all-to-all-done) | copy-start | bytes 3538948
  48.8 36.8 %all-to-all-start.1 = ((bf16[32,16,1152]{2,1,0:T(8,128)(2,1)}), bf16[32,16,1152]{2,1,0:T(8,128)(2,1)S(1)}, u32[]{:S(2)}, u32[]{:S(2)}) async-start(bf16[32,16,1152]{2,1,0:T(8,128)(2,1)} %bitcast.38), calls=%async_computation.1 | async-start | bytes 2359296 | tf_op jit(solution)/shard_map/all_to_all | solution.py:394
  57.4 14.8 %collective-permute-start.9 = (bf16[256,1024]{1,0:T(8,128)(2,1)S(1)}, bf16[256,1024]{1,0:T(8,128)(2,1)}, u32[]{:S(2)}, u32[]{:S(2)}) collective-permute-start(bf16[256,1024]{1,0:T(8,128)(2,1)S(1)} %bitcast.45), channel_id=1, source_target_pairs={{0,128},{32,160},{64,192},{96,224},{128,0},{160,32},{192,64},{224,... | collective-permute-start | bytes 1572872 | tf_op jit(solution)/shard_map/ppermute | solution.py:416
  60.2 13.3 %collective-permute-start.10 = (bf16[256,1024]{1,0:T(8,128)(2,1)S(1)}, bf16[256,1024]{1,0:T(8,128)(2,1)S(1)}, u32[]{:S(2)}, u32[]{:S(2)}) collective-permute-start(bf16[256,1024]{1,0:T(8,128)(2,1)S(1)} %bitcast.46), channel_id=1, source_target_pairs={{0,32},{32,0},{64,96},{96,64},{128,160},{160,128},{192,224},{224,1... | collective-permute-start | bytes 1572872 | tf_op jit(solution)/shard_map/ppermute | solution.py:416
  62.0 11.5 %collective-permute-start.11 = (bf16[256,1024]{1,0:T(8,128)(2,1)}, bf16[256,1024]{1,0:T(8,128)(2,1)S(1)}, u32[]{:S(2)}, u32[]{:S(2)}) collective-permute-start(bf16[256,1024]{1,0:T(8,128)(2,1)} %copy-done.16), channel_id=1, source_target_pairs={{0,32},{32,0},{64,96},{96,64},{128,160},{160,128},{192,224},{224,1... | collective-permute-start | bytes 1572872 | tf_op jit(solution)/shard_map/ppermute | solution.py:416
  62.0 11.5 %collective-permute-start.13 = (bf16[256,1024]{1,0:T(8,128)(2,1)}, bf16[256,1024]{1,0:T(8,128)(2,1)S(1)}, u32[]{:S(2)}, u32[]{:S(2)}) collective-permute-start(bf16[256,1024]{1,0:T(8,128)(2,1)} %copy-done.17), channel_id=1, source_target_pairs={{0,32},{32,0},{64,96},{96,64},{128,160},{160,128},{192,224},{224,1... | collective-permute-start | bytes 1572872 | tf_op jit(solution)/shard_map/ppermute | solution.py:416
  72.3 2.9 %collective-permute-start.12 = (bf16[256,1024]{1,0:T(8,128)(2,1)}, bf16[256,1024]{1,0:T(8,128)(2,1)S(1)}, u32[]{:S(2)}, u32[]{:S(2)}) collective-permute-start(bf16[256,1024]{1,0:T(8,128)(2,1)} %collective-permute-done.9.refs_2_), channel_id=1, source_target_pairs={{0,32},{32,0},{64,96},{96,64},{128,160},{160,128},{192,224},{224,1... | collective-permute-start | bytes 1572872 | tf_op jit(solution)/shard_map/ppermute | solution.py:416
  85.7 9.3 %copy-start.2 = (bf16[32,16,1152]{2,1,0:T(8,128)(2,1)}, bf16[32,16,1152]{2,1,0:T(8,128)(2,1)S(1)}, u32[]{:S(2)}) copy-start(bf16[32,16,1152]{2,1,0:T(8,128)(2,1)S(1)} %all-to-all-done.1) | copy-start | bytes 3538948
  85.7 39.7 %all-to-all-start.2 = ((bf16[32,16,1152]{2,1,0:T(8,128)(2,1)}), bf16[32,16,1152]{2,1,0:T(8,128)(2,1)S(1)}, u32[]{:S(2)}, u32[]{:S(2)}) async-start(bf16[32,16,1152]{2,1,0:T(8,128)(2,1)} %bitcast.39), calls=%async_computation.2 | async-start | bytes 2359296 | tf_op jit(solution)/shard_map/all_to_all | solution.py:394
  113.1 2.5 %collective-permute-start.14 = (bf16[128,2048]{1,0:T(8,128)(2,1)}, bf16[128,2048]{1,0:T(8,128)(2,1)S(1)}, u32[]{:S(2)}, u32[]{:S(2)}) collective-permute-start(bf16[128,2048]{1,0:T(8,128)(2,1)} %get-tuple-element.117), channel_id=1, source_target_pairs={{0,32},{32,0},{64,96},{96,64},{128,160},{160,128},{192,224},{224,1... | collective-permute-start | bytes 1572872 | tf_op jit(solution)/shard_map/ppermute | solution.py:416
  113.9 2.5 %collective-permute-start.15 = (bf16[128,2048]{1,0:T(8,128)(2,1)}, bf16[128,2048]{1,0:T(8,128)(2,1)S(1)}, u32[]{:S(2)}, u32[]{:S(2)}) collective-permute-start(bf16[128,2048]{1,0:T(8,128)(2,1)} %get-tuple-element.118), channel_id=1, source_target_pairs={{0,32},{32,0},{64,96},{96,64},{128,160},{160,128},{192,224},{224,1... | collective-permute-start | bytes 1572872 | tf_op jit(solution)/shard_map/ppermute | solution.py:416
  114.0 3.1 %collective-permute-start.16 = (bf16[128,2048]{1,0:T(8,128)(2,1)}, bf16[128,2048]{1,0:T(8,128)(2,1)S(1)}, u32[]{:S(2)}, u32[]{:S(2)}) collective-permute-start(bf16[128,2048]{1,0:T(8,128)(2,1)} %get-tuple-element.119), channel_id=1, source_target_pairs={{0,32},{32,0},{64,96},{96,64},{128,160},{160,128},{192,224},{224,1... | collective-permute-start | bytes 1572872 | tf_op jit(solution)/shard_map/ppermute | solution.py:416
  114.4 3.5 %collective-permute-start.17 = (bf16[128,2048]{1,0:T(8,128)(2,1)}, bf16[128,2048]{1,0:T(8,128)(2,1)S(1)}, u32[]{:S(2)}, u32[]{:S(2)}) collective-permute-start(bf16[128,2048]{1,0:T(8,128)(2,1)} %get-tuple-element.120), channel_id=1, source_target_pairs={{0,32},{32,0},{64,96},{96,64},{128,160},{160,128},{192,224},{224,1... | collective-permute-start | bytes 1572872 | tf_op jit(solution)/shard_map/ppermute | solution.py:416
  115.6 2.3 %copy-start.23 = (bf16[128,2048]{1,0:T(8,128)(2,1)}, bf16[128,2048]{1,0:T(8,128)(2,1)S(1)}, u32[]{:S(2)}) copy-start(bf16[128,2048]{1,0:T(8,128)(2,1)S(1)} %collective-permute-done.14.refs_0_) | copy-start | bytes 1572868
  122.0 27.7 %collective-permute-start.22 = (bf16[128,2048]{1,0:T(8,128)(2,1)}, bf16[128,2048]{1,0:T(8,128)(2,1)S(1)}, u32[]{:S(2)}, u32[]{:S(2)}) collective-permute-start(bf16[128,2048]{1,0:T(8,128)(2,1)} %get-tuple-element.135), channel_id=1, source_target_pairs={{0,192},{32,224},{64,0},{96,32},{128,64},{160,96},{192,128},{224,1... | collective-permute-start | bytes 1572872 | tf_op jit(solution)/shard_map/ppermute | solution.py:416
  124.7 25.5 %collective-permute-start.23 = (bf16[128,2048]{1,0:T(8,128)(2,1)}, bf16[128,2048]{1,0:T(8,128)(2,1)S(1)}, u32[]{:S(2)}, u32[]{:S(2)}) collective-permute-start(bf16[128,2048]{1,0:T(8,128)(2,1)} %get-tuple-element.136), channel_id=1, source_target_pairs={{0,128},{32,160},{64,192},{96,224},{128,0},{160,32},{192,64},{224,... | collective-permute-start | bytes 1572872 | tf_op jit(solution)/shard_map/ppermute | solution.py:416
  124.7 26.2 %collective-permute-start.24 = (bf16[128,2048]{1,0:T(8,128)(2,1)}, bf16[128,2048]{1,0:T(8,128)(2,1)S(1)}, u32[]{:S(2)}, u32[]{:S(2)}) collective-permute-start(bf16[128,2048]{1,0:T(8,128)(2,1)} %get-tuple-element.137), channel_id=1, source_target_pairs={{0,64},{32,96},{64,128},{96,160},{128,192},{160,224},{192,0},{224,... | collective-permute-start | bytes 1572872 | tf_op jit(solution)/shard_map/ppermute | solution.py:416
  130.8 40.6 %all-to-all-start.3 = ((bf16[32,16,1280]{2,1,0:T(8,128)(2,1)}), bf16[32,16,1280]{2,1,0:T(8,128)(2,1)S(1)}, u32[]{:S(2)}, u32[]{:S(2)}) async-start(bf16[32,16,1280]{2,1,0:T(8,128)(2,1)} %bitcast.29), calls=%async_computation.3 | async-start | bytes 2621440 | tf_op jit(solution)/shard_map/all_to_all | solution.py:394
  148.5 3.0 %collective-permute-start.18 = (bf16[256,1024]{1,0:T(8,128)(2,1)}, bf16[256,1024]{1,0:T(8,128)(2,1)S(1)}, u32[]{:S(2)}, u32[]{:S(2)}) collective-permute-start(bf16[256,1024]{1,0:T(8,128)(2,1)} %get-tuple-element.131), channel_id=1, source_target_pairs={{0,32},{32,0},{64,96},{96,64},{128,160},{160,128},{192,224},{224,1... | collective-permute-start | bytes 1572872 | tf_op jit(solution)/shard_map/ppermute | solution.py:416
  149.7 2.5 %collective-permute-start.19 = (bf16[256,1024]{1,0:T(8,128)(2,1)}, bf16[256,1024]{1,0:T(8,128)(2,1)S(1)}, u32[]{:S(2)}, u32[]{:S(2)}) collective-permute-start(bf16[256,1024]{1,0:T(8,128)(2,1)} %get-tuple-element.132), channel_id=1, source_target_pairs={{0,32},{32,0},{64,96},{96,64},{128,160},{160,128},{192,224},{224,1... | collective-permute-start | bytes 1572872 | tf_op jit(solution)/shard_map/ppermute | solution.py:416
  149.7 8.2 %copy-start.9 = (bf16[128,2048]{1,0:T(8,128)(2,1)}, bf16[128,2048]{1,0:T(8,128)(2,1)S(1)}, u32[]{:S(2)}) copy-start(bf16[128,2048]{1,0:T(8,128)(2,1)S(1)} %collective-permute-done.22.refs_3_) | copy-start | bytes 1572868
  149.7 3.2 %collective-permute-start.20 = (bf16[256,1024]{1,0:T(8,128)(2,1)}, bf16[256,1024]{1,0:T(8,128)(2,1)S(1)}, u32[]{:S(2)}, u32[]{:S(2)}) collective-permute-start(bf16[256,1024]{1,0:T(8,128)(2,1)} %get-tuple-element.133), channel_id=1, source_target_pairs={{0,32},{32,0},{64,96},{96,64},{128,160},{160,128},{192,224},{224,1... | collective-permute-start | bytes 1572872 | tf_op jit(solution)/shard_map/ppermute | solution.py:416
  150.2 7.7 %copy-start.10 = (bf16[128,2048]{1,0:T(8,128)(2,1)}, bf16[128,2048]{1,0:T(8,128)(2,1)S(1)}, u32[]{:S(2)}) copy-start(bf16[128,2048]{1,0:T(8,128)(2,1)S(1)} %collective-permute-done.23.refs_4_) | copy-start | bytes 1572868
  150.2 3.5 %collective-permute-start.21 = (bf16[256,1024]{1,0:T(8,128)(2,1)}, bf16[256,1024]{1,0:T(8,128)(2,1)S(1)}, u32[]{:S(2)}, u32[]{:S(2)}) collective-permute-start(bf16[256,1024]{1,0:T(8,128)(2,1)} %get-tuple-element.134), channel_id=1, source_target_pairs={{0,32},{32,0},{64,96},{96,64},{128,160},{160,128},{192,224},{224,1... | collective-permute-start | bytes 1572872 | tf_op jit(solution)/shard_map/ppermute | solution.py:416
  150.9 7.1 %copy-start.11 = (bf16[128,2048]{1,0:T(8,128)(2,1)}, bf16[128,2048]{1,0:T(8,128)(2,1)S(1)}, u32[]{:S(2)}) copy-start(bf16[128,2048]{1,0:T(8,128)(2,1)S(1)} %collective-permute-done.24.refs_5_) | copy-start | bytes 1572868
  151.4 2.3 %copy-start.18 = (bf16[256,1024]{1,0:T(8,128)(2,1)}, bf16[256,1024]{1,0:T(8,128)(2,1)S(1)}, u32[]{:S(2)}) copy-start(bf16[256,1024]{1,0:T(8,128)(2,1)S(1)} %collective-permute-done.18.refs_0_) | copy-start | bytes 1572868
  157.9 39.7 %collective-permute-start.25 = (bf16[256,1024]{1,0:T(8,128)(2,1)}, bf16[256,1024]{1,0:T(8,128)(2,1)S(1)}, u32[]{:S(2)}, u32[]{:S(2)}) collective-permute-start(bf16[256,1024]{1,0:T(8,128)(2,1)} %get-tuple-element.149), channel_id=1, source_target_pairs={{0,192},{32,224},{64,0},{96,32},{128,64},{160,96},{192,128},{224,1... | collective-permute-start | bytes 1572872 | tf_op jit(solution)/shard_map/ppermute | solution.py:416
  160.1 37.6 %collective-permute-start.26 = (bf16[256,1024]{1,0:T(8,128)(2,1)}, bf16[256,1024]{1,0:T(8,128)(2,1)S(1)}, u32[]{:S(2)}, u32[]{:S(2)}) collective-permute-start(bf16[256,1024]{1,0:T(8,128)(2,1)} %get-tuple-element.150), channel_id=1, source_target_pairs={{0,128},{32,160},{64,192},{96,224},{128,0},{160,32},{192,64},{224,... | collective-permute-start | bytes 1572872 | tf_op jit(solution)/shard_map/ppermute | solution.py:416
  162.1 35.6 %collective-permute-start.27 = (bf16[256,1024]{1,0:T(8,128)(2,1)}, bf16[256,1024]{1,0:T(8,128)(2,1)S(1)}, u32[]{:S(2)}, u32[]{:S(2)}) collective-permute-start(bf16[256,1024]{1,0:T(8,128)(2,1)} %get-tuple-element.151), channel_id=1, source_target_pairs={{0,64},{32,96},{64,128},{96,160},{128,192},{160,224},{192,0},{224,... | collective-permute-start | bytes 1572872 | tf_op jit(solution)/shard_map/ppermute | solution.py:416
  171.4 8.3 %copy-start = (bf16[32,16,1280]{2,1,0:T(8,128)(2,1)}, bf16[32,16,1280]{2,1,0:T(8,128)(2,1)S(1)}, u32[]{:S(2)}) copy-start(bf16[32,16,1280]{2,1,0:T(8,128)(2,1)S(1)} %all-to-all-done.3) | copy-start | bytes 3932164
  172.5 14.9 %all-to-all-start.4 = ((f32[8,8,256]{2,1,0:T(8,128)}), f32[8,8,256]{2,1,0:T(8,128)S(1)}, u32[]{:S(2)}, u32[]{:S(2)}) async-start(f32[8,8,256]{2,1,0:T(8,128)} %tally.1), calls=%async_computation.4 | async-start | bytes 131072 | tf_op jit(solution)/shard_map/all_to_all | solution.py:584
  188.1 18.9 %all-to-all-start.5 = ((f32[32,8,128]{2,1,0:T(8,128)}), f32[32,8,128]{2,1,0:T(8,128)S(1)}, u32[]{:S(2)}, u32[]{:S(2)}) async-start(f32[32,8,128]{2,1,0:T(8,128)} %get-tuple-element.158), calls=%async_computation.5 | async-start | bytes 262144 | tf_op jit(solution)/shard_map/all_to_all | solution.py:592
  (16 other events, 17.5 us)

commit v5 on v4

--- a/solution.py
+++ b/solution.py
@@ -424,7 +424,7 @@
         return ((self.place + steps) % self.length).astype(jnp.int32)
 
 
-def pair_sums(mine, theirs, y, name, cost=1):
+def pair_sums(mine, theirs, y, name, wait=None, cost=1):
     count, depth, width = mine.shape
     steps = 2
     block = ((count, depth // steps, width), lambda i: (0, i, 0))
@@ -439,7 +439,7 @@
         out_blocks=(flat,) * count,
         cost=cost,
     )(mine, *theirs)
-    return kept, [y.send(part, -k - 1) for k, part in enumerate(sums)]
+    return kept, [part if k == wait else y.send(part, -k - 1) for k, part in enumerate(sums)]
 
 
 def total_sums(kept, parts):
@@ -575,22 +575,26 @@
         cost=LONG,
     )(grad_incoming, hidden)
     arrived_out, in_parts = lax.optimization_barrier(([core.send(part, 1) for part in out_theirs], in_parts))
-    out_kept, out_parts = pair_sums(out_mine, arrived_out, y, "out_pair")
+    out_kept, out_parts = pair_sums(out_mine, arrived_out, y, "out_pair", wait=1)
     mixed = call(part(mixed_kernel, peers), "mixed", shape(count, width))(returned, frames, meta)
     back, out_kept, mixed = lax.optimization_barrier((back, out_kept, mixed))
     sums = call(
         part(tally_kernel, peers), "tally", shape(groups, 8, width // 4, dtype=f32), in_blocks=(last,), mib=4
     )(back)
+    sums, out_parts = lax.optimization_barrier((sums, out_parts))
     sums = lax.all_to_all(sums, "dp", 0, 0, tiled=True)
     grad_frames = call(part(finish_kernel, peers), "finish", shape(count, width))(
         back, frames, gain, out_grad, meta, grad_logits, router_rows
     )
-    sums, grad_frames = lax.optimization_barrier((sums, grad_frames))
+    sums, grad_frames, out_parts[1] = lax.optimization_barrier((sums, grad_frames, out_parts[1]))
+    out_parts[1] = y.send(out_parts[1], -2)
     router_mine, gain_gradient = call(
         sum_kernel, "sum", shape(peers, 8, width // 8, dtype=f32), shape(1, width, dtype=f32), mib=4
     )(sums)
-    grad_router = lax.all_to_all(router_mine, "expert", 0, 0, tiled=True).reshape(peers, width).T
-    grad_w_out, grad_w_in = total_sums((out_kept, in_kept), (out_parts, in_parts))
+    router_sums = lax.all_to_all(router_mine, "expert", 0, 0, tiled=True)
+    totals = total_sums((out_kept, in_kept), (out_parts, in_parts))
+    router_sums, (grad_w_out, grad_w_in) = lax.optimization_barrier((router_sums, totals))
+    grad_router = router_sums.reshape(peers, width).T
     return (mixed, grad_frames, grad_w_in[None], grad_w_out[None], grad_router, gain_gradient[0])
 
 

time: 209 us -> 208 us (level)
    ppermute x28, waiting for transfers between devices: 23.6 us -> 27.9 us  [send(): lax.ppermute(array, self.name, [(i, self.step(i, k)) for i in range(self....]
    all_to_all x1, waiting for transfers between devices: 3.73 us -> 0.87 us  [on_device(): sums = lax.all_to_all(sums, 'dp', 0, 0, tiled=True)]
    unnamed x61 -> x63, local copies, waits for them, and re-layouts: 7.52 us -> 6.58 us
  transfers between devices with their start and end apart: 34 -> 34, of which waited for: 18 -> 20; matrix products, arithmetic and copies ran while one was open for 1% -> 1% of each run, Pallas kernels for 37% -> 37%
where the time goes in v5:
time: 208 us; the launch traced here: 206 us
  starting transfers between devices  80.4 us (39%)
  Pallas kernels  76 us (37%)
  waiting for transfers between devices  41.3 us (20%)
  local copies, waits for them, and re-layouts  6.58 us (3%)
    pallas_call x14, Pallas kernels, run(): pl.pallas_call(kernel, out_shape=outs if len(outs) > 1 else outs[0], grid...  76 us
    all_to_all x4, starting transfers between devices, exchange(): lax.all_to_all(packed.reshape(peers, MAIN, packed.shape[1]), 'expert', sp...  37.9 us
    ppermute x28, starting transfers between devices, send(): lax.ppermute(array, self.name, [(i, self.step(i, k)) for i in range(self....  28.1 us
    ppermute x28, waiting for transfers between devices, send(): lax.ppermute(array, self.name, [(i, self.step(i, k)) for i in range(self....  27.9 us
    all_to_all x4, waiting for transfers between devices, exchange(): lax.all_to_all(packed.reshape(peers, MAIN, packed.shape[1]), 'expert', sp...  10.9 us
    all_to_all x1, starting transfers between devices, on_device(): router_sums = lax.all_to_all(router_mine, 'expert', 0, 0, tiled=True)  8.78 us
    unnamed x63, local copies, waits for them, and re-layouts  6.58 us
    all_to_all x1, starting transfers between devices, on_device(): sums = lax.all_to_all(sums, 'dp', 0, 0, tiled=True)  5.51 us
  transfers between devices with their start and end apart: 34, of which 20 were waited for; matrix products, arithmetic and copies ran while one was open for 1% of the time, Pallas kernels for 37%

profile of v5, /device:TPU:1, one launch (start us, length us, event | category | flops | bytes accessed | tf_op | source)
XLA Modules:
  0.0 206.4 jit_solution(4498939166674149021)
XLA Ops:
  0.6 2.2 %collective-permute-start = (bf16[128,2048]{1,0:T(8,128)(2,1)}, bf16[128,2048]{1,0:T(8,128)(2,1)}, u32[]{:S(2)}, u32[]{:S(2)}) collective-permute-start(bf16[128,2048]{1,0:T(8,128)(2,1)} %bitcast.32), channel_id=1, source_target_pairs={{0,64},{32,96},{64,128},{96,160},{128,192},{160,224},{192,0},{224,... | collective-permute-start | bytes 1572872 | tf_op jit(solution)/shard_map/ppermute | solution.py:416
  2.8 2.6 %collective-permute-start.1 = (bf16[128,2048]{1,0:T(8,128)(2,1)}, bf16[128,2048]{1,0:T(8,128)(2,1)}, u32[]{:S(2)}, u32[]{:S(2)}) collective-permute-start(bf16[128,2048]{1,0:T(8,128)(2,1)} %bitcast.33), channel_id=1, source_target_pairs={{0,128},{32,160},{64,192},{96,224},{128,0},{160,32},{192,64},{224,... | collective-permute-start | bytes 1572872 | tf_op jit(solution)/shard_map/ppermute | solution.py:416
  5.5 1.1 collective-permute-start.2
  6.5 3.2 %dispatch.1 = (bf16[512,1152]{1,0:T(8,128)(2,1)}, bf16[192,1024]{1,0:T(8,128)(2,1)}, s32[2,192]{1,0:T(2,128)}) custom-call(bf16[192,1024]{1,0:T(8,128)(2,1)} %frames_ref.5, f32[1,1024]{1,0:T(1,128)} %bitcast.51, s32[2,192]{1,0:T(2,128)} %bitcast.58), custom_call_target="tpu_custom_call" | custom-call | flops 99999997952 | bytes 1 | tf_op jit(solution)/shard_map/dispatch/pallas_call | solution.py:370
  9.7 11.0 %all-to-all-start = ((bf16[32,16,1152]{2,1,0:T(8,128)(2,1)}), bf16[32,16,1152]{2,1,0:T(8,128)(2,1)S(1)}, u32[]{:S(2)}, u32[]{:S(2)}) async-start(bf16[32,16,1152]{2,1,0:T(8,128)(2,1)} %bitcast.40), calls=%async_computation | async-start | bytes 2359296 | tf_op jit(solution)/shard_map/all_to_all | solution.py:394
  20.8 3.4 %grads.1 = (bf16[512,1152]{1,0:T(8,128)(2,1)}, f32[192,16]{1,0:T(8,128)}) custom-call(bf16[192,1024]{1,0:T(8,128)(2,1)} %get-tuple-element.92.normed_ref, bf16[32,1024]{1,0:T(8,128)(2,1)} %bitcast.47, s32[2,192]{1,0:T(2,128)} %bitcast.59, s32[1,192]{1,0:T(1,128)} %bitcast.60, s32[2,192]{1,0:T(2,128)} %get-tuple-element.93.place_ref, bf16[192,1024]{1,0:T(8,128)(2,1)} %grad_ref.5), custom_call_target="tpu_custom_call" | custom-call | flops 99999997952 | bytes 1 | tf_op jit(solution)/shard_map/grads/pallas_call | solution.py:370
  24.2 4.2 %collective-permute-done.1.refs_2_ = bf16[128,2048]{1,0:T(8,128)(2,1)} collective-permute-done((bf16[128,2048]{1,0:T(8,128)(2,1)}, bf16[128,2048]{1,0:T(8,128)(2,1)}, u32[]{:S(2)}, u32[]{:S(2)}) %collective-permute-start.1) | collective-permute-done | bytes 524320 | tf_op jit(solution)/shard_map/ppermute | solution.py:416
  28.3 1.5 collective-permute-start.3
  30.5 0.9 collective-permute-start.7
  31.4 2.5 %collective-permute-start.8 = (bf16[256,1024]{1,0:T(8,128)(2,1)S(1)}, bf16[256,1024]{1,0:T(8,128)(2,1)S(1)}, u32[]{:S(2)}, u32[]{:S(2)}) collective-permute-start(bf16[256,1024]{1,0:T(8,128)(2,1)S(1)} %bitcast.44), channel_id=1, source_target_pairs={{0,192},{32,224},{64,0},{96,32},{128,64},{160,96},{192,128},{224,1... | collective-permute-start | bytes 1572872 | tf_op jit(solution)/shard_map/ppermute | solution.py:416
  33.9 10.9 %collective-permute-done.7.refs_1_ = bf16[256,1024]{1,0:T(8,128)(2,1)S(1)} collective-permute-done((bf16[256,1024]{1,0:T(8,128)(2,1)S(1)}, bf16[256,1024]{1,0:T(8,128)(2,1)S(1)}, u32[]{:S(2)}, u32[]{:S(2)}) %collective-permute-start.7) | collective-permute-done | bytes 524320 | tf_op jit(solution)/shard_map/ppermute | solution.py:416
  44.8 0.8 copy-done.16
  45.6 0.8 copy-done.17
  46.4 2.4 %all-to-all-done = bf16[32,16,1152]{2,1,0:T(8,128)(2,1)S(1)} async-done(((bf16[32,16,1152]{2,1,0:T(8,128)(2,1)}), bf16[32,16,1152]{2,1,0:T(8,128)(2,1)S(1)}, u32[]{:S(2)}, u32[]{:S(2)}) %all-to-all-start) | async-done | bytes 1179680 | tf_op jit(solution)/shard_map/all_to_all | solution.py:394
  48.8 8.6 %all-to-all-start.1 = ((bf16[32,16,1152]{2,1,0:T(8,128)(2,1)}), bf16[32,16,1152]{2,1,0:T(8,128)(2,1)S(1)}, u32[]{:S(2)}, u32[]{:S(2)}) async-start(bf16[32,16,1152]{2,1,0:T(8,128)(2,1)} %bitcast.38), calls=%async_computation.1 | async-start | bytes 2359296 | tf_op jit(solution)/shard_map/all_to_all | solution.py:394
  57.5 2.1 collective-permute-start.9
  60.2 1.8 collective-permute-start.10
  62.5 9.6 %first.1 = (bf16[576,1024]{1,0:T(8,128)(2,1)}, bf16[576,2048]{1,0:T(8,128)(2,1)}, f32[576,2048]{1,0:T(8,128)}, bf16[1024,576]{1,0:T(8,128)(2,1)}) custom-call(s32[8]{0:T(128)} %pad_add_fusion.order_ref.holders_ref, bf16[512,1152]{1,0:T(8,128)(2,1)} %bitcast.31, bf16[128,2048]{1,0:T(8,128)(2,1)} %bitcast.35, bf16[128,2048]{1,0:T(8,128)(2,1)} %collective-permute-done.refs_1_, ...), custom_call_target="tpu_custom_call" | custom-call | flops 1 | bytes 1 | tf_op jit(solution)/shard_map/first/pallas_call | solution.py:370
  72.1 1.4 collective-permute-start.12
  73.5 1.7 collective-permute-done.12.refs_6_
  75.3 0.8 copy-done.29
  76.1 9.1 %second.1 = (bf16[512,1152]{1,0:T(8,128)(2,1)}, bf16[2048,1024]{1,0:T(8,128)(2,1)}) custom-call(s32[8]{0:T(128)} %pad_add_fusion.order_ref.holders_ref, bf16[576,2048]{1,0:T(8,128)(2,1)} %get-tuple-element.111.hidden_ref, bf16[256,1024]{1,0:T(8,128)(2,1)} %bitcast.42, bf16[256,1024]{1,0:T(8,128)(2,1)} %copy-done.16, ...), custom_call_target="tpu_custom_call" | custom-call | flops 1 | bytes 1 | tf_op jit(solution)/shard_map/second/pallas_call | solution.py:370
  85.7 8.8 %all-to-all-start.2 = ((bf16[32,16,1152]{2,1,0:T(8,128)(2,1)}), bf16[32,16,1152]{2,1,0:T(8,128)(2,1)S(1)}, u32[]{:S(2)}, u32[]{:S(2)}) async-start(bf16[32,16,1152]{2,1,0:T(8,128)(2,1)} %bitcast.39), calls=%async_computation.2 | async-start | bytes 2359296 | tf_op jit(solution)/shard_map/all_to_all | solution.py:394
  95.1 18.1 %backward.1 = (bf16[576,1024]{1,0:T(8,128)(2,1)}, bf16[128,2048]{1,0:T(8,128)(2,1)}, bf16[128,2048]{1,0:T(8,128)(2,1)}, bf16[128,2048]{1,0:T(8,128)(2,1)}, bf16[...) custom-call(s32[4]{0:T(128)} %and_select_fusion.order_ref, ...), custom_call_target="tpu_custom_call" | custom-call | flops 1 | bytes 1 | tf_op jit(solution)/shard_map/backward/pallas_call | solution.py:370
  113.2 0.8 collective-permute-start.14
  114.6 1.1 collective-permute-done.14.refs_0_
  118.8 3.3 %in_pair.1 = (f32[128,2048]{1,0:T(8,128)}, bf16[128,2048]{1,0:T(8,128)(2,1)}, bf16[128,2048]{1,0:T(8,128)(2,1)}, bf16[128,2048]{1,0:T(8,128)(2,1)}) custom-call(bf16[4,128,2048]{2,1,0:T(8,128)(2,1)} %get-tuple-element.124.mine_ref, bf16[128,2048]{1,0:T(8,128)(2,1)} %copy-done.23, bf16[128,2048]{1,0:T(8,128)(2,1)} %copy-done.25, ...), custom_call_target="tpu_custom_call" | custom-call | flops 1 | bytes 1 | tf_op jit(solution)/shard_map/in_pair/pallas_call | solution.py:370
  122.1 2.6 %collective-permute-start.22 = (bf16[128,2048]{1,0:T(8,128)(2,1)}, bf16[128,2048]{1,0:T(8,128)(2,1)S(1)}, u32[]{:S(2)}, u32[]{:S(2)}) collective-permute-start(bf16[128,2048]{1,0:T(8,128)(2,1)} %get-tuple-element.143), channel_id=1, source_target_pairs={{0,192},{32,224},{64,0},{96,32},{128,64},{160,96},{192,128},{224,1... | collective-permute-start | bytes 1572872 | tf_op jit(solution)/shard_map/ppermute | solution.py:416
  125.4 1.0 copy-done.1
  126.4 4.5 %route.1 = (bf16[512,1280]{1,0:T(8,128)(2,1)}, f32[192,32]{1,0:T(8,128)}) custom-call(bf16[512,1152]{1,0:T(8,128)(2,1)} %bitcast.27, bf16[192,1024]{1,0:T(8,128)(2,1)} %get-tuple-element.92.normed_ref, bf16[192,1024]{1,0:T(8,128)(2,1)} %grad_ref.5, f32[192,16]{1,0:T(8,128)} %get-tuple-element.95.meta_ref, ...), custom_call_target="tpu_custom_call", output_to_operand_aliasing={{0}: (7, {})} | custom-call | flops 1 | bytes 1 | tf_op jit(solution)/shard_map/route/pallas_call | solution.py:370
  130.9 9.5 %all-to-all-start.3 = ((bf16[32,16,1280]{2,1,0:T(8,128)(2,1)}), bf16[32,16,1280]{2,1,0:T(8,128)(2,1)S(1)}, u32[]{:S(2)}, u32[]{:S(2)}) async-start(bf16[32,16,1280]{2,1,0:T(8,128)(2,1)} %bitcast.29), calls=%async_computation.3 | async-start | bytes 2621440 | tf_op jit(solution)/shard_map/all_to_all | solution.py:394
  140.4 8.2 %outer.1 = (bf16[256,1024]{1,0:T(8,128)(2,1)}, bf16[256,1024]{1,0:T(8,128)(2,1)}, bf16[256,1024]{1,0:T(8,128)(2,1)}, bf16[256,1024]{1,0:T(8,128)(2,1)}, bf16[4,256,1024]{2,1,0:T(8,128)(2,1)}) custom-call(s32[4]{0:T(128)} %and_select_fusion.order_ref, s32[1]{0:T(128)} %bitcast.14.core_ref, bf16[576,1024]{1,0:T(8,128)(2,1)} %get-tuple-element.137.grads_ref, ...), custom_call_target="tpu_custom_call" | custom-call | flops 99999997952 | bytes 1 | tf_op jit(solution)/shard_map/outer/pallas_call | solution.py:370
  148.6 1.2 collective-permute-start.18
  154.6 3.4 %out_pair.1 = (f32[256,1024]{1,0:T(8,128)}, bf16[256,1024]{1,0:T(8,128)(2,1)}, bf16[256,1024]{1,0:T(8,128)(2,1)}, bf16[256,1024]{1,0:T(8,128)(2,1)}) custom-call(bf16[4,256,1024]{2,1,0:T(8,128)(2,1)} %get-tuple-element.138.mine_ref, bf16[256,1024]{1,0:T(8,128)(2,1)} %copy-done.18, bf16[256,1024]{1,0:T(8,128)(2,1)} %copy-done.19, ...), custom_call_target="tpu_custom_call" | custom-call | flops 1 | bytes 1 | tf_op jit(solution)/shard_map/out_pair/pallas_call | solution.py:370
  158.0 2.1 %collective-permute-start.25 = (bf16[256,1024]{1,0:T(8,128)(2,1)}, bf16[256,1024]{1,0:T(8,128)(2,1)S(1)}, u32[]{:S(2)}, u32[]{:S(2)}) collective-permute-start(bf16[256,1024]{1,0:T(8,128)(2,1)} %get-tuple-element.154), channel_id=1, source_target_pairs={{0,192},{32,224},{64,0},{96,32},{128,64},{160,96},{192,128},{224,1... | collective-permute-start | bytes 1572872 | tf_op jit(solution)/shard_map/ppermute | solution.py:416
  160.4 3.1 %mixed.1 = bf16[192,1024]{1,0:T(8,128)(2,1)} custom-call(bf16[512,1152]{1,0:T(8,128)(2,1)} %bitcast.28, bf16[192,1024]{1,0:T(8,128)(2,1)} %frames_ref.5, f32[192,16]{1,0:T(8,128)} %get-tuple-element.95.meta_ref), custom_call_target="tpu_custom_call" | custom-call | flops 1 | bytes 1 | tf_op jit(solution)/shard_map/mixed/pallas_call | solution.py:370
  163.5 8.0 %all-to-all-done.3 = bf16[32,16,1280]{2,1,0:T(8,128)(2,1)S(1)} async-done(((bf16[32,16,1280]{2,1,0:T(8,128)(2,1)}), bf16[32,16,1280]{2,1,0:T(8,128)(2,1)S(1)}, u32[]{:S(2)}, u32[]{:S(2)}) %all-to-all-start.3) | async-done | bytes 1310752 | tf_op jit(solution)/shard_map/all_to_all | solution.py:394
  171.5 1.1 tally.1
  172.6 1.8 collective-permute-done.26.refs_2_
  174.4 5.5 %all-to-all-start.4 = ((f32[8,8,256]{2,1,0:T(8,128)}), f32[8,8,256]{2,1,0:T(8,128)S(1)}, u32[]{:S(2)}, u32[]{:S(2)}) async-start(f32[8,8,256]{2,1,0:T(8,128)} %tally.1), calls=%async_computation.4 | async-start | bytes 131072 | tf_op jit(solution)/shard_map/all_to_all | solution.py:585
  179.9 4.0 %finish.1 = bf16[192,1024]{1,0:T(8,128)(2,1)} custom-call(bf16[512,1280]{1,0:T(8,128)(2,1)} %bitcast.26, bf16[192,1024]{1,0:T(8,128)(2,1)} %frames_ref.5, f32[1,1024]{1,0:T(1,128)} %bitcast.54, bf16[192,1024]{1,0:T(8,128)(2,1)} %grad_ref.5, f32[192,16]{1,0:T(8,128)} %get-tuple-element.95.meta_ref, f32[192,32]{1,0:T(8,128)} %get-tuple-element.136.logits_ref, ...), custom_call_target="tpu_custom_call" | custom-call | flops 1 | bytes 1 | tf_op jit(solution)/shard_map/finish/pallas_call | solution.py:370
  183.9 0.9 all-to-all-done.4.sums_ref
  184.7 2.1 %collective-permute-start.27 = (bf16[256,1024]{1,0:T(8,128)(2,1)S(1)}, bf16[256,1024]{1,0:T(8,128)(2,1)S(1)}, u32[]{:S(2)}, u32[]{:S(2)}) collective-permute-start(bf16[256,1024]{1,0:T(8,128)(2,1)S(1)} %copy-done.30), channel_id=1, source_target_pairs={{0,128},{32,160},{64,192},{96,224},{128,0},{160,32},{192,64},{224,... | collective-permute-start | bytes 1572872 | tf_op jit(solution)/shard_map/ppermute | solution.py:416
  187.6 8.8 %all-to-all-start.5 = ((f32[32,8,128]{2,1,0:T(8,128)}), f32[32,8,128]{2,1,0:T(8,128)S(1)}, u32[]{:S(2)}, u32[]{:S(2)}) async-start(f32[32,8,128]{2,1,0:T(8,128)} %get-tuple-element.161), calls=%async_computation.5 | async-start | bytes 262144 | tf_op jit(solution)/shard_map/all_to_all | solution.py:594
  196.4 2.5 %collective-permute-done.27.refs_1_ = bf16[256,1024]{1,0:T(8,128)(2,1)S(1)} collective-permute-done((bf16[256,1024]{1,0:T(8,128)(2,1)S(1)}, bf16[256,1024]{1,0:T(8,128)(2,1)S(1)}, u32[]{:S(2)}, u32[]{:S(2)}) %collective-permute-start.27) | collective-permute-done | bytes 524320 | tf_op jit(solution)/shard_map/ppermute | solution.py:416
  198.9 0.8 copy-done.14
  199.7 4.3 %total.1 = (f32[256,1024]{1,0:T(8,128)}, f32[128,2048]{1,0:T(8,128)}) custom-call(f32[256,1024]{1,0:T(8,128)} %get-tuple-element.162.first_ref, f32[128,2048]{1,0:T(8,128)} %get-tuple-element.163.second_ref, bf16[256,1024]{1,0:T(8,128)(2,1)} %copy-done.12, bf16[256,1024]{1,0:T(8,128)(2,1)} %copy-done.14, bf16[256,1024]{1,0:T(8,128)(2,1)} %copy-done.13, ...), custom_call_target="tpu_custom_call" | custom-call | flops 1 | bytes 1 | tf_op jit(solution)/shard_map/total/pallas_call | solution.py:370
  204.1 1.7 all-to-all-done.5
  (100 shorter events, 13.9 us)
Async XLA Ops:
  0.6 23.5 %collective-permute-start = (bf16[128,2048]{1,0:T(8,128)(2,1)}, bf16[128,2048]{1,0:T(8,128)(2,1)}, u32[]{:S(2)}, u32[]{:S(2)}) collective-permute-start(bf16[128,2048]{1,0:T(8,128)(2,1)} %bitcast.32), channel_id=1, source_target_pairs={{0,64},{32,96},{64,128},{96,160},{128,192},{160,224},{192,0},{224,... | collective-permute-start | bytes 1572872 | tf_op jit(solution)/shard_map/ppermute | solution.py:416
  2.8 25.5 %collective-permute-start.1 = (bf16[128,2048]{1,0:T(8,128)(2,1)}, bf16[128,2048]{1,0:T(8,128)(2,1)}, u32[]{:S(2)}, u32[]{:S(2)}) collective-permute-start(bf16[128,2048]{1,0:T(8,128)(2,1)} %bitcast.33), channel_id=1, source_target_pairs={{0,128},{32,160},{64,192},{96,224},{128,0},{160,32},{192,64},{224,... | collective-permute-start | bytes 1572872 | tf_op jit(solution)/shard_map/ppermute | solution.py:416
  5.5 22.9 %collective-permute-start.2 = (bf16[128,2048]{1,0:T(8,128)(2,1)}, bf16[128,2048]{1,0:T(8,128)(2,1)}, u32[]{:S(2)}, u32[]{:S(2)}) collective-permute-start(bf16[128,2048]{1,0:T(8,128)(2,1)} %bitcast.34), channel_id=1, source_target_pairs={{0,192},{32,224},{64,0},{96,32},{128,64},{160,96},{192,128},{224,1... | collective-permute-start | bytes 1572872 | tf_op jit(solution)/shard_map/ppermute | solution.py:416
  9.7 39.1 %all-to-all-start = ((bf16[32,16,1152]{2,1,0:T(8,128)(2,1)}), bf16[32,16,1152]{2,1,0:T(8,128)(2,1)S(1)}, u32[]{:S(2)}, u32[]{:S(2)}) async-start(bf16[32,16,1152]{2,1,0:T(8,128)(2,1)} %bitcast.40), calls=%async_computation | async-start | bytes 2359296 | tf_op jit(solution)/shard_map/all_to_all | solution.py:394
  20.8 7.6 %copy-start.4 = (bf16[1,128,2048]{2,1,0:T(8,128)(2,1)S(1)}, bf16[1,128,2048]{2,1,0:T(8,128)(2,1)}, u32[]{:S(2)}) copy-start(bf16[1,128,2048]{2,1,0:T(8,128)(2,1)} %param.11) | copy-start | bytes 1572868
  20.8 9.7 %copy-start.15 = (bf16[1,256,1024]{2,1,0:T(8,128)(2,1)S(1)}, bf16[1,256,1024]{2,1,0:T(8,128)(2,1)}, u32[]{:S(2)}) copy-start(bf16[1,256,1024]{2,1,0:T(8,128)(2,1)} %param.12) | copy-start | bytes 1572868
  28.3 3.1 %collective-permute-start.3 = (bf16[128,2048]{1,0:T(8,128)(2,1)S(1)}, bf16[128,2048]{1,0:T(8,128)(2,1)S(1)}, u32[]{:S(2)}, u32[]{:S(2)}) collective-permute-start(bf16[128,2048]{1,0:T(8,128)(2,1)S(1)} %bitcast.37), channel_id=1, source_target_pairs={{0,32},{32,0},{64,96},{96,64},{128,160},{160,128},{192,224},{224,1... | collective-permute-start | bytes 1572872 | tf_op jit(solution)/shard_map/ppermute | solution.py:416
  29.9 4.0 %collective-permute-start.4 = (bf16[128,2048]{1,0:T(8,128)(2,1)}, bf16[128,2048]{1,0:T(8,128)(2,1)S(1)}, u32[]{:S(2)}, u32[]{:S(2)}) collective-permute-start(bf16[128,2048]{1,0:T(8,128)(2,1)} %collective-permute-done.refs_1_), channel_id=1, source_target_pairs={{0,32},{32,0},{64,96},{96,64},{128,160},{160,128},{192,224},{224,1... | collective-permute-start | bytes 1572872 | tf_op jit(solution)/shard_map/ppermute | solution.py:416
  30.0 3.9 %collective-permute-start.5 = (bf16[128,2048]{1,0:T(8,128)(2,1)}, bf16[128,2048]{1,0:T(8,128)(2,1)S(1)}, u32[]{:S(2)}, u32[]{:S(2)}) collective-permute-start(bf16[128,2048]{1,0:T(8,128)(2,1)} %collective-permute-done.1.refs_2_), channel_id=1, source_target_pairs={{0,32},{32,0},{64,96},{96,64},{128,160},{160,128},{192,224},{224,1... | collective-permute-start | bytes 1572872 | tf_op jit(solution)/shard_map/ppermute | solution.py:416
  30.4 3.5 %collective-permute-start.6 = (bf16[128,2048]{1,0:T(8,128)(2,1)}, bf16[128,2048]{1,0:T(8,128)(2,1)S(1)}, u32[]{:S(2)}, u32[]{:S(2)}) collective-permute-start(bf16[128,2048]{1,0:T(8,128)(2,1)} %collective-permute-done.2.refs_3_), channel_id=1, source_target_pairs={{0,32},{32,0},{64,96},{96,64},{128,160},{160,128},{192,224},{224,1... | collective-permute-start | bytes 1572872 | tf_op jit(solution)/shard_map/ppermute | solution.py:416
  30.5 14.3 %collective-permute-start.7 = (bf16[256,1024]{1,0:T(8,128)(2,1)S(1)}, bf16[256,1024]{1,0:T(8,128)(2,1)S(1)}, u32[]{:S(2)}, u32[]{:S(2)}) collective-permute-start(bf16[256,1024]{1,0:T(8,128)(2,1)S(1)} %bitcast.43), channel_id=1, source_target_pairs={{0,64},{32,96},{64,128},{96,160},{128,192},{160,224},{192,0},{224,... | collective-permute-start | bytes 1572872 | tf_op jit(solution)/shard_map/ppermute | solution.py:416
  31.4 31.0 %copy-start.5 = (bf16[128,2048]{1,0:T(8,128)(2,1)}, bf16[128,2048]{1,0:T(8,128)(2,1)S(1)}, u32[]{:S(2)}) copy-start(bf16[128,2048]{1,0:T(8,128)(2,1)S(1)} %collective-permute-done.3.refs_4_) | copy-start | bytes 1572868
  31.4 13.4 %collective-permute-start.8 = (bf16[256,1024]{1,0:T(8,128)(2,1)S(1)}, bf16[256,1024]{1,0:T(8,128)(2,1)S(1)}, u32[]{:S(2)}, u32[]{:S(2)}) collective-permute-start(bf16[256,1024]{1,0:T(8,128)(2,1)S(1)} %bitcast.44), channel_id=1, source_target_pairs={{0,192},{32,224},{64,0},{96,32},{128,64},{160,96},{192,128},{224,1... | collective-permute-start | bytes 1572872 | tf_op jit(solution)/shard_map/ppermute | solution.py:416
  33.9 14.9 %copy-start.6 = (bf16[128,2048]{1,0:T(8,128)(2,1)}, bf16[128,2048]{1,0:T(8,128)(2,1)S(1)}, u32[]{:S(2)}) copy-start(bf16[128,2048]{1,0:T(8,128)(2,1)S(1)} %collective-permute-done.4.refs_5_) | copy-start | bytes 1572868
  33.9 14.9 %copy-start.7 = (bf16[128,2048]{1,0:T(8,128)(2,1)}, bf16[128,2048]{1,0:T(8,128)(2,1)S(1)}, u32[]{:S(2)}) copy-start(bf16[128,2048]{1,0:T(8,128)(2,1)S(1)} %collective-permute-done.5.refs_6_) | copy-start | bytes 1572868
  33.9 10.9 %copy-start.8 = (bf16[128,2048]{1,0:T(8,128)(2,1)}, bf16[128,2048]{1,0:T(8,128)(2,1)S(1)}, u32[]{:S(2)}) copy-start(bf16[128,2048]{1,0:T(8,128)(2,1)S(1)} %collective-permute-done.6.refs_7_) | copy-start | bytes 1572868
  48.8 13.6 %copy-start.3 = (bf16[32,16,1152]{2,1,0:T(8,128)(2,1)}, bf16[32,16,1152]{2,1,0:T(8,128)(2,1)S(1)}, u32[]{:S(2)}) copy-start(bf16[32,16,1152]{2,1,0:T(8,128)(2,1)S(1)} %all-to-all-done) | copy-start | bytes 3538948
  48.8 36.9 %all-to-all-start.1 = ((bf16[32,16,1152]{2,1,0:T(8,128)(2,1)}), bf16[32,16,1152]{2,1,0:T(8,128)(2,1)S(1)}, u32[]{:S(2)}, u32[]{:S(2)}) async-start(bf16[32,16,1152]{2,1,0:T(8,128)(2,1)} %bitcast.38), calls=%async_computation.1 | async-start | bytes 2359296 | tf_op jit(solution)/shard_map/all_to_all | solution.py:394
  57.5 14.7 %collective-permute-start.9 = (bf16[256,1024]{1,0:T(8,128)(2,1)S(1)}, bf16[256,1024]{1,0:T(8,128)(2,1)}, u32[]{:S(2)}, u32[]{:S(2)}) collective-permute-start(bf16[256,1024]{1,0:T(8,128)(2,1)S(1)} %bitcast.45), channel_id=1, source_target_pairs={{0,128},{32,160},{64,192},{96,224},{128,0},{160,32},{192,64},{224,... | collective-permute-start | bytes 1572872 | tf_op jit(solution)/shard_map/ppermute | solution.py:416
  60.2 13.3 %collective-permute-start.10 = (bf16[256,1024]{1,0:T(8,128)(2,1)S(1)}, bf16[256,1024]{1,0:T(8,128)(2,1)S(1)}, u32[]{:S(2)}, u32[]{:S(2)}) collective-permute-start(bf16[256,1024]{1,0:T(8,128)(2,1)S(1)} %bitcast.46), channel_id=1, source_target_pairs={{0,32},{32,0},{64,96},{96,64},{128,160},{160,128},{192,224},{224,1... | collective-permute-start | bytes 1572872 | tf_op jit(solution)/shard_map/ppermute | solution.py:416
  61.9 11.6 %collective-permute-start.11 = (bf16[256,1024]{1,0:T(8,128)(2,1)}, bf16[256,1024]{1,0:T(8,128)(2,1)S(1)}, u32[]{:S(2)}, u32[]{:S(2)}) collective-permute-start(bf16[256,1024]{1,0:T(8,128)(2,1)} %copy-done.16), channel_id=1, source_target_pairs={{0,32},{32,0},{64,96},{96,64},{128,160},{160,128},{192,224},{224,1... | collective-permute-start | bytes 1572872 | tf_op jit(solution)/shard_map/ppermute | solution.py:416
  61.9 11.6 %collective-permute-start.13 = (bf16[256,1024]{1,0:T(8,128)(2,1)}, bf16[256,1024]{1,0:T(8,128)(2,1)S(1)}, u32[]{:S(2)}, u32[]{:S(2)}) collective-permute-start(bf16[256,1024]{1,0:T(8,128)(2,1)} %copy-done.17), channel_id=1, source_target_pairs={{0,32},{32,0},{64,96},{96,64},{128,160},{160,128},{192,224},{224,1... | collective-permute-start | bytes 1572872 | tf_op jit(solution)/shard_map/ppermute | solution.py:416
  72.1 3.1 %collective-permute-start.12 = (bf16[256,1024]{1,0:T(8,128)(2,1)}, bf16[256,1024]{1,0:T(8,128)(2,1)S(1)}, u32[]{:S(2)}, u32[]{:S(2)}) collective-permute-start(bf16[256,1024]{1,0:T(8,128)(2,1)} %collective-permute-done.9.refs_2_), channel_id=1, source_target_pairs={{0,32},{32,0},{64,96},{96,64},{128,160},{160,128},{192,224},{224,1... | collective-permute-start | bytes 1572872 | tf_op jit(solution)/shard_map/ppermute | solution.py:416
  85.7 9.4 %copy-start.2 = (bf16[32,16,1152]{2,1,0:T(8,128)(2,1)}, bf16[32,16,1152]{2,1,0:T(8,128)(2,1)S(1)}, u32[]{:S(2)}) copy-start(bf16[32,16,1152]{2,1,0:T(8,128)(2,1)S(1)} %all-to-all-done.1) | copy-start | bytes 3538948
  85.7 39.7 %all-to-all-start.2 = ((bf16[32,16,1152]{2,1,0:T(8,128)(2,1)}), bf16[32,16,1152]{2,1,0:T(8,128)(2,1)S(1)}, u32[]{:S(2)}, u32[]{:S(2)}) async-start(bf16[32,16,1152]{2,1,0:T(8,128)(2,1)} %bitcast.39), calls=%async_computation.2 | async-start | bytes 2359296 | tf_op jit(solution)/shard_map/all_to_all | solution.py:394
  113.2 2.5 %collective-permute-start.14 = (bf16[128,2048]{1,0:T(8,128)(2,1)}, bf16[128,2048]{1,0:T(8,128)(2,1)S(1)}, u32[]{:S(2)}, u32[]{:S(2)}) collective-permute-start(bf16[128,2048]{1,0:T(8,128)(2,1)} %get-tuple-element.125), channel_id=1, source_target_pairs={{0,32},{32,0},{64,96},{96,64},{128,160},{160,128},{192,224},{224,1... | collective-permute-start | bytes 1572872 | tf_op jit(solution)/shard_map/ppermute | solution.py:416
  113.9 2.5 %collective-permute-start.15 = (bf16[128,2048]{1,0:T(8,128)(2,1)}, bf16[128,2048]{1,0:T(8,128)(2,1)S(1)}, u32[]{:S(2)}, u32[]{:S(2)}) collective-permute-start(bf16[128,2048]{1,0:T(8,128)(2,1)} %get-tuple-element.126), channel_id=1, source_target_pairs={{0,32},{32,0},{64,96},{96,64},{128,160},{160,128},{192,224},{224,1... | collective-permute-start | bytes 1572872 | tf_op jit(solution)/shard_map/ppermute | solution.py:416
  114.0 3.1 %collective-permute-start.16 = (bf16[128,2048]{1,0:T(8,128)(2,1)}, bf16[128,2048]{1,0:T(8,128)(2,1)S(1)}, u32[]{:S(2)}, u32[]{:S(2)}) collective-permute-start(bf16[128,2048]{1,0:T(8,128)(2,1)} %get-tuple-element.127), channel_id=1, source_target_pairs={{0,32},{32,0},{64,96},{96,64},{128,160},{160,128},{192,224},{224,1... | collective-permute-start | bytes 1572872 | tf_op jit(solution)/shard_map/ppermute | solution.py:416
  114.5 3.5 %collective-permute-start.17 = (bf16[128,2048]{1,0:T(8,128)(2,1)}, bf16[128,2048]{1,0:T(8,128)(2,1)S(1)}, u32[]{:S(2)}, u32[]{:S(2)}) collective-permute-start(bf16[128,2048]{1,0:T(8,128)(2,1)} %get-tuple-element.128), channel_id=1, source_target_pairs={{0,32},{32,0},{64,96},{96,64},{128,160},{160,128},{192,224},{224,1... | collective-permute-start | bytes 1572872 | tf_op jit(solution)/shard_map/ppermute | solution.py:416
  122.1 27.7 %collective-permute-start.22 = (bf16[128,2048]{1,0:T(8,128)(2,1)}, bf16[128,2048]{1,0:T(8,128)(2,1)S(1)}, u32[]{:S(2)}, u32[]{:S(2)}) collective-permute-start(bf16[128,2048]{1,0:T(8,128)(2,1)} %get-tuple-element.143), channel_id=1, source_target_pairs={{0,192},{32,224},{64,0},{96,32},{128,64},{160,96},{192,128},{224,1... | collective-permute-start | bytes 1572872 | tf_op jit(solution)/shard_map/ppermute | solution.py:416
  124.7 25.6 %collective-permute-start.23 = (bf16[128,2048]{1,0:T(8,128)(2,1)}, bf16[128,2048]{1,0:T(8,128)(2,1)S(1)}, u32[]{:S(2)}, u32[]{:S(2)}) collective-permute-start(bf16[128,2048]{1,0:T(8,128)(2,1)} %get-tuple-element.144), channel_id=1, source_target_pairs={{0,128},{32,160},{64,192},{96,224},{128,0},{160,32},{192,64},{224,... | collective-permute-start | bytes 1572872 | tf_op jit(solution)/shard_map/ppermute | solution.py:416
  124.7 26.2 %collective-permute-start.24 = (bf16[128,2048]{1,0:T(8,128)(2,1)}, bf16[128,2048]{1,0:T(8,128)(2,1)S(1)}, u32[]{:S(2)}, u32[]{:S(2)}) collective-permute-start(bf16[128,2048]{1,0:T(8,128)(2,1)} %get-tuple-element.145), channel_id=1, source_target_pairs={{0,64},{32,96},{64,128},{96,160},{128,192},{160,224},{192,0},{224,... | collective-permute-start | bytes 1572872 | tf_op jit(solution)/shard_map/ppermute | solution.py:416
  130.9 40.6 %all-to-all-start.3 = ((bf16[32,16,1280]{2,1,0:T(8,128)(2,1)}), bf16[32,16,1280]{2,1,0:T(8,128)(2,1)S(1)}, u32[]{:S(2)}, u32[]{:S(2)}) async-start(bf16[32,16,1280]{2,1,0:T(8,128)(2,1)} %bitcast.29), calls=%async_computation.3 | async-start | bytes 2621440 | tf_op jit(solution)/shard_map/all_to_all | solution.py:394
  148.6 3.0 %collective-permute-start.18 = (bf16[256,1024]{1,0:T(8,128)(2,1)}, bf16[256,1024]{1,0:T(8,128)(2,1)S(1)}, u32[]{:S(2)}, u32[]{:S(2)}) collective-permute-start(bf16[256,1024]{1,0:T(8,128)(2,1)} %get-tuple-element.139), channel_id=1, source_target_pairs={{0,32},{32,0},{64,96},{96,64},{128,160},{160,128},{192,224},{224,1... | collective-permute-start | bytes 1572872 | tf_op jit(solution)/shard_map/ppermute | solution.py:416
  149.8 2.5 %collective-permute-start.19 = (bf16[256,1024]{1,0:T(8,128)(2,1)}, bf16[256,1024]{1,0:T(8,128)(2,1)S(1)}, u32[]{:S(2)}, u32[]{:S(2)}) collective-permute-start(bf16[256,1024]{1,0:T(8,128)(2,1)} %get-tuple-element.140), channel_id=1, source_target_pairs={{0,32},{32,0},{64,96},{96,64},{128,160},{160,128},{192,224},{224,1... | collective-permute-start | bytes 1572872 | tf_op jit(solution)/shard_map/ppermute | solution.py:416
  149.8 8.2 %copy-start.9 = (bf16[128,2048]{1,0:T(8,128)(2,1)}, bf16[128,2048]{1,0:T(8,128)(2,1)S(1)}, u32[]{:S(2)}) copy-start(bf16[128,2048]{1,0:T(8,128)(2,1)S(1)} %collective-permute-done.22.refs_3_) | copy-start | bytes 1572868
  149.8 3.2 %collective-permute-start.20 = (bf16[256,1024]{1,0:T(8,128)(2,1)}, bf16[256,1024]{1,0:T(8,128)(2,1)S(1)}, u32[]{:S(2)}, u32[]{:S(2)}) collective-permute-start(bf16[256,1024]{1,0:T(8,128)(2,1)} %get-tuple-element.141), channel_id=1, source_target_pairs={{0,32},{32,0},{64,96},{96,64},{128,160},{160,128},{192,224},{224,1... | collective-permute-start | bytes 1572872 | tf_op jit(solution)/shard_map/ppermute | solution.py:416
  150.3 7.7 %copy-start.10 = (bf16[128,2048]{1,0:T(8,128)(2,1)}, bf16[128,2048]{1,0:T(8,128)(2,1)S(1)}, u32[]{:S(2)}) copy-start(bf16[128,2048]{1,0:T(8,128)(2,1)S(1)} %collective-permute-done.23.refs_4_) | copy-start | bytes 1572868
  150.3 3.5 %collective-permute-start.21 = (bf16[256,1024]{1,0:T(8,128)(2,1)}, bf16[256,1024]{1,0:T(8,128)(2,1)S(1)}, u32[]{:S(2)}, u32[]{:S(2)}) collective-permute-start(bf16[256,1024]{1,0:T(8,128)(2,1)} %get-tuple-element.142), channel_id=1, source_target_pairs={{0,32},{32,0},{64,96},{96,64},{128,160},{160,128},{192,224},{224,1... | collective-permute-start | bytes 1572872 | tf_op jit(solution)/shard_map/ppermute | solution.py:416
  150.9 7.1 %copy-start.11 = (bf16[128,2048]{1,0:T(8,128)(2,1)}, bf16[128,2048]{1,0:T(8,128)(2,1)S(1)}, u32[]{:S(2)}) copy-start(bf16[128,2048]{1,0:T(8,128)(2,1)S(1)} %collective-permute-done.24.refs_5_) | copy-start | bytes 1572868
  158.0 14.6 %collective-permute-start.25 = (bf16[256,1024]{1,0:T(8,128)(2,1)}, bf16[256,1024]{1,0:T(8,128)(2,1)S(1)}, u32[]{:S(2)}, u32[]{:S(2)}) collective-permute-start(bf16[256,1024]{1,0:T(8,128)(2,1)} %get-tuple-element.154), channel_id=1, source_target_pairs={{0,192},{32,224},{64,0},{96,32},{128,64},{160,96},{192,128},{224,1... | collective-permute-start | bytes 1572872 | tf_op jit(solution)/shard_map/ppermute | solution.py:416
  160.1 14.2 %collective-permute-start.26 = (bf16[256,1024]{1,0:T(8,128)(2,1)}, bf16[256,1024]{1,0:T(8,128)(2,1)S(1)}, u32[]{:S(2)}, u32[]{:S(2)}) collective-permute-start(bf16[256,1024]{1,0:T(8,128)(2,1)} %get-tuple-element.156), channel_id=1, source_target_pairs={{0,64},{32,96},{64,128},{96,160},{128,192},{160,224},{192,0},{224,... | collective-permute-start | bytes 1572872 | tf_op jit(solution)/shard_map/ppermute | solution.py:416
  171.5 8.4 %copy-start = (bf16[32,16,1280]{2,1,0:T(8,128)(2,1)}, bf16[32,16,1280]{2,1,0:T(8,128)(2,1)S(1)}, u32[]{:S(2)}) copy-start(bf16[32,16,1280]{2,1,0:T(8,128)(2,1)S(1)} %all-to-all-done.3) | copy-start | bytes 3932164
  172.6 11.3 %copy-start.12 = (bf16[256,1024]{1,0:T(8,128)(2,1)}, bf16[256,1024]{1,0:T(8,128)(2,1)S(1)}, u32[]{:S(2)}) copy-start(bf16[256,1024]{1,0:T(8,128)(2,1)S(1)} %collective-permute-done.25.refs_0_) | copy-start | bytes 1572868
  174.4 9.5 %copy-start.13 = (bf16[256,1024]{1,0:T(8,128)(2,1)}, bf16[256,1024]{1,0:T(8,128)(2,1)S(1)}, u32[]{:S(2)}) copy-start(bf16[256,1024]{1,0:T(8,128)(2,1)S(1)} %collective-permute-done.26.refs_2_) | copy-start | bytes 1572868
  174.4 10.4 %all-to-all-start.4 = ((f32[8,8,256]{2,1,0:T(8,128)}), f32[8,8,256]{2,1,0:T(8,128)S(1)}, u32[]{:S(2)}, u32[]{:S(2)}) async-start(f32[8,8,256]{2,1,0:T(8,128)} %tally.1), calls=%async_computation.4 | async-start | bytes 131072 | tf_op jit(solution)/shard_map/all_to_all | solution.py:585
  184.7 14.2 %collective-permute-start.27 = (bf16[256,1024]{1,0:T(8,128)(2,1)S(1)}, bf16[256,1024]{1,0:T(8,128)(2,1)S(1)}, u32[]{:S(2)}, u32[]{:S(2)}) collective-permute-start(bf16[256,1024]{1,0:T(8,128)(2,1)S(1)} %copy-done.30), channel_id=1, source_target_pairs={{0,128},{32,160},{64,192},{96,224},{128,0},{160,32},{192,64},{224,... | collective-permute-start | bytes 1572872 | tf_op jit(solution)/shard_map/ppermute | solution.py:416
  187.6 18.1 %all-to-all-start.5 = ((f32[32,8,128]{2,1,0:T(8,128)}), f32[32,8,128]{2,1,0:T(8,128)S(1)}, u32[]{:S(2)}, u32[]{:S(2)}) async-start(f32[32,8,128]{2,1,0:T(8,128)} %get-tuple-element.161), calls=%async_computation.5 | async-start | bytes 262144 | tf_op jit(solution)/shard_map/all_to_all | solution.py:594
  (17 other events, 25.1 us)
